TPU v7x, 512 devices: a whole 4x8x8 slice. The times are simulated.
512 devices in a mesh: dom: 512 (over x, z, y, core).
Axes of the slice: x: 4, y: 8, z: 8, core: 2. Of those that a mesh axis runs over, the one named last changes fastest.
Arguments:
- connectivity: int32 [65536, 64], P('dom'), may hold values from 0 to 4991, as said below
- send_down: int32 [512, 768], P('dom'), may hold values from 0 to 3455, as said below
- send_up: int32 [512, 768], P('dom'), may hold values from 0 to 3455, as said below
- jacobian: float32 [65536], P('dom'), may hold values from 0.5 to 4
- pair_blocks: bfloat16 [131072, 4096], P('dom'), may hold values from -0.75 to 0.75
- pair_target: int32 [131072], P('dom'), may hold values from 0 to 127
- pair_source: int32 [131072], P('dom'), may hold values from 0 to 127
- source_values: bfloat16 [32, 4194304], P(None, 'dom'), may hold values from -6 to 6
Outputs:
- solution: float32 [32, 1769472], P(None, 'dom')
- residual: float32 [32, 1769472], P(None, 'dom')
- new_basis: float32 [32, 1769472], P(None, 'dom')
Inputs may be any that keep to these rules, and one draw needn't show every extreme that they name: `connectivity`: slots below 3456 are the partition's own nodes, the next 768 the lower neighbour's send_up list in order, the last 768 the upper neighbour's send_down list in order; the first partition uses no lower slots, the last no upper ones. `send_down`: distinct own node indices in each row. `send_up`: distinct own node indices in each row.
All inputs are finite; a program needn't handle non-finite values.
Results may differ from a plain program's by a relative error of at most 0.0003.
Values sent between devices are 32-bit elements; how exact they have to be, the bound alone decides.
No kernel may reach another device: no remote copies, remote signals or barrier semaphores. Data moves between devices by JAX's collectives and lax.ppermute only.
A program may use at most 64 MiB of HBM per device.

v0:
```python
import jax
import jax.numpy as jnp
import numpy as np
from jax import lax
from jax.sharding import PartitionSpec as P

NP = 64
NODE_DEV = 3456
F = 768


line_mass = (
    np.array(
        [
            [128.0, 99.0, -36.0, 19.0],
            [99.0, 648.0, -81.0, -36.0],
            [-36.0, -81.0, 648.0, 99.0],
            [19.0, -36.0, 99.0, 128.0],
        ]
    )
    / 504.0
)
mass_table = np.kron(np.kron(line_mass, line_mass), line_mass)


def shifted(value, axis, by):
    size = lax.axis_size(axis)
    pairs = [(i, i + by) for i in range(size) if 0 <= i + by < size]
    return lax.ppermute(value, axis, pairs)


def per_device(
    connectivity, send_down, send_up, jacobian, pair_blocks, pair_target, pair_source, source_values
):
    high = lax.Precision.HIGHEST
    tracers = source_values.shape[0]
    owned = NODE_DEV
    lows = send_down[0]
    highs = send_up[0]
    elements = connectivity.shape[0]
    pairs = pair_target.shape[0]
    flat_ids = connectivity.reshape(-1)
    element_mass = jnp.asarray(mass_table, dtype=jnp.float32)

    def spread(values, slots):
        return jnp.zeros((tracers, owned + 2 * F), jnp.float32).at[:, slots].add(values)

    def settle(extended):
        own_part = extended[:, :owned]
        from_above = shifted(extended[:, owned : owned + F], "dom", -1)
        from_below = shifted(extended[:, owned + F :], "dom", 1)
        return own_part.at[:, highs].add(from_above).at[:, lows].add(from_below)

    def lower_solve(lower, matrix):
        return jax.scipy.linalg.solve_triangular(lower, matrix, lower=True)

    offsets = jnp.arange(NP, dtype=jnp.int32)
    columns = (pair_source[:, None] * NP + offsets[None, :]).reshape(-1)
    gathered = source_values[:, columns].reshape(tracers, pairs, NP)
    mixed = pair_blocks.reshape(pairs, NP, NP)
    contrib = jnp.einsum("pij,tpj->tpi", mixed, gathered, preferred_element_type=jnp.float32)
    targets = connectivity[pair_target].reshape(-1)
    right_side = settle(spread(contrib.reshape(tracers, pairs * NP), targets))
    rhs_gram_local = jnp.dot(right_side, right_side.T, precision=high)
    sums = lax.psum((rhs_gram_local,), "dom")
    gram_rhs = sums[0]
    lower_rhs = jnp.linalg.cholesky(gram_rhs)
    basis = lower_solve(lower_rhs, right_side)
    below = shifted(basis[:, highs], "dom", 1)
    above = shifted(basis[:, lows], "dom", -1)
    values = jnp.concatenate([basis, below, above], axis=1)[:, flat_ids].reshape(
        tracers, elements, NP
    )
    image = (
        jnp.einsum("tep,pq->teq", values, element_mass, precision=high) * jacobian[None, :, None]
    )
    image = settle(spread(image.reshape(tracers, elements * NP), flat_ids))
    step_gram = lax.psum(jnp.dot(basis, image.T, precision=high), "dom")
    lower_step = jnp.linalg.cholesky(step_gram)
    coeffs = jax.scipy.linalg.cho_solve((lower_step, True), lower_rhs.T).T
    solution = jnp.dot(coeffs, basis, precision=high)
    residual = right_side - jnp.dot(coeffs, image, precision=high)
    gram_new = lax.psum(jnp.dot(residual, residual.T, precision=high), "dom")
    lower_new = jnp.linalg.cholesky(gram_new)
    new_basis = lower_solve(lower_new, residual)
    return (solution, residual, new_basis)


def solution(mesh):
    return jax.shard_map(
        per_device,
        mesh=mesh,
        in_specs=(
            P("dom", None),
            P("dom", None),
            P("dom", None),
            P("dom"),
            P("dom", None),
            P("dom"),
            P("dom"),
            P(None, "dom"),
        ),
        out_specs=(P(None, "dom"), P(None, "dom"), P(None, "dom")),
        check_vma=False,
    )
```

profile of v0, /device:TPU:1, one launch (start us, length us, event | category | flops | bytes accessed | tf_op | source)
XLA Modules:
  0.0 681.9 jit_solution(16039400882109215339)
XLA Ops:
  5.4 4.1 copy.30
  9.5 7.5 %copy.32 = bf16[256,64,64]{2,1,0:T(8,128)(2,1)} copy(bf16[256,64,64]{0,2,1:T(8,128)(2,1)} %bitcast.80) | data formatting | bytes 4194304 | tf_op jit(solution)/shard_map/reshape | solution.py:60
  17.0 57.4 %gather_fusion.1 = bf16[16384,32]{1,0:T(8,128)(2,1)} fusion(bf16[32,8192]{0,1:T(8,128)(2,1)S(1)} %copy.29, s32[16384]{0:T(1024)S(1)} %broadcast_clamp_fusion), kind=kCustom, calls=%fused_computation.1 | custom fusion | bytes 2162688 | tf_op jit(solution)/shard_map/gather | solution.py:59
  74.3 5.8 convolution_bitcast_fusion
  80.1 4.4 copy.33
  87.4 4.7 copy.34
  92.1 88.3 %scatter_custom_fusion = f32[32,4992]{0,1:T(8,128)S(1)} fusion(s32[16384]{0:T(1024)S(1)} %bitcast.89, f32[16384,32]{1,0:T(8,128)} %copy.34, f32[]{:T(128)} %constant.56.clone.1), kind=kCustom, calls=%fused_computation.15 | custom fusion | flops 524288 | bytes 639488 | tf_op jit(solution)/shard_map/scatter-add | solution.py:46
  180.5 8.9 %collective-permute-start = (f32[32,768]{0,1:T(8,128)S(1)}, f32[32,768]{0,1:T(8,128)}, u32[]{:S(2)}, u32[]{:S(2)}) collective-permute-start(f32[32,768]{0,1:T(8,128)S(1)} %get-tuple-element.8), channel_id=1, source_target_pairs={{1,0},{2,1},{3,2},{4,3},{5,4},{6,5},{7,6},{8,7},{9,8},{10,9},{11,1... | collective-permute-start | bytes 294920 | tf_op jit(solution)/shard_map/ppermute | solution.py:29
  193.2 7.6 %scatter_custom_fusion.1 = f32[32,3456]{0,1:T(8,128)S(1)} fusion(f32[32,3456]{0,1:T(8,128)S(1)} %slice.54, s32[768]{0:T(1024)S(1)} %fusion.30, f32[32,768]{0,1:T(8,128)} %collective-permute-done), kind=kCustom, calls=%fused_computation.24 | custom fusion | flops 24576 | bytes 540672 | tf_op jit(solution)/shard_map/scatter-add | solution.py:52
  200.8 7.1 %scatter_custom_fusion.2 = f32[32,3456]{0,1:T(8,128)S(1)} fusion(f32[32,3456]{0,1:T(8,128)S(1)} %scatter_custom_fusion.1, s32[768]{0:T(1024)S(1)} %fusion.31, f32[32,768]{0,1:T(8,128)} %collective-permute-done.1), kind=kCustom, calls=%fused_computation.22 | custom fusion | flops 24576 | bytes 540672 | tf_op jit(solution)/shard_map/scatter-add | solution.py:52
  210.9 105.8 %psum.21 = f32[32,32]{0,1:T(8,128)S(1)} all-reduce(f32[32,32]{0,1:T(8,128)S(1)} %fusion.36), channel_id=1, replica_groups=mesh['dom'=512] {'dom'}, use_global_device_ids=true, to_apply=%region_3.0 | all-reduce | flops 1024 | bytes 8192 | tf_op jit(solution)/shard_map/psum | solution.py:65
  327.2 3.0 gather_fusion.2
  332.3 3.0 gather_fusion.3
  338.1 3.3 collective-permute-done.3
  344.5 27.7 %gather_fusion.4 = f32[8192,32]{1,0:T(8,128)} fusion(f32[32,4992]{0,1:T(8,128)S(1)} %copy.42, s32[8192]{0:T(1024)S(1)} %broadcast_clamp_fusion.1), kind=kCustom, calls=%fused_computation.4 | custom fusion | bytes 2129920 | tf_op jit(solution)/shard_map/gather | solution.py:71
  372.2 4.1 copy.43
  381.9 3.6 copy.45
  385.5 46.0 %scatter_custom_fusion.3 = f32[32,4992]{0,1:T(8,128)} fusion(s32[8192]{0:T(1024)S(1)} %bitcast.86, f32[8192,32]{1,0:T(8,128)} %copy.45, f32[]{:T(128)} %constant.56.clone.1), kind=kCustom, calls=%fused_computation.13 | custom fusion | flops 262144 | bytes 639488 | tf_op jit(solution)/shard_map/scatter-add | solution.py:46
  435.4 3.6 collective-permute-start.5
  439.5 3.3 collective-permute-done.4
  442.9 7.1 %scatter_custom_fusion.4 = f32[32,3456]{0,1:T(8,128)S(1)} fusion(f32[32,3456]{0,1:T(8,128)S(1)} %slice-done, s32[768]{0:T(1024)S(1)} %fusion.30, f32[32,768]{0,1:T(8,128)} %collective-permute-done.4), kind=kCustom, calls=%fused_computation.20 | custom fusion | flops 24576 | bytes 540672 | tf_op jit(solution)/shard_map/scatter-add | solution.py:52
  450.0 7.3 %scatter_custom_fusion.5 = f32[32,3456]{0,1:T(8,128)S(1)} fusion(f32[32,3456]{0,1:T(8,128)S(1)} %scatter_custom_fusion.4, s32[768]{0:T(1024)S(1)} %fusion.31, f32[32,768]{0,1:T(8,128)} %collective-permute-done.5), kind=kCustom, calls=%fused_computation.18 | custom fusion | flops 24576 | bytes 540672 | tf_op jit(solution)/shard_map/scatter-add | solution.py:52
  460.2 107.5 %psum.22 = f32[32,32]{0,1:T(8,128)S(1)} all-reduce(f32[32,32]{0,1:T(8,128)S(1)} %fusion.37), channel_id=1, replica_groups=mesh['dom'=512] {'dom'}, use_global_device_ids=true, to_apply=%region_9.12 | all-reduce | flops 1024 | bytes 8192 | tf_op jit(solution)/shard_map/psum | solution.py:78
  579.4 94.2 %psum.23 = f32[32,32]{0,1:T(8,128)S(1)} all-reduce(f32[32,32]{0,1:T(8,128)S(1)} %fusion.40), channel_id=1, replica_groups=mesh['dom'=512] {'dom'}, use_global_device_ids=true, to_apply=%region_10.13 | all-reduce | flops 1024 | bytes 8192 | tf_op jit(solution)/shard_map/psum | solution.py:83
  (91 shorter events, 65.2 us)
Async XLA Ops:
  0.6 4.4 copy-start.7
  180.4 9.0 %copy-start.2 = (f32[32,4992]{0,1:T(8,128)}, f32[32,4992]{0,1:T(8,128)S(1)}, u32[]{:S(2)}) copy-start(f32[32,4992]{0,1:T(8,128)S(1)} %scatter_custom_fusion) | copy-start | bytes 1916932
  180.4 12.6 %copy-start.5 = (s32[1,768]{1,0:T(1,128)S(1)}, s32[1,768]{1,0:T(1,128)}, u32[]{:S(2)}) copy-start(s32[1,768]{1,0:T(1,128)} %param.14) | copy-start | bytes 9220
  180.4 12.6 %copy-start.6 = (s32[1,768]{1,0:T(1,128)S(1)}, s32[1,768]{1,0:T(1,128)}, u32[]{:S(2)}) copy-start(s32[1,768]{1,0:T(1,128)} %param.13) | copy-start | bytes 9220
  180.5 12.7 %collective-permute-start = (f32[32,768]{0,1:T(8,128)S(1)}, f32[32,768]{0,1:T(8,128)}, u32[]{:S(2)}, u32[]{:S(2)}) collective-permute-start(f32[32,768]{0,1:T(8,128)S(1)} %get-tuple-element.8), channel_id=1, source_target_pairs={{1,0},{2,1},{3,2},{4,3},{5,4},{6,5},{7,6},{8,7},{9,8},{10,9},{11,1... | collective-permute-start | bytes 294920 | tf_op jit(solution)/shard_map/ppermute | solution.py:29
  189.4 11.4 %collective-permute-start.1 = (f32[32,768]{0,1:T(8,128)S(1)}, f32[32,768]{0,1:T(8,128)}, u32[]{:S(2)}, u32[]{:S(2)}) collective-permute-start(f32[32,768]{0,1:T(8,128)S(1)} %get-tuple-element.7), channel_id=1, source_target_pairs={{0,1},{1,2},{2,3},{3,4},{4,5},{5,6},{6,7},{7,8},{8,9},{9,10},{10,1... | collective-permute-start | bytes 294920 | tf_op jit(solution)/shard_map/ppermute | solution.py:29
  207.9 117.5 %copy-start = (f32[32,3456]{0,1:T(8,128)}, f32[32,3456]{0,1:T(8,128)S(1)}, u32[]{:S(2)}) copy-start(f32[32,3456]{0,1:T(8,128)S(1)} %scatter_custom_fusion.2) | copy-start | bytes 1327108
  330.4 7.7 %collective-permute-start.2 = (f32[32,768]{1,0:T(8,128)S(1)}, f32[32,768]{1,0:T(8,128)S(1)}, u32[]{:S(2)}, u32[]{:S(2)}) collective-permute-start(f32[32,768]{1,0:T(8,128)S(1)} %bitcast.87), channel_id=1, source_target_pairs={{0,1},{1,2},{2,3},{3,4},{4,5},{5,6},{6,7},{7,8},{8,9},{9,10},{10,1... | collective-permute-start | bytes 294920 | tf_op jit(solution)/shard_map/ppermute | solution.py:29
  335.5 5.9 collective-permute-start.3
  372.2 4.1 copy-start.4
  372.2 4.2 copy-start.8
  385.5 53.5 %copy-start.1 = (f32[32,3456]{0,1:T(8,128)S(1)}, f32[32,3456]{0,1:T(8,128)}, u32[]{:S(2)}) copy-start(f32[32,3456]{0,1:T(8,128)} %copy-done) | copy-start | bytes 1327108
  433.5 9.4 %collective-permute-start.4 = (f32[32,768]{0,1:T(8,128)}, f32[32,768]{0,1:T(8,128)}, u32[]{:S(2)}, u32[]{:S(2)}) collective-permute-start(f32[32,768]{0,1:T(8,128)} %get-tuple-element.6), channel_id=1, source_target_pairs={{1,0},{2,1},{3,2},{4,3},{5,4},{6,5},{7,6},{8,7},{9,8},{10,9},{11,1... | collective-permute-start | bytes 294920 | tf_op jit(solution)/shard_map/ppermute | solution.py:29
  435.4 14.6 %collective-permute-start.5 = (f32[32,768]{0,1:T(8,128)S(1)}, f32[32,768]{0,1:T(8,128)}, u32[]{:S(2)}, u32[]{:S(2)}) collective-permute-start(f32[32,768]{0,1:T(8,128)S(1)} %get-tuple-element.5), channel_id=1, source_target_pairs={{0,1},{1,2},{2,3},{3,4},{4,5},{5,6},{6,7},{7,8},{8,9},{9,10},{10,1... | collective-permute-start | bytes 294920 | tf_op jit(solution)/shard_map/ppermute | solution.py:29
  439.5 3.3 slice-start
  578.9 102.8 %copy-start.3 = (f32[32,3456]{1,0:T(8,128)}, f32[32,3456]{1,0:T(8,128)S(1)}, u32[]{:S(2)}) copy-start(f32[32,3456]{1,0:T(8,128)S(1)} %sub.3) | copy-start | bytes 1327108
where the time goes:
time: 691 us; the launch traced here: 682 us
  blocking collectives  307 us (44%)
  other arithmetic  185 us (27%)
  local copies, waits for them, and re-layouts  138 us (20%)
  matrix products  21.9 us (3%)
  starting transfers between devices  20.9 us (3%)
    scatter-add x2, other arithmetic, spread(): jnp.zeros((tracers, owned + 2 * F), jnp.float32).at[:, slots].add(values)  134 us
    psum x1, blocking collectives, per_device(): step_gram = lax.psum(jnp.dot(basis, image.T, precision=high), 'dom')  107 us
    psum x1, blocking collectives, per_device(): sums = lax.psum((rhs_gram_local,), 'dom')  106 us
    psum x1, blocking collectives, per_device(): gram_new = lax.psum(jnp.dot(residual, residual.T, precision=high), 'dom')  94.2 us
    gather x1, local copies, waits for them, and re-layouts, per_device(): gathered = source_values[:, columns].reshape(tracers, pairs, NP)  57.4 us
    scatter-add x4, other arithmetic, settle(): return own_part.at[:, highs].add(from_above).at[:, lows].add(from_below)  29.2 us
    gather x1, local copies, waits for them, and re-layouts, per_device(): jnp.concatenate([basis, below, above], axis=1)[:, flat_ids]  27.7 us
    ppermute x6, starting transfers between devices, shifted(): return lax.ppermute(value, axis, pairs)  20.9 us
  transfers between devices with their start and end apart: 6, of which 2 were waited for; matrix products, arithmetic and copies ran while one was open for 3% of the time, Pallas kernels for 0%

commit v1 on v0

v1 whole, which is shorter than its diff:
```python
import jax
import jax.numpy as jnp
import numpy as np
from jax import lax
from jax.experimental import pallas as pl
from jax.experimental.pallas import tpu as pltpu
from jax.sharding import Mesh
from jax.sharding import PartitionSpec as P

TR = 32
NODE_DEV = 3456
F = 768
SLOTS = 8192
L = 512
OWN_BLOCKS = 7
HALO_BLOCKS = 3
PAD = OWN_BLOCKS * L - NODE_DEV
BF = jnp.bfloat16
F32 = jnp.float32
I16 = jnp.int16
NT = (((1,), (1,)), ((), ()))
AXES = ("x", "z", "y", "c")
SIZES = {"x": 4, "z": 8, "y": 8, "c": 2}

line_mass = (
    np.array(
        [
            [128.0, 99.0, -36.0, 19.0],
            [99.0, 648.0, -81.0, -36.0],
            [-36.0, -81.0, 648.0, 99.0],
            [19.0, -36.0, 99.0, 128.0],
        ]
    )
    / 504.0
)
mass_table = np.kron(np.kron(line_mass, line_mass), line_mass)


def mass_tiles():
    order = np.arange(64).reshape(32, 2).T.reshape(-1)
    block = mass_table[np.ix_(order, order)].astype(np.float32)
    whole = np.kron(np.eye(4, dtype=np.float32), block)
    high = whole.astype(jnp.bfloat16)
    low = (whole - high.astype(np.float32)).astype(jnp.bfloat16)
    return np.concatenate([high, low], axis=1)


def params(**extra):
    return pltpu.CompilerParams(vmem_limit_bytes=56 * 2**20, **extra)


def vmem(count):
    return [pl.BlockSpec(memory_space=pltpu.VMEM)] * count


def shape(dims, kind=F32):
    return jax.ShapeDtypeStruct(dims, kind)


def aligned(start, size):
    return pl.ds(pl.multiple_of(start, size), size)


def split2(value):
    high = value.astype(BF)
    low = (value - high.astype(F32)).astype(BF)
    return high, low


def one_hot(row):
    spread = jnp.broadcast_to(row.astype(I16), (L, 128))
    index = lax.broadcasted_iota(I16, (L, 128), 0)
    return jnp.where(spread == index, jnp.ones((), BF), jnp.zeros((), BF))


def tiles_of(ids, count):
    blocks = lax.shift_right_logical(ids, 9)
    places = ids & (L - 1)
    hot = jnp.concatenate([one_hot(places[j : j + 1]) for j in range(count)], axis=1)
    return hot, [blocks[j : j + 1] for j in range(count)]


def masked(parts, blocks, first, number):
    out = []
    for j, row in enumerate(blocks):
        here = jnp.broadcast_to(row.astype(I16), (2 * TR, 128))
        tile = parts[:, j * 128 : (j + 1) * 128]
        out.append(
            jnp.concatenate(
                [jnp.where(here == first + b, tile, jnp.zeros((), BF)) for b in range(number)], axis=0
            )
        )
    return jnp.concatenate(out, axis=1)


def picked(rows, blocks, first, number, start):
    out = []
    for j, row in enumerate(blocks):
        here = jnp.broadcast_to(row, (TR, 128))
        tile = start[j]
        for b in range(number):
            tile = jnp.where(here == first + b, rows[b * TR : (b + 1) * TR, j * 128 : (j + 1) * 128], tile)
        out.append(tile)
    return out


def add_scatter(acc, parts, ids, count, first, number):
    hot, blocks = tiles_of(ids, count)
    acc[...] += lax.dot_general(
        masked(parts, blocks, first, number), hot, NT, preferred_element_type=F32
    )


def fold(acc, b):
    return acc[b * 2 * TR : b * 2 * TR + TR] + acc[b * 2 * TR + TR : (b + 1) * 2 * TR]


CHUNK = 2048
TILES = CHUNK // 128
UNROLL = 32


def rhs_kernel(tgt_ref, src_ref, conn_ref, pb_ref, sv_ref, ids_ref, parts_ref, halo_ref, blocks, source, total, wide, acc):
    zero = jnp.zeros((), F32)
    zero16 = jnp.zeros((), BF)
    for g in range(16):
        stack = jnp.concatenate([sv_ref[:, (4 * g + k) * 128 : (4 * g + k + 1) * 128] for k in range(4)], axis=0)
        source[g * 128 : (g + 1) * 128, :] = stack.astype(F32).T.astype(BF)
    @pl.loop(0, 16)
    def _(g):
        for c in range(32):
            rows = pb_ref[aligned(g * 16, 16), c * 128 : (c + 1) * 128].astype(F32)
            blocks[pl.ds(g * 512 + c, 16, stride=32), :] = rows

    conn = conn_ref[...]
    row = lax.broadcasted_iota(jnp.int32, (64, 64), 0)
    col = lax.broadcasted_iota(jnp.int32, (64, 64), 1)
    swap = jnp.where(row == 2 * (col & 31) + lax.shift_right_logical(col, 5), 1.0, 0.0).astype(BF)
    upper = lax.shift_right_logical(conn, 7).astype(F32).astype(BF)
    lower = (conn & 127).astype(F32).astype(BF)
    ids = jnp.dot(upper, swap, preferred_element_type=F32) * 128.0 + jnp.dot(lower, swap, preferred_element_type=F32)
    ids = ids.astype(jnp.int32)
    ids = jnp.where(ids >= NODE_DEV, ids + PAD, ids)
    wide[...] = jnp.concatenate([ids, ids], axis=1)
    lane64 = lax.broadcasted_iota(jnp.int32, (64, 128), 1)
    ids_ref[...] = jnp.where(lane64 < 64, wide[pl.ds(0, 64, stride=2), :], wide[pl.ds(1, 64, stride=2), :])

    total[...] = jnp.zeros_like(total)
    low32 = lax.broadcasted_iota(jnp.int32, (32, 128), 1) < 64
    group = lax.shift_right_logical(lane64, 5).astype(I16)

    @pl.loop(0, 256 // UNROLL)
    def _(i):
        for u in range(UNROLL):
            p = i * UNROLL + u
            s = src_ref[p]
            e = tgt_ref[p]
            k = lax.shift_right_logical(s, 1) & 3
            start = lax.shift_right_logical(s, 3) * 128 + (s & 1) * 64
            value = jnp.where(group == k.astype(I16), source[aligned(start, 64), :], zero16)
            block = blocks[aligned(p * 32, 32), :]
            rows = jnp.concatenate([jnp.where(low32, block, zero), jnp.where(low32, zero, block)], axis=0).astype(BF)
            total[aligned(e * 64, 64), :] += jnp.dot(
                rows, jnp.concatenate([value, value], axis=0), preferred_element_type=F32
            )

    lanes = lax.shift_right_logical(lax.broadcasted_iota(jnp.int32, (128, 128), 1), 5)
    odd = (lanes & 1) == 1
    up = lanes >= 2

    def join(a, b, mask, by):
        return jnp.where(mask, b, a) + pltpu.roll(jnp.where(mask, a, b), by, 1)

    @pl.loop(0, 16, unroll=4)
    def _(g):
        e = [total[aligned(g * 512 + j * 128, 128), :] for j in range(4)]
        both = join(join(e[0], e[1], odd, 32), join(e[2], e[3], odd, 32), up, 64).T
        for j in range(4):
            high, low = split2(both[j * TR : (j + 1) * TR])
            parts_ref[:, aligned(g * 512 + j * 128, 128)] = jnp.concatenate([high, low], axis=0)

    scatter_halo(ids_ref, parts_ref, halo_ref, acc)


def scatter_halo(ids_ref, parts_ref, halo_ref, acc):
    acc[...] = jnp.zeros_like(acc)

    @pl.loop(0, SLOTS // CHUNK)
    def _(k):
        add_scatter(
            acc, parts_ref[:, aligned(k * CHUNK, CHUNK)], ids_ref[aligned(k * TILES, TILES), :], TILES, OWN_BLOCKS, HALO_BLOCKS
        )

    for b in range(HALO_BLOCKS):
        halo_ref[:, b * L : (b + 1) * L] = fold(acc, b)


def right_side_halo(tgt, src, conn, pair_blocks, source_values):
    return pl.pallas_call(
        rhs_kernel,
        out_shape=(shape((64, 128), jnp.int32), shape((2 * TR, SLOTS), BF), shape((TR, 2 * F))),
        in_specs=[pl.BlockSpec(memory_space=pltpu.SMEM)] * 2 + vmem(3),
        out_specs=tuple(vmem(3)),
        scratch_shapes=[
            pltpu.VMEM((8192, 128), F32),
            pltpu.VMEM((2048, 128), BF),
            pltpu.VMEM((8192, 128), F32),
            pltpu.VMEM((128, 128), jnp.int32),
            pltpu.VMEM((HALO_BLOCKS * 2 * TR, L), F32),
        ],
        compiler_params=params(),
        name="rhs",
    )(tgt, src, conn, pair_blocks, source_values)


def own_kernel(ids_ref, parts_ref, out_ref, acc):
    acc[...] = jnp.zeros_like(acc)

    @pl.loop(0, SLOTS // CHUNK)
    def _(k):
        add_scatter(acc, parts_ref[:, aligned(k * CHUNK, CHUNK)], ids_ref[aligned(k * TILES, TILES), :], TILES, 0, OWN_BLOCKS)

    for b in range(OWN_BLOCKS):
        out_ref[:, b * L : (b + 1) * L] = fold(acc, b)


def scatter_own(ids, parts):
    return pl.pallas_call(
        own_kernel,
        out_shape=shape((TR, OWN_BLOCKS * L)),
        in_specs=vmem(2),
        out_specs=vmem(1)[0],
        scratch_shapes=[pltpu.VMEM((OWN_BLOCKS * 2 * TR, L), F32)],
        compiler_params=params(),
        cost_estimate=pl.CostEstimate(flops=2 * 448 * 512 * 8192, bytes_accessed=2**21, transcendentals=0),
        name="own",
    )(ids, parts)


def settle(own_ref, above_ref, below_ref, highs_ref, lows_ref, acc):
    rows = [highs_ref[:, j * 128 : (j + 1) * 128] for j in range(6)] + [lows_ref[:, j * 128 : (j + 1) * 128] for j in range(6)]
    hot = jnp.concatenate([one_hot(r & (L - 1)) for r in rows], axis=1)
    blocks = [lax.shift_right_logical(r, 9) for r in rows]
    high, low = split2(jnp.concatenate([above_ref[...], below_ref[...]], axis=1))
    parts = jnp.concatenate([high, low], axis=0)
    acc[...] = lax.dot_general(masked(parts, blocks, 0, OWN_BLOCKS), hot, NT, preferred_element_type=F32)
    whole = [own_ref[:, b * L : (b + 1) * L] + fold(acc, b) for b in range(OWN_BLOCKS)]
    return whole, hot, blocks


def settle_kernel(own_ref, above_ref, below_ref, highs_ref, lows_ref, out_ref, up_ref, down_ref, table_ref, acc):
    whole, hot, blocks = settle(own_ref, above_ref, below_ref, highs_ref, lows_ref, acc)
    for b, value in enumerate(whole):
        end = min(NODE_DEV, (b + 1) * L)
        out_ref[:, b * L : end] = value[:, : end - b * L]
        high, low = split2(value)
        table_ref[b * TR : (b + 1) * TR, :] = jnp.concatenate([high, low], axis=1)
    rows = jnp.dot(table_ref[...], jnp.concatenate([hot, hot], axis=0), preferred_element_type=F32)
    zeros = [jnp.zeros((TR, 128), F32)] * 12
    values = picked(rows, blocks, 0, OWN_BLOCKS, zeros)
    for j in range(6):
        up_ref[:, j * 128 : (j + 1) * 128] = values[j]
        down_ref[:, j * 128 : (j + 1) * 128] = values[6 + j]


def settle_right(own, above, below, highs, lows):
    return pl.pallas_call(
        settle_kernel,
        out_shape=(
            shape((TR, NODE_DEV)),
            shape((TR, F)),
            shape((TR, F)),
            shape((OWN_BLOCKS * TR, 2 * L), BF),
        ),
        in_specs=vmem(5),
        out_specs=tuple(vmem(4)),
        scratch_shapes=[pltpu.VMEM((OWN_BLOCKS * 2 * TR, L), F32)],
        compiler_params=params(),
        name="settle",
    )(own, above, below, highs, lows)


def gather_kernel(ids_ref, table_ref, jac_ref, out_ref, scale_ref, wide):
    wide[...] = jnp.broadcast_to(jac_ref[...], (128, 128)).T
    lane64 = lax.broadcasted_iota(jnp.int32, (64, 128), 1)
    scale_ref[...] = jnp.where(lane64 < 64, wide[pl.ds(0, 64, stride=2), :], wide[pl.ds(1, 64, stride=2), :])

    @pl.loop(0, SLOTS // CHUNK)
    def _(k):
        hot, blocks = tiles_of(ids_ref[aligned(k * TILES, TILES), :], TILES)
        rows = jnp.dot(table_ref[...], jnp.concatenate([hot, hot], axis=0), preferred_element_type=F32)
        values = picked(rows, blocks, 0, OWN_BLOCKS, [jnp.zeros((TR, 128), F32)] * TILES)
        out_ref[:, aligned(k * CHUNK, CHUNK)] = jnp.concatenate(values, axis=1)


def gather_own(ids, table, jac):
    return pl.pallas_call(
        gather_kernel,
        out_shape=(shape((TR, SLOTS)), shape((64, 128))),
        in_specs=vmem(3),
        out_specs=tuple(vmem(2)),
        scratch_shapes=[pltpu.VMEM((128, 128), F32)],
        compiler_params=params(),
        cost_estimate=pl.CostEstimate(flops=2 * 448 * 512 * 8192, bytes_accessed=2**21, transcendentals=0),
        name="gather",
    )(ids, table, jac)


def mass_kernel(ids_ref, start_ref, below_ref, above_ref, scale_ref, mass_ref, parts_ref, halo_ref, table, acc):
    both = jnp.concatenate([below_ref[...], above_ref[...]], axis=1)
    for b in range(HALO_BLOCKS):
        high, low = split2(both[:, b * L : (b + 1) * L])
        table[b * TR : (b + 1) * TR, :] = jnp.concatenate([high, low], axis=1)
    acc[...] = jnp.zeros_like(acc)

    @pl.loop(0, SLOTS // CHUNK)
    def _(k):
        hot, blocks = tiles_of(ids_ref[aligned(k * TILES, TILES), :], TILES)
        rows = jnp.dot(table[...], jnp.concatenate([hot, hot], axis=0), preferred_element_type=F32)
        start = [start_ref[:, aligned(k * CHUNK + j * 128, 128)] for j in range(TILES)]
        values = picked(rows, blocks, OWN_BLOCKS, HALO_BLOCKS, start)
        split = [split2(jnp.concatenate(values[2 * j : 2 * j + 2], axis=1)) for j in range(TILES // 2)]
        highs = jnp.concatenate([s[0] for s in split], axis=0)
        lows = jnp.concatenate([s[1] for s in split], axis=0)
        image = (
            jnp.dot(highs, mass_ref[:, :256], preferred_element_type=F32)
            + jnp.dot(lows, mass_ref[:, :256], preferred_element_type=F32)
            + jnp.dot(highs, mass_ref[:, 256:], preferred_element_type=F32)
        )
        tiles = []
        scales = scale_ref[aligned(k * TILES, TILES), :]
        for j in range(TILES):
            tile = image[(j // 2) * TR : (j // 2 + 1) * TR, (j % 2) * 128 : (j % 2 + 1) * 128]
            high, low = split2(tile * scales[j : j + 1])
            tiles.append(jnp.concatenate([high, low], axis=0))
        parts = jnp.concatenate(tiles, axis=1)
        parts_ref[:, aligned(k * CHUNK, CHUNK)] = parts
        acc[...] += lax.dot_general(
            masked(parts, blocks, OWN_BLOCKS, HALO_BLOCKS), hot, NT, preferred_element_type=F32
        )

    for b in range(HALO_BLOCKS):
        halo_ref[:, b * L : (b + 1) * L] = fold(acc, b)


def mass_halo(ids, start, below, above, scale, mass):
    return pl.pallas_call(
        mass_kernel,
        out_shape=(shape((2 * TR, SLOTS), BF), shape((TR, 2 * F))),
        in_specs=vmem(6),
        out_specs=tuple(vmem(2)),
        scratch_shapes=[
            pltpu.VMEM((HALO_BLOCKS * TR, 2 * L), BF),
            pltpu.VMEM((HALO_BLOCKS * 2 * TR, L), F32),
        ],
        compiler_params=params(),
        name="mass",
    )(ids, start, below, above, scale, mass)


def lay_flat(square):
    return jnp.concatenate([square[8 * i : 8 * i + 8] for i in range(4)], axis=1)


def lay_square(flat):
    return jnp.concatenate([flat[:, 32 * i : 32 * i + 32] for i in range(4)], axis=0)


def gram_kernel(own_ref, above_ref, below_ref, highs_ref, lows_ref, right_ref, out_ref, gram_ref, acc):
    whole, _, _ = settle(own_ref, above_ref, below_ref, highs_ref, lows_ref, acc)
    for b, value in enumerate(whole):
        end = min(NODE_DEV, (b + 1) * L)
        out_ref[:, b * L : end] = value[:, : end - b * L]
    right = split2(right_ref[...])
    image = split2(out_ref[...])
    stack = jnp.concatenate([right[0], image[0], right[1], image[1]], axis=0)
    full = lax.dot_general(stack, stack, NT, preferred_element_type=F32)
    full = full[:64] + full[64:]
    full = full[:, :64] + full[:, 64:]
    cross = full[:TR, TR:]
    cross = 0.5 * (cross + full[TR:, :TR])
    for i, g in enumerate((full[:TR, :TR], cross, full[TR:, TR:])):
        gram_ref[8 * i : 8 * i + 8, :] = lay_flat(g)


def grams(own, above, below, highs, lows, right):
    return pl.pallas_call(
        gram_kernel,
        out_shape=(shape((TR, NODE_DEV)), shape((24, 128))),
        in_specs=vmem(6),
        out_specs=tuple(vmem(2)),
        scratch_shapes=[pltpu.VMEM((OWN_BLOCKS * 2 * TR, L), F32)],
        compiler_params=params(),
        name="grams",
    )(own, above, below, highs, lows, right)


def hdot(a, b, dims=(((1,), (0,)), ((), ()))):
    return lax.dot_general(a, b, dims, precision=lax.Precision.HIGHEST, preferred_element_type=F32)


def final_kernel(gram_ref, right_ref, image_ref, sol_ref, res_ref, new_ref):
    total = gram_ref[0]
    for i in range(1, gram_ref.shape[0]):
        total = total + gram_ref[i]
    rhs, cross, images = (lay_square(total[8 * i : 8 * i + 8]) for i in range(3))
    row = lax.broadcasted_iota(jnp.int32, (TR, 64), 0)
    col = lax.broadcasted_iota(jnp.int32, (TR, 64), 1)
    cross = 0.5 * (cross + cross.T)

    work = jnp.concatenate([cross, rhs], axis=1)
    for k in range(TR):
        line = work[k : k + 1] * (1.0 / work[k : k + 1, k : k + 1])
        column = jnp.where(row[:, :1] == k, 0.0, work[:, k : k + 1])
        work = jnp.where(row == k, line, work) - column * line
    weights_t = work[:, TR:]
    weights = weights_t.T
    half = hdot(weights, cross)
    gram = rhs - half - half.T + hdot(hdot(weights, images), weights_t)
    gram = 0.5 * (gram + gram.T)

    work = jnp.concatenate([gram, jnp.where(row[:, :TR] == col[:, :TR], 1.0, 0.0)], axis=1)
    for k in range(TR):
        line = work[k : k + 1] * lax.rsqrt(work[k : k + 1, k : k + 1])
        column = work[:, k : k + 1] * lax.rsqrt(work[k : k + 1, k : k + 1])
        column = jnp.where(row[:, :1] > k, column, 0.0)
        work = jnp.where(row == k, line, work) - column * line
    inverse = work[:, TR:]

    mixed = hdot(inverse, weights)
    zero = jnp.zeros((TR, TR), F32)
    eye = jnp.where(row[:, :TR] == col[:, :TR], 1.0, 0.0)
    coeffs = jnp.concatenate(
        [
            jnp.concatenate([weights, zero], axis=1),
            jnp.concatenate([zero, -weights], axis=1),
            jnp.concatenate([inverse, -mixed], axis=1),
        ],
        axis=0,
    )
    high, low = split2(coeffs)
    lhs = jnp.concatenate([high, high, low], axis=1)
    right = right_ref[...]
    rh, rl = split2(right)
    ih, il = split2(image_ref[...])
    stack = jnp.concatenate([rh, ih, rl, il, rh, ih], axis=0)
    out = jnp.dot(lhs, stack, preferred_element_type=F32)
    sol_ref[...] = out[:TR]
    res_ref[...] = right + out[TR : 2 * TR]
    new_ref[...] = out[2 * TR :]


def finish(gram, right, image):
    return pl.pallas_call(
        final_kernel,
        out_shape=(shape((TR, NODE_DEV)),) * 3,
        in_specs=vmem(3),
        out_specs=tuple(vmem(3)),
        compiler_params=params(),
        name="finish",
    )(gram, right, image)


def shifted(value, by):
    pairs = [(i, i + by) for i in range(512) if 0 <= i + by < 512]
    return lax.ppermute(value, AXES, pairs)


def exchanged(value, axes):
    count = int(np.prod([SIZES[a] for a in axes]))
    copies = lax.optimization_barrier(jnp.broadcast_to(value[None], (count,) + value.shape))
    return lax.all_to_all(copies, axes, 0, 0)


def per_device(connectivity, send_down, send_up, jacobian, pair_blocks, pair_target, pair_source, source_values):
    lows = send_down
    highs = send_up
    mass = jnp.asarray(mass_tiles())
    ids, parts, halo = right_side_halo(pair_target, pair_source, connectivity, pair_blocks, source_values)
    above = shifted(halo[:, :F], -1)
    below = shifted(halo[:, F:], 1)
    own = scatter_own(ids, parts)
    right, up, down, table = settle_right(own, above, below, highs, lows)
    below = shifted(up, 1)
    above = shifted(down, -1)
    start, scale = gather_own(ids, table, jacobian[None, :])
    parts, halo = mass_halo(ids, start, below, above, scale, mass)
    above = shifted(halo[:, :F], -1)
    below = shifted(halo[:, F:], 1)
    own = scatter_own(ids, parts)
    image, gram = grams(own, above, below, highs, lows, right)
    gram = exchanged(gram, ("x", "y")).sum(0)
    gram = exchanged(gram, ("z", "c"))
    return finish(gram, right, image)


def solution(mesh):
    mesh = Mesh(mesh.devices.reshape(4, 8, 8, 2), AXES)
    return jax.shard_map(
        per_device,
        mesh=mesh,
        in_specs=(
            P(AXES, None),
            P(AXES, None),
            P(AXES, None),
            P(AXES),
            P(AXES, None),
            P(AXES),
            P(AXES),
            P(None, AXES),
        ),
        out_specs=(P(None, AXES), P(None, AXES), P(None, AXES)),
        check_vma=False,
    )
```

time: 691 us -> 136 us (0.20); the launches traced: 682 us -> 135 us
  blocking collectives: 307 us -> 47.5 us
  other arithmetic: 185 us -> 0.04 us
  local copies, waits for them, and re-layouts: 138 us -> 6.73 us
  Pallas kernels: 0 us -> 60.6 us
  matrix products: 21.9 us -> 0 us
    psum x3 -> x0, blocking collectives: 307 us -> none  [the longest x1 107 us: per_device(): step_gram = lax.psum(jnp.dot(basis, image.T, precision=high), 'dom')]
    scatter-add x6 -> x0, other arithmetic: 163 us -> none  [the longest x2 134 us: spread(): jnp.zeros((tracers, owned + 2 * F), jnp.float32).at[:, slots].add(values)]
    gather x7 -> x0, local copies, waits for them, and re-layouts: 92.1 us -> none  [the longest x1 57.4 us: per_device(): gathered = source_values[:, columns].reshape(tracers, pairs, NP)]
    pallas_call x0 -> x8, Pallas kernels: none -> 60.6 us  [the longest x1 15.3 us: right_side_halo(): pl.pallas_call(rhs_kernel, out_shape=(shape((64, 128), jnp.int32), shape(...]
    all_to_all x0 -> x2, blocking collectives: none -> 47.5 us  [exchanged(): return lax.all_to_all(copies, axes, 0, 0)]
    reshape x8 -> x0, local copies, waits for them, and re-layouts: 24.6 us -> none  [the longest x2 7.58 us: per_device(): right_side = settle(spread(contrib.reshape(tracers, pairs * NP), targets))]
    another operation x15 -> x0, other arithmetic: 20 us -> none  [the longest x4 6.17 us: lower_solve(): return jax.scipy.linalg.solve_triangular(lower, matrix, lower=True)]
    dot_general x7 -> x0, matrix products: 17.5 us -> none  [the longest x1 5.79 us: per_device(): jnp.einsum('pij,tpj->tpi', mixed, gathered, preferred_element_type=jnp.fl...]
  transfers between devices with their start and end apart: 6 -> 6, of which waited for: 2 -> 0; matrix products, arithmetic and copies ran while one was open for 3% -> 0% of each run, Pallas kernels for 0% -> 15%
where the time goes in v1:
time: 136 us; the launch traced here: 135 us
  Pallas kernels  60.6 us (45%)
  blocking collectives  47.5 us (35%)
  starting transfers between devices  19.5 us (14%)
  local copies, waits for them, and re-layouts  6.73 us (5%)
    all_to_all x2, blocking collectives, exchanged(): return lax.all_to_all(copies, axes, 0, 0)  47.5 us
    ppermute x6, starting transfers between devices, shifted(): return lax.ppermute(value, AXES, pairs)  19.5 us
    pallas_call x1, Pallas kernels, right_side_halo(): pl.pallas_call(rhs_kernel, out_shape=(shape((64, 128), jnp.int32), shape(...  15.3 us
    pallas_call x2, Pallas kernels, scatter_own(): pl.pallas_call(own_kernel, out_shape=shape((TR, OWN_BLOCKS * L)), in_spec...  13.5 us
    pallas_call x1, Pallas kernels, mass_halo(): pl.pallas_call(mass_kernel, out_shape=(shape((2 * TR, SLOTS), BF), shape(...  9.08 us
    pallas_call x1, Pallas kernels, finish(): pl.pallas_call(final_kernel, out_shape=(shape((TR, NODE_DEV)),) * 3, in_s...  8.9 us
    pallas_call x1, Pallas kernels, gather_own(): pl.pallas_call(gather_kernel, out_shape=(shape((TR, SLOTS)), shape((64, 1...  6.63 us
    unnamed x13, local copies, waits for them, and re-layouts  4.08 us
  transfers between devices with their start and end apart: 6, of which 0 were waited for; matrix products, arithmetic and copies ran while one was open for 0% of the time, Pallas kernels for 15%

profile of v1, /device:TPU:1, one launch (start us, length us, event | category | flops | bytes accessed | tf_op | source)
XLA Modules:
  0.0 135.1 jit_solution(9062803398407143230)
XLA Ops:
  0.6 1.5 %copy.13.conn_ref = s32[128,64]{1,0:T(8,128)} copy(s32[128,64]{0,1:T(8,128)} %param.9) | data formatting | bytes 65536 | tf_op args[0]
  2.1 15.3 %rhs.1 = (s32[64,128]{1,0:T(8,128)}, bf16[64,8192]{1,0:T(8,128)(2,1)}, f32[32,1536]{1,0:T(8,128)}) custom-call(s32[256]{0:T(256)} %tgt_ref.1, s32[256]{0:T(256)} %src_ref.1, s32[128,64]{1,0:T(8,128)} %copy.13.conn_ref, bf16[256,4096]{1,0:T(8,128)(2,1)} %pb_ref.1, bf16[32,8192]{1,0:T(8,128)(2,1)} %sv_ref.1), custom_call_target="tpu_custom_call" | custom-call | tf_op jit(solution)/shard_map/rhs/pallas_call | solution.py:199
  17.4 1.0 fusion.1
  18.4 4.6 %collective-permute-start.1 = (f32[32,768]{1,0:T(8,128)S(1)}, f32[32,768]{1,0:T(8,128)S(1)}, u32[]{:S(2)}, u32[]{:S(2)}) collective-permute-start(f32[32,768]{1,0:T(8,128)S(1)} %get-tuple-element.31), channel_id=1, source_target_pairs={{0,1},{1,2},{2,3},{3,4},{4,5},{5,6},{6,7},{7,8},{8,9},{9,10},{10,1... | collective-permute-start | bytes 294920 | tf_op jit(solution)/shard_map/ppermute | solution.py:466
  23.0 5.5 %collective-permute-start = (f32[32,768]{1,0:T(8,128)S(1)}, f32[32,768]{1,0:T(8,128)S(1)}, u32[]{:S(2)}, u32[]{:S(2)}) collective-permute-start(f32[32,768]{1,0:T(8,128)S(1)} %get-tuple-element.32), channel_id=1, source_target_pairs={{1,0},{2,1},{3,2},{4,3},{5,4},{6,5},{7,6},{8,7},{9,8},{10,9},{11,1... | collective-permute-start | bytes 294920 | tf_op jit(solution)/shard_map/ppermute | solution.py:466
  28.5 6.7 %own.2.own_ref = f32[32,3584]{1,0:T(8,128)} custom-call(s32[64,128]{1,0:T(8,128)} %get-tuple-element.16.ids_ref, bf16[64,8192]{1,0:T(8,128)(2,1)} %get-tuple-element.17.parts_ref), custom_call_target="tpu_custom_call" | custom-call | flops 3758096384 | bytes 2097152 | tf_op jit(solution)/shard_map/own/pallas_call | solution.py:228
  35.2 0.6 copy-done
  35.9 0.6 copy-done.4
  36.5 3.5 %settle.1 = (f32[32,3456]{1,0:T(8,128)}, f32[32,768]{1,0:T(8,128)}, f32[32,768]{1,0:T(8,128)}, bf16[224,1024]{1,0:T(8,128)(2,1)}) custom-call(f32[32,3584]{1,0:T(8,128)} %own.2.own_ref, f32[32,768]{1,0:T(8,128)} %copy-done.4, f32[32,768]{1,0:T(8,128)} %copy-done, s32[1,768]{1,0:T(1,128)} %highs_ref.3, s32[1,768]{1,0:T(1,128)} %lows_ref.3), custom_call_target="tpu_custom_call" | custom-call | tf_op jit(solution)/shard_map/settle/pallas_call | solution.py:267
  40.0 1.9 %collective-permute-start.2 = (f32[32,768]{1,0:T(8,128)}, f32[32,768]{1,0:T(8,128)S(1)}, u32[]{:S(2)}, u32[]{:S(2)}) collective-permute-start(f32[32,768]{1,0:T(8,128)} %get-tuple-element.21), channel_id=1, source_target_pairs={{0,1},{1,2},{2,3},{3,4},{4,5},{5,6},{6,7},{7,8},{8,9},{9,10},{10,1... | collective-permute-start | bytes 294920 | tf_op jit(solution)/shard_map/ppermute | solution.py:466
  41.9 2.4 %collective-permute-start.3 = (f32[32,768]{1,0:T(8,128)}, f32[32,768]{1,0:T(8,128)S(1)}, u32[]{:S(2)}, u32[]{:S(2)}) collective-permute-start(f32[32,768]{1,0:T(8,128)} %get-tuple-element.22), channel_id=1, source_target_pairs={{1,0},{2,1},{3,2},{4,3},{5,4},{6,5},{7,6},{8,7},{9,8},{10,9},{11,1... | collective-permute-start | bytes 294920 | tf_op jit(solution)/shard_map/ppermute | solution.py:466
  44.3 6.6 %gather.1 = (f32[32,8192]{1,0:T(8,128)}, f32[64,128]{1,0:T(8,128)}) custom-call(s32[64,128]{1,0:T(8,128)} %get-tuple-element.16.ids_ref, bf16[224,1024]{1,0:T(8,128)(2,1)} %get-tuple-element.19.table_ref, f32[1,128]{1,0:T(1,128)} %bitcast.1), custom_call_target="tpu_custom_call" | custom-call | flops 3758096384 | bytes 2097152 | tf_op jit(solution)/shard_map/gather/pallas_call | solution.py:297
  51.0 0.6 copy-done.1
  51.6 9.1 %mass.1 = (bf16[64,8192]{1,0:T(8,128)(2,1)}, f32[32,1536]{1,0:T(8,128)}) custom-call(s32[64,128]{1,0:T(8,128)} %get-tuple-element.16.ids_ref, f32[32,8192]{1,0:T(8,128)} %get-tuple-element.20.start_ref, f32[32,768]{1,0:T(8,128)} %copy-done.1, f32[32,768]{1,0:T(8,128)} %copy-done.3, f32[64,128]{1,0:T(8,128)} %get-tuple-element.23.scale_ref, ...), custom_call_target="tpu_custom_call" | custom-call | tf_op jit(solution)/shard_map/mass/pallas_call | solution.py:347
  60.7 1.0 fusion
  61.7 3.1 %collective-permute-start.5 = (f32[32,768]{1,0:T(8,128)S(1)}, f32[32,768]{1,0:T(8,128)S(1)}, u32[]{:S(2)}, u32[]{:S(2)}) collective-permute-start(f32[32,768]{1,0:T(8,128)S(1)} %get-tuple-element.29), channel_id=1, source_target_pairs={{0,1},{1,2},{2,3},{3,4},{4,5},{5,6},{6,7},{7,8},{8,9},{9,10},{10,1... | collective-permute-start | bytes 294920 | tf_op jit(solution)/shard_map/ppermute | solution.py:466
  64.8 1.9 %collective-permute-start.4 = (f32[32,768]{1,0:T(8,128)S(1)}, f32[32,768]{1,0:T(8,128)S(1)}, u32[]{:S(2)}, u32[]{:S(2)}) collective-permute-start(f32[32,768]{1,0:T(8,128)S(1)} %get-tuple-element.30), channel_id=1, source_target_pairs={{1,0},{2,1},{3,2},{4,3},{5,4},{6,5},{7,6},{8,7},{9,8},{10,9},{11,1... | collective-permute-start | bytes 294920 | tf_op jit(solution)/shard_map/ppermute | solution.py:466
  66.7 6.7 %own.3.own_ref = f32[32,3584]{1,0:T(8,128)} custom-call(s32[64,128]{1,0:T(8,128)} %get-tuple-element.16.ids_ref, bf16[64,8192]{1,0:T(8,128)(2,1)} %get-tuple-element.24.parts_ref), custom_call_target="tpu_custom_call" | custom-call | flops 3758096384 | bytes 2097152 | tf_op jit(solution)/shard_map/own/pallas_call | solution.py:228
  73.5 0.6 copy-done.2
  74.1 3.7 %grams.1 = (f32[32,3456]{1,0:T(8,128)}, f32[24,128]{1,0:T(8,128)}) custom-call(f32[32,3584]{1,0:T(8,128)} %own.3.own_ref, f32[32,768]{1,0:T(8,128)} %copy-done.5, f32[32,768]{1,0:T(8,128)} %copy-done.2, s32[1,768]{1,0:T(1,128)} %highs_ref.3, s32[1,768]{1,0:T(1,128)} %lows_ref.3, f32[32,3456]{1,0:T(8,128)} %get-tuple-element.26.right_ref), custom_call_target="tpu_custom_call" | custom-call | tf_op jit(solution)/shard_map/grams/pallas_call | solution.py:387
  77.8 0.7 broadcast_in_dim.7
  78.6 25.3 %all_to_all.10 = f32[32,24,128]{2,1,0:T(8,128)S(1)} all-to-all(f32[32,24,128]{2,1,0:T(8,128)S(1)} %broadcast_in_dim.7), channel_id=1, replica_groups=mesh['x'=4,'z'=8,'y'=8,'c'=2] {'x','y'}, dimensions={0} | all-to-all | bytes 786432 | tf_op jit(solution)/shard_map/all_to_all | solution.py:472
  104.0 22.2 %all_to_all.11.gram_ref = f32[16,24,128]{2,1,0:T(8,128)} all-to-all(f32[16,24,128]{2,1,0:T(8,128)S(1)} %broadcast_in_dim.8), channel_id=1, replica_groups=mesh['x'=4,'z'=8,'y'=8,'c'=2] {'z','c'}, dimensions={0} | all-to-all | bytes 393216 | tf_op jit(solution)/shard_map/all_to_all | solution.py:472
  126.2 8.9 %finish.1 = (f32[32,3456]{1,0:T(8,128)}, f32[32,3456]{1,0:T(8,128)}, f32[32,3456]{1,0:T(8,128)}) custom-call(f32[16,24,128]{2,1,0:T(8,128)} %all_to_all.11.gram_ref, f32[32,3456]{1,0:T(8,128)} %get-tuple-element.26.right_ref, f32[32,3456]{1,0:T(8,128)} %get-tuple-element.28.image_ref), custom_call_target="tpu_custom_call" | custom-call | tf_op jit(solution)/shard_map/finish/pallas_call | solution.py:454
  (16 shorter events, 0.1 us)
Async XLA Ops:
  18.4 16.8 %collective-permute-start.1 = (f32[32,768]{1,0:T(8,128)S(1)}, f32[32,768]{1,0:T(8,128)S(1)}, u32[]{:S(2)}, u32[]{:S(2)}) collective-permute-start(f32[32,768]{1,0:T(8,128)S(1)} %get-tuple-element.31), channel_id=1, source_target_pairs={{0,1},{1,2},{2,3},{3,4},{4,5},{5,6},{6,7},{7,8},{8,9},{9,10},{10,1... | collective-permute-start | bytes 294920 | tf_op jit(solution)/shard_map/ppermute | solution.py:466
  23.0 12.2 %collective-permute-start = (f32[32,768]{1,0:T(8,128)S(1)}, f32[32,768]{1,0:T(8,128)S(1)}, u32[]{:S(2)}, u32[]{:S(2)}) collective-permute-start(f32[32,768]{1,0:T(8,128)S(1)} %get-tuple-element.32), channel_id=1, source_target_pairs={{1,0},{2,1},{3,2},{4,3},{5,4},{6,5},{7,6},{8,7},{9,8},{10,9},{11,1... | collective-permute-start | bytes 294920 | tf_op jit(solution)/shard_map/ppermute | solution.py:466
  35.2 0.6 copy-start
  35.9 0.6 copy-start.4
  40.0 11.0 %collective-permute-start.2 = (f32[32,768]{1,0:T(8,128)}, f32[32,768]{1,0:T(8,128)S(1)}, u32[]{:S(2)}, u32[]{:S(2)}) collective-permute-start(f32[32,768]{1,0:T(8,128)} %get-tuple-element.21), channel_id=1, source_target_pairs={{0,1},{1,2},{2,3},{3,4},{4,5},{5,6},{6,7},{7,8},{8,9},{9,10},{10,1... | collective-permute-start | bytes 294920 | tf_op jit(solution)/shard_map/ppermute | solution.py:466
  41.9 9.1 %collective-permute-start.3 = (f32[32,768]{1,0:T(8,128)}, f32[32,768]{1,0:T(8,128)S(1)}, u32[]{:S(2)}, u32[]{:S(2)}) collective-permute-start(f32[32,768]{1,0:T(8,128)} %get-tuple-element.22), channel_id=1, source_target_pairs={{1,0},{2,1},{3,2},{4,3},{5,4},{6,5},{7,6},{8,7},{9,8},{10,9},{11,1... | collective-permute-start | bytes 294920 | tf_op jit(solution)/shard_map/ppermute | solution.py:466
  50.9 0.6 copy-start.1
  51.0 0.7 copy-start.3
  61.7 11.8 %collective-permute-start.5 = (f32[32,768]{1,0:T(8,128)S(1)}, f32[32,768]{1,0:T(8,128)S(1)}, u32[]{:S(2)}, u32[]{:S(2)}) collective-permute-start(f32[32,768]{1,0:T(8,128)S(1)} %get-tuple-element.29), channel_id=1, source_target_pairs={{0,1},{1,2},{2,3},{3,4},{4,5},{5,6},{6,7},{7,8},{8,9},{9,10},{10,1... | collective-permute-start | bytes 294920 | tf_op jit(solution)/shard_map/ppermute | solution.py:466
  64.8 8.7 %collective-permute-start.4 = (f32[32,768]{1,0:T(8,128)S(1)}, f32[32,768]{1,0:T(8,128)S(1)}, u32[]{:S(2)}, u32[]{:S(2)}) collective-permute-start(f32[32,768]{1,0:T(8,128)S(1)} %get-tuple-element.30), channel_id=1, source_target_pairs={{1,0},{2,1},{3,2},{4,3},{5,4},{6,5},{7,6},{8,7},{9,8},{10,9},{11,1... | collective-permute-start | bytes 294920 | tf_op jit(solution)/shard_map/ppermute | solution.py:466
  73.5 0.6 copy-start.2
  73.5 0.7 copy-start.5

commit v2 on v1

--- a/solution.py
+++ b/solution.py
@@ -45,12 +45,16 @@
     return np.concatenate([high, low], axis=1)
 
 
-def params(**extra):
-    return pltpu.CompilerParams(vmem_limit_bytes=56 * 2**20, **extra)
+def params(mebibytes=24):
+    return pltpu.CompilerParams(vmem_limit_bytes=mebibytes * 2**20)
 
 
 def vmem(count):
     return [pl.BlockSpec(memory_space=pltpu.VMEM)] * count
+
+
+def hbm(count):
+    return [pl.BlockSpec(memory_space=pltpu.MemorySpace.HBM)] * count
 
 
 def shape(dims, kind=F32):
@@ -117,22 +121,61 @@
 
 CHUNK = 2048
 TILES = CHUNK // 128
-UNROLL = 32
-
-
-def rhs_kernel(tgt_ref, src_ref, conn_ref, pb_ref, sv_ref, ids_ref, parts_ref, halo_ref, blocks, source, total, wide, acc):
+UNROLL = 128
+
+
+def rhs_kernel(
+    tgt_hbm,
+    src_hbm,
+    conn_hbm,
+    pb_hbm,
+    sv_hbm,
+    ids_hbm,
+    parts_hbm,
+    low_ref,
+    high_ref,
+    tgt_ref,
+    src_ref,
+    conn_ref,
+    pb_ref,
+    sv_ref,
+    ids_ref,
+    parts_ref,
+    blocks,
+    source,
+    total,
+    wide,
+    acc,
+    sems,
+):
     zero = jnp.zeros((), F32)
     zero16 = jnp.zeros((), BF)
+    small = [
+        pltpu.make_async_copy(a, b, sems.at[i])
+        for i, (a, b) in enumerate(((sv_hbm, sv_ref), (conn_hbm, conn_ref), (tgt_hbm, tgt_ref), (src_hbm, src_ref)))
+    ]
+    large = [
+        pltpu.make_async_copy(pb_hbm.at[pl.ds(64 * i, 64), :], pb_ref.at[pl.ds(64 * i, 64), :], sems.at[4 + i]) for i in range(4)
+    ]
+    for copy in small + large:
+        copy.start()
+    total[...] = jnp.zeros_like(total)
+    small[0].wait()
     for g in range(16):
         stack = jnp.concatenate([sv_ref[:, (4 * g + k) * 128 : (4 * g + k + 1) * 128] for k in range(4)], axis=0)
         source[g * 128 : (g + 1) * 128, :] = stack.astype(F32).T.astype(BF)
-    @pl.loop(0, 16)
-    def _(g):
-        for c in range(32):
-            rows = pb_ref[aligned(g * 16, 16), c * 128 : (c + 1) * 128].astype(F32)
-            blocks[pl.ds(g * 512 + c, 16, stride=32), :] = rows
-
-    conn = conn_ref[...]
+    for copy in small[1:]:
+        copy.wait()
+    for i in range(4):
+        large[i].wait()
+
+        @pl.loop(4 * i, 4 * i + 4)
+        def _(g):
+            for c in range(32):
+                rows = pb_ref[aligned(g * 16, 16), c * 128 : (c + 1) * 128].astype(F32)
+                blocks[pl.ds(g * 528 + c, 16, stride=33), :] = rows
+
+    conn = conn_ref[...].astype(F32).T.astype(jnp.int32)
     row = lax.broadcasted_iota(jnp.int32, (64, 64), 0)
     col = lax.broadcasted_iota(jnp.int32, (64, 64), 1)
     swap = jnp.where(row == 2 * (col & 31) + lax.shift_right_logical(col, 5), 1.0, 0.0).astype(BF)
@@ -145,7 +188,6 @@
     lane64 = lax.broadcasted_iota(jnp.int32, (64, 128), 1)
     ids_ref[...] = jnp.where(lane64 < 64, wide[pl.ds(0, 64, stride=2), :], wide[pl.ds(1, 64, stride=2), :])
 
-    total[...] = jnp.zeros_like(total)
     low32 = lax.broadcasted_iota(jnp.int32, (32, 128), 1) < 64
     group = lax.shift_right_logical(lane64, 5).astype(I16)
 
@@ -158,7 +200,7 @@
             k = lax.shift_right_logical(s, 1) & 3
             start = lax.shift_right_logical(s, 3) * 128 + (s & 1) * 64
             value = jnp.where(group == k.astype(I16), source[aligned(start, 64), :], zero16)
-            block = blocks[aligned(p * 32, 32), :]
+            block = blocks[pl.ds(p * 33,32), :]
             rows = jnp.concatenate([jnp.where(low32, block, zero), jnp.where(low32, zero, block)], axis=0).astype(BF)
             total[aligned(e * 64, 64), :] += jnp.dot(
                 rows, jnp.concatenate([value, value], axis=0), preferred_element_type=F32
@@ -171,7 +213,7 @@
     def join(a, b, mask, by):
         return jnp.where(mask, b, a) + pltpu.roll(jnp.where(mask, a, b), by, 1)
 
-    @pl.loop(0, 16, unroll=4)
+    @pl.loop(0, 16, unroll=True)
     def _(g):
         e = [total[aligned(g * 512 + j * 128, 128), :] for j in range(4)]
         both = join(join(e[0], e[1], odd, 32), join(e[2], e[3], odd, 32), up, 64).T
@@ -179,36 +221,57 @@
             high, low = split2(both[j * TR : (j + 1) * TR])
             parts_ref[:, aligned(g * 512 + j * 128, 128)] = jnp.concatenate([high, low], axis=0)
 
-    scatter_halo(ids_ref, parts_ref, halo_ref, acc)
-
-
-def scatter_halo(ids_ref, parts_ref, halo_ref, acc):
+    results = [
+        pltpu.make_async_copy(a, b, sems.at[8 + i]) for i, (a, b) in enumerate(((ids_ref, ids_hbm), (parts_ref, parts_hbm)))
+    ]
+    for copy in results:
+        copy.start()
+    scatter_halo(ids_ref, parts_ref, acc)
+    halves(acc, low_ref, high_ref)
+    for copy in results:
+        copy.wait()
+
+
+def scatter_halo(ids_ref, parts_ref, acc):
     acc[...] = jnp.zeros_like(acc)
 
-    @pl.loop(0, SLOTS // CHUNK)
+    @pl.loop(0, SLOTS // CHUNK, unroll=True)
     def _(k):
         add_scatter(
             acc, parts_ref[:, aligned(k * CHUNK, CHUNK)], ids_ref[aligned(k * TILES, TILES), :], TILES, OWN_BLOCKS, HALO_BLOCKS
         )
 
-    for b in range(HALO_BLOCKS):
-        halo_ref[:, b * L : (b + 1) * L] = fold(acc, b)
+
+def halves(acc, low_ref, high_ref):
+    first, middle, last = (fold(acc, b) for b in range(HALO_BLOCKS))
+    low_ref[:, :L] = first
+    low_ref[:, L:] = middle[:, : F - L]
+    high_ref[:, : F - L] = middle[:, F - L :]
+    high_ref[:, F - L :] = last
 
 
 def right_side_halo(tgt, src, conn, pair_blocks, source_values):
     return pl.pallas_call(
         rhs_kernel,
-        out_shape=(shape((64, 128), jnp.int32), shape((2 * TR, SLOTS), BF), shape((TR, 2 * F))),
-        in_specs=[pl.BlockSpec(memory_space=pltpu.SMEM)] * 2 + vmem(3),
-        out_specs=tuple(vmem(3)),
+        out_shape=(shape((64, 128), jnp.int32), shape((2 * TR, SLOTS), BF), shape((TR, F)), shape((TR, F))),
+        in_specs=hbm(5),
+        out_specs=tuple(hbm(2) + vmem(2)),
         scratch_shapes=[
-            pltpu.VMEM((8192, 128), F32),
+            pltpu.SMEM((256,), jnp.int32),
+            pltpu.SMEM((256,), jnp.int32),
+            pltpu.VMEM((64, 128), jnp.int32),
+            pltpu.VMEM((256, 4096), BF),
+            pltpu.VMEM((TR, SLOTS), BF),
+            pltpu.VMEM((64, 128), jnp.int32),
+            pltpu.VMEM((2 * TR, SLOTS), BF),
+            pltpu.VMEM((8448, 128), F32),
             pltpu.VMEM((2048, 128), BF),
             pltpu.VMEM((8192, 128), F32),
             pltpu.VMEM((128, 128), jnp.int32),
             pltpu.VMEM((HALO_BLOCKS * 2 * TR, L), F32),
+            pltpu.SemaphoreType.DMA((10,)),
         ],
-        compiler_params=params(),
+        compiler_params=params(54),
         name="rhs",
     )(tgt, src, conn, pair_blocks, source_values)
 
@@ -216,7 +279,7 @@
 def own_kernel(ids_ref, parts_ref, out_ref, acc):
     acc[...] = jnp.zeros_like(acc)
 
-    @pl.loop(0, SLOTS // CHUNK)
+    @pl.loop(0, SLOTS // CHUNK, unroll=True)
     def _(k):
         add_scatter(acc, parts_ref[:, aligned(k * CHUNK, CHUNK)], ids_ref[aligned(k * TILES, TILES), :], TILES, 0, OWN_BLOCKS)
 
@@ -285,7 +348,7 @@
     lane64 = lax.broadcasted_iota(jnp.int32, (64, 128), 1)
     scale_ref[...] = jnp.where(lane64 < 64, wide[pl.ds(0, 64, stride=2), :], wide[pl.ds(1, 64, stride=2), :])
 
-    @pl.loop(0, SLOTS // CHUNK)
+    @pl.loop(0, SLOTS // CHUNK, unroll=True)
     def _(k):
         hot, blocks = tiles_of(ids_ref[aligned(k * TILES, TILES), :], TILES)
         rows = jnp.dot(table_ref[...], jnp.concatenate([hot, hot], axis=0), preferred_element_type=F32)
@@ -306,14 +369,14 @@
     )(ids, table, jac)
 
 
-def mass_kernel(ids_ref, start_ref, below_ref, above_ref, scale_ref, mass_ref, parts_ref, halo_ref, table, acc):
+def mass_kernel(ids_ref, start_ref, below_ref, above_ref, scale_ref, mass_ref, parts_ref, low_ref, high_ref, table, acc):
     both = jnp.concatenate([below_ref[...], above_ref[...]], axis=1)
     for b in range(HALO_BLOCKS):
         high, low = split2(both[:, b * L : (b + 1) * L])
         table[b * TR : (b + 1) * TR, :] = jnp.concatenate([high, low], axis=1)
     acc[...] = jnp.zeros_like(acc)
 
-    @pl.loop(0, SLOTS // CHUNK)
+    @pl.loop(0, SLOTS // CHUNK, unroll=True)
     def _(k):
         hot, blocks = tiles_of(ids_ref[aligned(k * TILES, TILES), :], TILES)
         rows = jnp.dot(table[...], jnp.concatenate([hot, hot], axis=0), preferred_element_type=F32)
@@ -339,16 +402,15 @@
             masked(parts, blocks, OWN_BLOCKS, HALO_BLOCKS), hot, NT, preferred_element_type=F32
         )
 
-    for b in range(HALO_BLOCKS):
-        halo_ref[:, b * L : (b + 1) * L] = fold(acc, b)
+    halves(acc, low_ref, high_ref)
 
 
 def mass_halo(ids, start, below, above, scale, mass):
     return pl.pallas_call(
         mass_kernel,
-        out_shape=(shape((2 * TR, SLOTS), BF), shape((TR, 2 * F))),
+        out_shape=(shape((2 * TR, SLOTS), BF), shape((TR, F)), shape((TR, F))),
         in_specs=vmem(6),
-        out_specs=tuple(vmem(2)),
+        out_specs=tuple(vmem(3)),
         scratch_shapes=[
             pltpu.VMEM((HALO_BLOCKS * TR, 2 * L), BF),
             pltpu.VMEM((HALO_BLOCKS * 2 * TR, L), F32),
@@ -356,6 +418,10 @@
         compiler_params=params(),
         name="mass",
     )(ids, start, below, above, scale, mass)
+
+
+def places():
+    return tuple(lax.broadcasted_iota(jnp.int32, (TR, TR), i) for i in range(2))
 
 
 def lay_flat(square):
@@ -379,14 +445,19 @@
     full = full[:, :64] + full[:, 64:]
     cross = full[:TR, TR:]
     cross = 0.5 * (cross + full[TR:, :TR])
-    for i, g in enumerate((full[:TR, :TR], cross, full[TR:, TR:])):
-        gram_ref[8 * i : 8 * i + 8, :] = lay_flat(g)
+    rhs, images = full[:TR, :TR], full[TR:, TR:]
+    row, col = places()
+    diagonal = jnp.sum(jnp.where(row == col, images, 0.0), axis=0, keepdims=True)
+    first = jnp.where(row >= col, rhs, images)
+    second = jnp.where(row == 0, diagonal, images[:1, :1])
+    gram_ref[0:8, :] = lay_flat(first)
+    gram_ref[8:16, :] = lay_flat(jnp.where(row >= col, cross, second))
 
 
 def grams(own, above, below, highs, lows, right):
     return pl.pallas_call(
         gram_kernel,
-        out_shape=(shape((TR, NODE_DEV)), shape((24, 128))),
+        out_shape=(shape((TR, NODE_DEV)), shape((16, 128))),
         in_specs=vmem(6),
         out_specs=tuple(vmem(2)),
         scratch_shapes=[pltpu.VMEM((OWN_BLOCKS * 2 * TR, L), F32)],
@@ -399,37 +470,71 @@
     return lax.dot_general(a, b, dims, precision=lax.Precision.HIGHEST, preferred_element_type=F32)
 
 
+def eliminate(work, above):
+    groups = TR // 8
+    row = lax.broadcasted_iota(jnp.int32, (8, 128), 0)
+    work = [work[8 * g : 8 * g + 8] for g in range(groups)]
+    scale = [jnp.zeros((8, 128), F32)] * groups
+    for panel in range(groups):
+        columns = {
+            k: [jnp.broadcast_to(work[g][:, k : k + 1], (8, 128)) for g in range(groups)]
+            for k in range(8 * panel, 8 * panel + 8)
+        }
+        for k in range(8 * panel, 8 * panel + 8):
+            g0, r = divmod(k, 8)
+            column = columns[k]
+            pivot = column[g0][r : r + 1]
+            inverse = 1.0 / pivot
+            if not above:
+                scale[g0] = jnp.where(row == r, jnp.broadcast_to(pivot, (8, 128)), scale[g0])
+
+            def update(target):
+                line = jnp.broadcast_to(target[g0][r : r + 1] * inverse, (8, 128))
+                out = []
+                for g in range(groups):
+                    if g < g0 and not above:
+                        out.append(target[g])
+                    elif g == g0:
+                        less = target[g] - column[g] * line
+                        if above:
+                            out.append(jnp.where(row == r, line, less))
+                        else:
+                            out.append(jnp.where(row > r, less, target[g]))
+                    else:
+                        out.append(target[g] - column[g] * line)
+                return out
+
+            work = update(work)
+            for j in range(k + 1, 8 * panel + 8):
+                columns[j] = update(columns[j])
+    if not above:
+        work = [w * lax.rsqrt(s) for w, s in zip(work, scale)]
+    return jnp.concatenate(work, axis=0)
+
+
 def final_kernel(gram_ref, right_ref, image_ref, sol_ref, res_ref, new_ref):
     total = gram_ref[0]
     for i in range(1, gram_ref.shape[0]):
         total = total + gram_ref[i]
-    rhs, cross, images = (lay_square(total[8 * i : 8 * i + 8]) for i in range(3))
-    row = lax.broadcasted_iota(jnp.int32, (TR, 64), 0)
-    col = lax.broadcasted_iota(jnp.int32, (TR, 64), 1)
-    cross = 0.5 * (cross + cross.T)
-
-    work = jnp.concatenate([cross, rhs], axis=1)
-    for k in range(TR):
-        line = work[k : k + 1] * (1.0 / work[k : k + 1, k : k + 1])
-        column = jnp.where(row[:, :1] == k, 0.0, work[:, k : k + 1])
-        work = jnp.where(row == k, line, work) - column * line
-    weights_t = work[:, TR:]
+    first = lay_square(total[:8])
+    second = lay_square(total[8:])
+    first_t = first.T
+    second_t = second.T
+    row, col = places()
+    rhs = jnp.where(row >= col, first, first_t)
+    cross = jnp.where(row >= col, second, second_t)
+    diagonal = jnp.where(col == 0, second[1:2, 2:3], second[:1, :])
+    images = jnp.where(row < col, first, jnp.where(row == col, diagonal, first_t))
+    zero = jnp.zeros((TR, TR), F32)
+    eye = jnp.where(row == col, 1.0, 0.0)
+
+    weights_t = eliminate(jnp.concatenate([cross, rhs, zero, zero], axis=1), True)[:, TR : 2 * TR]
     weights = weights_t.T
-    half = hdot(weights, cross)
-    gram = rhs - half - half.T + hdot(hdot(weights, images), weights_t)
-    gram = 0.5 * (gram + gram.T)
-
-    work = jnp.concatenate([gram, jnp.where(row[:, :TR] == col[:, :TR], 1.0, 0.0)], axis=1)
-    for k in range(TR):
-        line = work[k : k + 1] * lax.rsqrt(work[k : k + 1, k : k + 1])
-        column = work[:, k : k + 1] * lax.rsqrt(work[k : k + 1, k : k + 1])
-        column = jnp.where(row[:, :1] > k, column, 0.0)
-        work = jnp.where(row == k, line, work) - column * line
-    inverse = work[:, TR:]
-
-    mixed = hdot(inverse, weights)
-    zero = jnp.zeros((TR, TR), F32)
-    eye = jnp.where(row[:, :TR] == col[:, :TR], 1.0, 0.0)
+    both = hdot(weights, jnp.concatenate([cross, images], axis=1))
+    gram = rhs - 2.0 * both[:, :TR] + hdot(both[:, TR:], weights_t)
+    work = eliminate(jnp.concatenate([gram, eye, weights, zero], axis=1), False)
+    inverse = work[:, TR : 2 * TR]
+    mixed = work[:, 2 * TR : 3 * TR]
     coeffs = jnp.concatenate(
         [
             jnp.concatenate([weights, zero], axis=1),
@@ -439,12 +544,16 @@
         axis=0,
     )
     high, low = split2(coeffs)
-    lhs = jnp.concatenate([high, high, low], axis=1)
     right = right_ref[...]
     rh, rl = split2(right)
     ih, il = split2(image_ref[...])
-    stack = jnp.concatenate([rh, ih, rl, il, rh, ih], axis=0)
-    out = jnp.dot(lhs, stack, preferred_element_type=F32)
+    highs = jnp.concatenate([rh, ih], axis=0)
+    lows = jnp.concatenate([rl, il], axis=0)
+    out = (
+        jnp.dot(high, highs, preferred_element_type=F32)
+        + jnp.dot(high, lows, preferred_element_type=F32)
+        + jnp.dot(low, highs, preferred_element_type=F32)
+    )
     sol_ref[...] = out[:TR]
     res_ref[...] = right + out[TR : 2 * TR]
     new_ref[...] = out[2 * TR :]
@@ -476,17 +585,17 @@
     lows = send_down
     highs = send_up
     mass = jnp.asarray(mass_tiles())
-    ids, parts, halo = right_side_halo(pair_target, pair_source, connectivity, pair_blocks, source_values)
-    above = shifted(halo[:, :F], -1)
-    below = shifted(halo[:, F:], 1)
+    ids, parts, low, high = right_side_halo(pair_target, pair_source, connectivity.T, pair_blocks, source_values)
+    above = shifted(low, -1)
+    below = shifted(high, 1)
     own = scatter_own(ids, parts)
     right, up, down, table = settle_right(own, above, below, highs, lows)
     below = shifted(up, 1)
     above = shifted(down, -1)
     start, scale = gather_own(ids, table, jacobian[None, :])
-    parts, halo = mass_halo(ids, start, below, above, scale, mass)
-    above = shifted(halo[:, :F], -1)
-    below = shifted(halo[:, F:], 1)
+    parts, low, high = mass_halo(ids, start, below, above, scale, mass)
+    above = shifted(low, -1)
+    below = shifted(high, 1)
     own = scatter_own(ids, parts)
     image, gram = grams(own, above, below, highs, lows, right)
     gram = exchanged(gram, ("x", "y")).sum(0)

time: 136 us -> 108 us (0.79)
  Pallas kernels: 60.6 us -> 36.6 us
  local copies, waits for them, and re-layouts: 6.73 us -> 2.03 us
    pallas_call x1, Pallas kernels: 15.3 us -> 9.69 us  [right_side_halo(): pl.pallas_call(rhs_kernel, out_shape=(shape((64, 128), jnp.int32), shape(...]
    pallas_call x2, Pallas kernels: 13.5 us -> 8.48 us  [scatter_own(): pl.pallas_call(own_kernel, out_shape=shape((TR, OWN_BLOCKS * L)), in_spec...]
    pallas_call x1, Pallas kernels: 8.9 us -> 4.02 us  [finish(): pl.pallas_call(final_kernel, out_shape=(shape((TR, NODE_DEV)),) * 3, in_s...]
    pallas_call x1, Pallas kernels: 6.63 us -> 3.98 us  [gather_own(): pl.pallas_call(gather_kernel, out_shape=(shape((TR, SLOTS)), shape((64, 1...]
    pallas_call x1, Pallas kernels: 9.08 us -> 6.8 us  [mass_halo(): pl.pallas_call(mass_kernel, out_shape=(shape((2 * TR, SLOTS), BF), shape(...]
    unnamed x13 -> x12, local copies, waits for them, and re-layouts: 4.08 us -> 2 us
    slice x2 -> x0, local copies, waits for them, and re-layouts: 1.91 us -> none  [per_device(): below = shifted(halo[:, F:], 1)]
    pallas_call x1, Pallas kernels: 3.7 us -> 1.9 us  [grams(): pl.pallas_call(gram_kernel, out_shape=(shape((TR, NODE_DEV)), shape((16,...]
  transfers between devices with their start and end apart: 6 -> 6, of which waited for: 0 -> 0; matrix products, arithmetic and copies ran while one was open for 0% -> 0% of each run, Pallas kernels for 15% -> 12%
where the time goes in v2:
time: 108 us; the launch traced here: 107 us
  blocking collectives  46.8 us (43%)
  Pallas kernels  36.6 us (34%)
  starting transfers between devices  20.8 us (19%)
  local copies, waits for them, and re-layouts  2.03 us (2%)
    all_to_all x2, blocking collectives, exchanged(): return lax.all_to_all(copies, axes, 0, 0)  46.8 us
    ppermute x6, starting transfers between devices, shifted(): return lax.ppermute(value, AXES, pairs)  20.8 us
    pallas_call x1, Pallas kernels, right_side_halo(): pl.pallas_call(rhs_kernel, out_shape=(shape((64, 128), jnp.int32), shape(...  9.69 us
    pallas_call x2, Pallas kernels, scatter_own(): pl.pallas_call(own_kernel, out_shape=shape((TR, OWN_BLOCKS * L)), in_spec...  8.48 us
    pallas_call x1, Pallas kernels, mass_halo(): pl.pallas_call(mass_kernel, out_shape=(shape((2 * TR, SLOTS), BF), shape(...  6.8 us
    pallas_call x1, Pallas kernels, finish(): pl.pallas_call(final_kernel, out_shape=(shape((TR, NODE_DEV)),) * 3, in_s...  4.02 us
    pallas_call x1, Pallas kernels, gather_own(): pl.pallas_call(gather_kernel, out_shape=(shape((TR, SLOTS)), shape((64, 1...  3.98 us
  transfers between devices with their start and end apart: 6, of which 0 were waited for; matrix products, arithmetic and copies ran while one was open for 0% of the time, Pallas kernels for 12%

profile of v2, /device:TPU:1, one launch (start us, length us, event | category | flops | bytes accessed | tf_op | source)
XLA Modules:
  0.0 107.1 jit_solution(4580545728142355538)
XLA Ops:
  0.6 9.7 %rhs.1 = (s32[64,128]{1,0:T(8,128)}, bf16[64,8192]{1,0:T(8,128)(2,1)}, f32[32,768]{1,0:T(8,128)}, f32[32,768]{1,0:T(8,128)}) custom-call(s32[256]{0:T(256)} %tgt_hbm.1, s32[256]{0:T(256)} %src_hbm.1, s32[64,128]{1,0:T(8,128)} %bitcast.3, bf16[256,4096]{1,0:T(8,128)(2,1)} %pb_hbm.1, bf16[32,8192]{1,0:T(8,128)(2,1)} %sv_hbm.1), custom_call_target="tpu_custom_call" | custom-call | tf_op jit(solution)/shard_map/rhs/pallas_call | solution.py:254
  10.3 8.8 %collective-permute-start = (f32[32,768]{1,0:T(8,128)}, f32[32,768]{1,0:T(8,128)S(1)}, u32[]{:S(2)}, u32[]{:S(2)}) collective-permute-start(f32[32,768]{1,0:T(8,128)} %get-tuple-element.20), channel_id=1, source_target_pairs={{1,0},{2,1},{3,2},{4,3},{5,4},{6,5},{7,6},{8,7},{9,8},{10,9},{11,1... | collective-permute-start | bytes 294920 | tf_op jit(solution)/shard_map/ppermute | solution.py:575
  19.1 1.9 %collective-permute-start.1 = (f32[32,768]{1,0:T(8,128)}, f32[32,768]{1,0:T(8,128)S(1)}, u32[]{:S(2)}, u32[]{:S(2)}) collective-permute-start(f32[32,768]{1,0:T(8,128)} %get-tuple-element.21), channel_id=1, source_target_pairs={{0,1},{1,2},{2,3},{3,4},{4,5},{5,6},{6,7},{7,8},{8,9},{9,10},{10,1... | collective-permute-start | bytes 294920 | tf_op jit(solution)/shard_map/ppermute | solution.py:575
  21.0 0.0 copy-start.1
  21.1 0.7 copy-done.1
  21.8 1.2 %copy-done.4 = bf16[64,8192]{1,0:T(8,128)(2,1)S(1)} copy-done((bf16[64,8192]{1,0:T(8,128)(2,1)S(1)}, bf16[64,8192]{1,0:T(8,128)(2,1)}, u32[]{:S(2)}) %copy-start.4) | copy-done | bytes 1048600
  23.0 4.2 %own.2.own_ref = f32[32,3584]{1,0:T(8,128)S(1)} custom-call(s32[64,128]{1,0:T(8,128)S(1)} %copy-done.1, bf16[64,8192]{1,0:T(8,128)(2,1)S(1)} %copy-done.4), custom_call_target="tpu_custom_call" | custom-call | flops 3758096384 | bytes 2097152 | tf_op jit(solution)/shard_map/own/pallas_call | solution.py:291
  27.3 0.0 collective-permute-done.1.below_ref
  27.3 1.7 %settle.1 = (f32[32,3456]{1,0:T(8,128)S(1)}, f32[32,768]{1,0:T(8,128)S(1)}, f32[32,768]{1,0:T(8,128)S(1)}, bf16[224,1024]{1,0:T(8,128)(2,1)S(1)}) custom-call(f32[32,3584]{1,0:T(8,128)S(1)} %own.2.own_ref, f32[32,768]{1,0:T(8,128)S(1)} %collective-permute-done.above_ref, f32[32,768]{1,0:T(8,128)S(1)} %collective-permute-done.1.below_ref, ...), custom_call_target="tpu_custom_call" | custom-call | tf_op jit(solution)/shard_map/settle/pallas_call | solution.py:330
  29.1 1.9 %collective-permute-start.2 = (f32[32,768]{1,0:T(8,128)S(1)}, f32[32,768]{1,0:T(8,128)S(1)}, u32[]{:S(2)}, u32[]{:S(2)}) collective-permute-start(f32[32,768]{1,0:T(8,128)S(1)} %get-tuple-element.24), channel_id=1, source_target_pairs={{0,1},{1,2},{2,3},{3,4},{4,5},{5,6},{6,7},{7,8},{8,9},{9,10},{10,1... | collective-permute-start | bytes 294920 | tf_op jit(solution)/shard_map/ppermute | solution.py:575
  31.0 2.6 %collective-permute-start.3 = (f32[32,768]{1,0:T(8,128)S(1)}, f32[32,768]{1,0:T(8,128)S(1)}, u32[]{:S(2)}, u32[]{:S(2)}) collective-permute-start(f32[32,768]{1,0:T(8,128)S(1)} %get-tuple-element.25), channel_id=1, source_target_pairs={{1,0},{2,1},{3,2},{4,3},{5,4},{6,5},{7,6},{8,7},{9,8},{10,9},{11,1... | collective-permute-start | bytes 294920 | tf_op jit(solution)/shard_map/ppermute | solution.py:575
  33.6 0.0 copy-start
  33.6 4.0 %gather.1 = (f32[32,8192]{1,0:T(8,128)S(1)}, f32[64,128]{1,0:T(8,128)S(1)}) custom-call(s32[64,128]{1,0:T(8,128)S(1)} %copy-done.1, bf16[224,1024]{1,0:T(8,128)(2,1)S(1)} %get-tuple-element.22.table_ref, f32[1,128]{1,0:T(1,128)S(1)} %bitcast.2), custom_call_target="tpu_custom_call" | custom-call | flops 3758096384 | bytes 2097152 | tf_op jit(solution)/shard_map/gather/pallas_call | solution.py:360
  37.6 0.0 collective-permute-done.2.below_ref
  37.6 0.0 collective-permute-done.3.above_ref
  37.6 6.8 %mass.1 = (bf16[64,8192]{1,0:T(8,128)(2,1)S(1)}, f32[32,768]{1,0:T(8,128)S(1)}, f32[32,768]{1,0:T(8,128)S(1)}) custom-call(s32[64,128]{1,0:T(8,128)S(1)} %copy-done.1, f32[32,8192]{1,0:T(8,128)S(1)} %get-tuple-element.23.start_ref, f32[32,768]{1,0:T(8,128)S(1)} %collective-permute-done.2.below_ref, f32[32,768]{1,0:T(8,128)S(1)} %collective-permute-done.3.above_ref, ...), custom_call_target="tpu_custom_call" | custom-call | tf_op jit(solution)/shard_map/mass/pallas_call | solution.py:409
  44.4 1.9 %collective-permute-start.4 = (f32[32,768]{1,0:T(8,128)S(1)}, f32[32,768]{1,0:T(8,128)S(1)}, u32[]{:S(2)}, u32[]{:S(2)}) collective-permute-start(f32[32,768]{1,0:T(8,128)S(1)} %get-tuple-element.28), channel_id=1, source_target_pairs={{1,0},{2,1},{3,2},{4,3},{5,4},{6,5},{7,6},{8,7},{9,8},{10,9},{11,1... | collective-permute-start | bytes 294920 | tf_op jit(solution)/shard_map/ppermute | solution.py:575
  46.4 3.6 %collective-permute-start.5 = (f32[32,768]{1,0:T(8,128)S(1)}, f32[32,768]{1,0:T(8,128)S(1)}, u32[]{:S(2)}, u32[]{:S(2)}) collective-permute-start(f32[32,768]{1,0:T(8,128)S(1)} %get-tuple-element.29), channel_id=1, source_target_pairs={{0,1},{1,2},{2,3},{3,4},{4,5},{5,6},{6,7},{7,8},{8,9},{9,10},{10,1... | collective-permute-start | bytes 294920 | tf_op jit(solution)/shard_map/ppermute | solution.py:575
  50.0 4.2 %own.3.own_ref = f32[32,3584]{1,0:T(8,128)S(1)} custom-call(s32[64,128]{1,0:T(8,128)S(1)} %copy-done.1, bf16[64,8192]{1,0:T(8,128)(2,1)S(1)} %get-tuple-element.27.parts_ref), custom_call_target="tpu_custom_call" | custom-call | flops 3758096384 | bytes 2097152 | tf_op jit(solution)/shard_map/own/pallas_call | solution.py:291
  54.2 0.0 collective-permute-done.4.above_ref
  54.3 1.9 %grams.1 = (f32[32,3456]{1,0:T(8,128)S(1)}, f32[16,128]{1,0:T(8,128)S(1)}) custom-call(f32[32,3584]{1,0:T(8,128)S(1)} %own.3.own_ref, f32[32,768]{1,0:T(8,128)S(1)} %collective-permute-done.4.above_ref, f32[32,768]{1,0:T(8,128)S(1)} %collective-permute-done.5.below_ref, s32[1,768]{1,0:T(1,128)S(1)} %copy-done.2, s32[1,768]{1,0:T(1,128)S(1)} %copy-done.3, ...), custom_call_target="tpu_custom_call" | custom-call | tf_op jit(solution)/shard_map/grams/pallas_call | solution.py:458
  56.2 26.3 %all_to_all.10 = f32[32,16,128]{2,1,0:T(8,128)S(1)} all-to-all(f32[32,16,128]{2,1,0:T(8,128)S(1)} %broadcast_in_dim.7), channel_id=1, replica_groups=mesh['x'=4,'z'=8,'y'=8,'c'=2] {'x','y'}, dimensions={0} | all-to-all | bytes 524288 | tf_op jit(solution)/shard_map/all_to_all | solution.py:581
  82.5 20.5 %all_to_all.11.gram_ref = f32[16,16,128]{2,1,0:T(8,128)S(1)} all-to-all(f32[16,16,128]{2,1,0:T(8,128)S(1)} %broadcast_in_dim.8), channel_id=1, replica_groups=mesh['x'=4,'z'=8,'y'=8,'c'=2] {'z','c'}, dimensions={0} | all-to-all | bytes 262144 | tf_op jit(solution)/shard_map/all_to_all | solution.py:581
  103.0 4.0 %finish.1 = (f32[32,3456]{1,0:T(8,128)}, f32[32,3456]{1,0:T(8,128)}, f32[32,3456]{1,0:T(8,128)}) custom-call(f32[16,16,128]{2,1,0:T(8,128)S(1)} %all_to_all.11.gram_ref, f32[32,3456]{1,0:T(8,128)S(1)} %get-tuple-element.30.right_ref, f32[32,3456]{1,0:T(8,128)S(1)} %get-tuple-element.32.image_ref), custom_call_target="tpu_custom_call" | custom-call | tf_op jit(solution)/shard_map/finish/pallas_call | solution.py:563
  (13 shorter events, 0.1 us)
Async XLA Ops:
  10.3 17.0 %collective-permute-start = (f32[32,768]{1,0:T(8,128)}, f32[32,768]{1,0:T(8,128)S(1)}, u32[]{:S(2)}, u32[]{:S(2)}) collective-permute-start(f32[32,768]{1,0:T(8,128)} %get-tuple-element.20), channel_id=1, source_target_pairs={{1,0},{2,1},{3,2},{4,3},{5,4},{6,5},{7,6},{8,7},{9,8},{10,9},{11,1... | collective-permute-start | bytes 294920 | tf_op jit(solution)/shard_map/ppermute | solution.py:575
  19.1 8.2 %collective-permute-start.1 = (f32[32,768]{1,0:T(8,128)}, f32[32,768]{1,0:T(8,128)S(1)}, u32[]{:S(2)}, u32[]{:S(2)}) collective-permute-start(f32[32,768]{1,0:T(8,128)} %get-tuple-element.21), channel_id=1, source_target_pairs={{0,1},{1,2},{2,3},{3,4},{4,5},{5,6},{6,7},{7,8},{8,9},{9,10},{10,1... | collective-permute-start | bytes 294920 | tf_op jit(solution)/shard_map/ppermute | solution.py:575
  21.0 0.8 copy-start.1
  21.8 1.2 %copy-start.4 = (bf16[64,8192]{1,0:T(8,128)(2,1)S(1)}, bf16[64,8192]{1,0:T(8,128)(2,1)}, u32[]{:S(2)}) copy-start(bf16[64,8192]{1,0:T(8,128)(2,1)} %get-tuple-element.19.parts_ref) | copy-start | bytes 3145732
  23.0 4.3 %copy-start.2 = (s32[1,768]{1,0:T(1,128)S(1)}, s32[1,768]{1,0:T(1,128)}, u32[]{:S(2)}) copy-start(s32[1,768]{1,0:T(1,128)} %highs_ref.3) | copy-start | bytes 9220
  23.0 4.3 %copy-start.3 = (s32[1,768]{1,0:T(1,128)S(1)}, s32[1,768]{1,0:T(1,128)}, u32[]{:S(2)}) copy-start(s32[1,768]{1,0:T(1,128)} %lows_ref.3) | copy-start | bytes 9220
  23.0 10.5 %copy-start.5 = (f32[128]{0:T(128)S(1)}, f32[128]{0:T(128)}, u32[]{:S(2)}) copy-start(f32[128]{0:T(128)} %param.12) | copy-start | bytes 1540
  29.1 8.5 %collective-permute-start.2 = (f32[32,768]{1,0:T(8,128)S(1)}, f32[32,768]{1,0:T(8,128)S(1)}, u32[]{:S(2)}, u32[]{:S(2)}) collective-permute-start(f32[32,768]{1,0:T(8,128)S(1)} %get-tuple-element.24), channel_id=1, source_target_pairs={{0,1},{1,2},{2,3},{3,4},{4,5},{5,6},{6,7},{7,8},{8,9},{9,10},{10,1... | collective-permute-start | bytes 294920 | tf_op jit(solution)/shard_map/ppermute | solution.py:575
  31.0 6.6 %collective-permute-start.3 = (f32[32,768]{1,0:T(8,128)S(1)}, f32[32,768]{1,0:T(8,128)S(1)}, u32[]{:S(2)}, u32[]{:S(2)}) collective-permute-start(f32[32,768]{1,0:T(8,128)S(1)} %get-tuple-element.25), channel_id=1, source_target_pairs={{1,0},{2,1},{3,2},{4,3},{5,4},{6,5},{7,6},{8,7},{9,8},{10,9},{11,1... | collective-permute-start | bytes 294920 | tf_op jit(solution)/shard_map/ppermute | solution.py:575
  33.6 4.0 %copy-start = (bf16[256,512]{1,0:T(8,128)(2,1)S(1)}, bf16[256,512]{1,0:T(8,128)(2,1)}, u32[]{:S(2)}) copy-start(bf16[256,512]{1,0:T(8,128)(2,1)} %constant.4.clone.mass_ref) | copy-start | bytes 786436
  44.4 9.8 %collective-permute-start.4 = (f32[32,768]{1,0:T(8,128)S(1)}, f32[32,768]{1,0:T(8,128)S(1)}, u32[]{:S(2)}, u32[]{:S(2)}) collective-permute-start(f32[32,768]{1,0:T(8,128)S(1)} %get-tuple-element.28), channel_id=1, source_target_pairs={{1,0},{2,1},{3,2},{4,3},{5,4},{6,5},{7,6},{8,7},{9,8},{10,9},{11,1... | collective-permute-start | bytes 294920 | tf_op jit(solution)/shard_map/ppermute | solution.py:575
  46.4 7.9 %collective-permute-start.5 = (f32[32,768]{1,0:T(8,128)S(1)}, f32[32,768]{1,0:T(8,128)S(1)}, u32[]{:S(2)}, u32[]{:S(2)}) collective-permute-start(f32[32,768]{1,0:T(8,128)S(1)} %get-tuple-element.29), channel_id=1, source_target_pairs={{0,1},{1,2},{2,3},{3,4},{4,5},{5,6},{6,7},{7,8},{8,9},{9,10},{10,1... | collective-permute-start | bytes 294920 | tf_op jit(solution)/shard_map/ppermute | solution.py:575

commit v3 on v2

--- a/solution.py
+++ b/solution.py
@@ -100,10 +100,11 @@
 def picked(rows, blocks, first, number, start):
     out = []
     for j, row in enumerate(blocks):
-        here = jnp.broadcast_to(row, (TR, 128))
         tile = start[j]
+        height = tile.shape[0]
+        here = jnp.broadcast_to(row, (height, 128))
         for b in range(number):
-            tile = jnp.where(here == first + b, rows[b * TR : (b + 1) * TR, j * 128 : (j + 1) * 128], tile)
+            tile = jnp.where(here == first + b, rows[b * height : (b + 1) * height, j * 128 : (j + 1) * 128], tile)
         out.append(tile)
     return out
 
@@ -132,8 +133,8 @@
     sv_hbm,
     ids_hbm,
     parts_hbm,
-    low_ref,
-    high_ref,
+    near_ref,
+    far_ref,
     tgt_ref,
     src_ref,
     conn_ref,
@@ -227,7 +228,7 @@
     for copy in results:
         copy.start()
     scatter_halo(ids_ref, parts_ref, acc)
-    halves(acc, low_ref, high_ref)
+    halves(acc, near_ref, far_ref)
     for copy in results:
         copy.wait()
 
@@ -242,12 +243,23 @@
         )
 
 
-def halves(acc, low_ref, high_ref):
+def upper_first():
+    return lax.axis_index("c") == 0
+
+
+def halves(acc, near_ref, far_ref):
     first, middle, last = (fold(acc, b) for b in range(HALO_BLOCKS))
-    low_ref[:, :L] = first
-    low_ref[:, L:] = middle[:, : F - L]
-    high_ref[:, : F - L] = middle[:, F - L :]
-    high_ref[:, F - L :] = last
+    low = jnp.concatenate([first, middle[:, : F - L]], axis=1)
+    high = jnp.concatenate([middle[:, F - L :], last], axis=1)
+    upward = upper_first()
+    near_ref[...] = jnp.where(upward, high, low)
+    far_ref[...] = jnp.where(upward, low, high)
+
+
+def arrived(near_ref, far_ref):
+    upward = upper_first()
+    near, far = near_ref[...], far_ref[...]
+    return jnp.where(upward, near, far), jnp.where(upward, far, near)
 
 
 def right_side_halo(tgt, src, conn, pair_blocks, source_values):
@@ -300,19 +312,19 @@
     )(ids, parts)
 
 
-def settle(own_ref, above_ref, below_ref, highs_ref, lows_ref, acc):
+def settle(own_ref, near_ref, far_ref, highs_ref, lows_ref, acc):
     rows = [highs_ref[:, j * 128 : (j + 1) * 128] for j in range(6)] + [lows_ref[:, j * 128 : (j + 1) * 128] for j in range(6)]
     hot = jnp.concatenate([one_hot(r & (L - 1)) for r in rows], axis=1)
     blocks = [lax.shift_right_logical(r, 9) for r in rows]
-    high, low = split2(jnp.concatenate([above_ref[...], below_ref[...]], axis=1))
+    high, low = split2(jnp.concatenate(arrived(near_ref, far_ref), axis=1))
     parts = jnp.concatenate([high, low], axis=0)
     acc[...] = lax.dot_general(masked(parts, blocks, 0, OWN_BLOCKS), hot, NT, preferred_element_type=F32)
     whole = [own_ref[:, b * L : (b + 1) * L] + fold(acc, b) for b in range(OWN_BLOCKS)]
     return whole, hot, blocks
 
 
-def settle_kernel(own_ref, above_ref, below_ref, highs_ref, lows_ref, out_ref, up_ref, down_ref, table_ref, acc):
-    whole, hot, blocks = settle(own_ref, above_ref, below_ref, highs_ref, lows_ref, acc)
+def settle_kernel(own_ref, near_ref, far_ref, highs_ref, lows_ref, out_ref, near_out, far_out, table_ref, acc):
+    whole, hot, blocks = settle(own_ref, near_ref, far_ref, highs_ref, lows_ref, acc)
     for b, value in enumerate(whole):
         end = min(NODE_DEV, (b + 1) * L)
         out_ref[:, b * L : end] = value[:, : end - b * L]
@@ -321,12 +333,13 @@
     rows = jnp.dot(table_ref[...], jnp.concatenate([hot, hot], axis=0), preferred_element_type=F32)
     zeros = [jnp.zeros((TR, 128), F32)] * 12
     values = picked(rows, blocks, 0, OWN_BLOCKS, zeros)
+    upward = upper_first()
     for j in range(6):
-        up_ref[:, j * 128 : (j + 1) * 128] = values[j]
-        down_ref[:, j * 128 : (j + 1) * 128] = values[6 + j]
-
-
-def settle_right(own, above, below, highs, lows):
+        near_out[:, j * 128 : (j + 1) * 128] = jnp.where(upward, values[j], values[6 + j])
+        far_out[:, j * 128 : (j + 1) * 128] = jnp.where(upward, values[6 + j], values[j])
+
+
+def settle_right(own, near, far, highs, lows):
     return pl.pallas_call(
         settle_kernel,
         out_shape=(
@@ -340,7 +353,7 @@
         scratch_shapes=[pltpu.VMEM((OWN_BLOCKS * 2 * TR, L), F32)],
         compiler_params=params(),
         name="settle",
-    )(own, above, below, highs, lows)
+    )(own, near, far, highs, lows)
 
 
 def gather_kernel(ids_ref, table_ref, jac_ref, out_ref, scale_ref, wide):
@@ -369,19 +382,23 @@
     )(ids, table, jac)
 
 
-def mass_kernel(ids_ref, start_ref, below_ref, above_ref, scale_ref, mass_ref, parts_ref, low_ref, high_ref, table, acc):
-    both = jnp.concatenate([below_ref[...], above_ref[...]], axis=1)
+def mass_kernel(ids_ref, start_ref, near_ref, far_ref, scale_ref, mass_ref, parts_ref, near_out, far_out, table, acc):
+    above, below = arrived(near_ref, far_ref)
+    both = jnp.concatenate([below, above], axis=1)
     for b in range(HALO_BLOCKS):
         high, low = split2(both[:, b * L : (b + 1) * L])
-        table[b * TR : (b + 1) * TR, :] = jnp.concatenate([high, low], axis=1)
+        table[b * 2 * TR : (b + 1) * 2 * TR, :] = jnp.concatenate([high, low], axis=0)
     acc[...] = jnp.zeros_like(acc)
 
     @pl.loop(0, SLOTS // CHUNK, unroll=True)
     def _(k):
         hot, blocks = tiles_of(ids_ref[aligned(k * TILES, TILES), :], TILES)
-        rows = jnp.dot(table[...], jnp.concatenate([hot, hot], axis=0), preferred_element_type=F32)
-        start = [start_ref[:, aligned(k * CHUNK + j * 128, 128)] for j in range(TILES)]
-        values = picked(rows, blocks, OWN_BLOCKS, HALO_BLOCKS, start)
+        rows = jnp.dot(table[...], hot, preferred_element_type=F32)
+        zeros = [jnp.zeros((2 * TR, 128), F32)] * TILES
+        found = picked(rows, blocks, OWN_BLOCKS, HALO_BLOCKS, zeros)
+        values = [
+            start_ref[:, aligned(k * CHUNK + j * 128, 128)] + found[j][:TR] + found[j][TR:] for j in range(TILES)
+        ]
         split = [split2(jnp.concatenate(values[2 * j : 2 * j + 2], axis=1)) for j in range(TILES // 2)]
         highs = jnp.concatenate([s[0] for s in split], axis=0)
         lows = jnp.concatenate([s[1] for s in split], axis=0)
@@ -402,22 +419,22 @@
             masked(parts, blocks, OWN_BLOCKS, HALO_BLOCKS), hot, NT, preferred_element_type=F32
         )
 
-    halves(acc, low_ref, high_ref)
-
-
-def mass_halo(ids, start, below, above, scale, mass):
+    halves(acc, near_out, far_out)
+
+
+def mass_halo(ids, start, near, far, scale, mass):
     return pl.pallas_call(
         mass_kernel,
         out_shape=(shape((2 * TR, SLOTS), BF), shape((TR, F)), shape((TR, F))),
         in_specs=vmem(6),
         out_specs=tuple(vmem(3)),
         scratch_shapes=[
-            pltpu.VMEM((HALO_BLOCKS * TR, 2 * L), BF),
+            pltpu.VMEM((HALO_BLOCKS * 2 * TR, L), BF),
             pltpu.VMEM((HALO_BLOCKS * 2 * TR, L), F32),
         ],
         compiler_params=params(),
         name="mass",
-    )(ids, start, below, above, scale, mass)
+    )(ids, start, near, far, scale, mass)
 
 
 def places():
@@ -432,8 +449,8 @@
     return jnp.concatenate([flat[:, 32 * i : 32 * i + 32] for i in range(4)], axis=0)
 
 
-def gram_kernel(own_ref, above_ref, below_ref, highs_ref, lows_ref, right_ref, out_ref, gram_ref, acc):
-    whole, _, _ = settle(own_ref, above_ref, below_ref, highs_ref, lows_ref, acc)
+def gram_kernel(own_ref, near_ref, far_ref, highs_ref, lows_ref, right_ref, out_ref, gram_ref, acc):
+    whole, _, _ = settle(own_ref, near_ref, far_ref, highs_ref, lows_ref, acc)
     for b, value in enumerate(whole):
         end = min(NODE_DEV, (b + 1) * L)
         out_ref[:, b * L : end] = value[:, : end - b * L]
@@ -454,7 +471,7 @@
     gram_ref[8:16, :] = lay_flat(jnp.where(row >= col, cross, second))
 
 
-def grams(own, above, below, highs, lows, right):
+def grams(own, near, far, highs, lows, right):
     return pl.pallas_call(
         gram_kernel,
         out_shape=(shape((TR, NODE_DEV)), shape((16, 128))),
@@ -463,7 +480,7 @@
         scratch_shapes=[pltpu.VMEM((OWN_BLOCKS * 2 * TR, L), F32)],
         compiler_params=params(),
         name="grams",
-    )(own, above, below, highs, lows, right)
+    )(own, near, far, highs, lows, right)
 
 
 def hdot(a, b, dims=(((1,), (0,)), ((), ()))):
@@ -570,9 +587,11 @@
     )(gram, right, image)
 
 
-def shifted(value, by):
-    pairs = [(i, i + by) for i in range(512) if 0 <= i + by < 512]
-    return lax.ppermute(value, AXES, pairs)
+def swapped(near, far):
+    outer = [(i, j) for k in range(1, 511, 2) for i, j in ((k, k + 1), (k + 1, k))]
+    far = lax.ppermute(far, AXES, outer)
+    near = lax.ppermute(near, AXES, [(i, i ^ 1) for i in range(512)])
+    return near, far
 
 
 def exchanged(value, axes):
@@ -585,19 +604,16 @@
     lows = send_down
     highs = send_up
     mass = jnp.asarray(mass_tiles())
-    ids, parts, low, high = right_side_halo(pair_target, pair_source, connectivity.T, pair_blocks, source_values)
-    above = shifted(low, -1)
-    below = shifted(high, 1)
+    ids, parts, near, far = right_side_halo(pair_target, pair_source, connectivity.T, pair_blocks, source_values)
+    near, far = swapped(near, far)
     own = scatter_own(ids, parts)
-    right, up, down, table = settle_right(own, above, below, highs, lows)
-    below = shifted(up, 1)
-    above = shifted(down, -1)
+    right, near, far, table = settle_right(own, near, far, highs, lows)
+    near, far = swapped(near, far)
     start, scale = gather_own(ids, table, jacobian[None, :])
-    parts, low, high = mass_halo(ids, start, below, above, scale, mass)
-    above = shifted(low, -1)
-    below = shifted(high, 1)
+    parts, near, far = mass_halo(ids, start, near, far, scale, mass)
+    near, far = swapped(near, far)
     own = scatter_own(ids, parts)
-    image, gram = grams(own, above, below, highs, lows, right)
+    image, gram = grams(own, near, far, highs, lows, right)
     gram = exchanged(gram, ("x", "y")).sum(0)
     gram = exchanged(gram, ("z", "c"))
     return finish(gram, right, image)

time: 108 us -> 99.3 us (0.919)
  blocking collectives: 46.8 us -> 39.4 us
    all_to_all x2, blocking collectives: 46.8 us -> 39.4 us  [exchanged(): return lax.all_to_all(copies, axes, 0, 0)]
  transfers between devices with their start and end apart: 6 -> 6, of which waited for: 0 -> 0; matrix products, arithmetic and copies ran while one was open for 0% -> 0% of each run, Pallas kernels for 12% -> 13%
where the time goes in v3:
time: 99.3 us; the launch traced here: 98.9 us
  blocking collectives  39.4 us (40%)
  Pallas kernels  35.8 us (36%)
  starting transfers between devices  20.8 us (21%)
  local copies, waits for them, and re-layouts  2.03 us (2%)
    all_to_all x2, blocking collectives, exchanged(): return lax.all_to_all(copies, axes, 0, 0)  39.4 us
    ppermute x3, starting transfers between devices, swapped(): near = lax.ppermute(near, AXES, [(i, i ^ 1) for i in range(512)])  12.6 us
    pallas_call x1, Pallas kernels, right_side_halo(): pl.pallas_call(rhs_kernel, out_shape=(shape((64, 128), jnp.int32), shape(...  9.68 us
    pallas_call x2, Pallas kernels, scatter_own(): pl.pallas_call(own_kernel, out_shape=shape((TR, OWN_BLOCKS * L)), in_spec...  8.49 us
    ppermute x3, starting transfers between devices, swapped(): far = lax.ppermute(far, AXES, outer)  8.14 us
    pallas_call x1, Pallas kernels, mass_halo(): pl.pallas_call(mass_kernel, out_shape=(shape((2 * TR, SLOTS), BF), shape(...  5.98 us
    pallas_call x1, Pallas kernels, finish(): pl.pallas_call(final_kernel, out_shape=(shape((TR, NODE_DEV)),) * 3, in_s...  4.02 us
    pallas_call x1, Pallas kernels, gather_own(): pl.pallas_call(gather_kernel, out_shape=(shape((TR, SLOTS)), shape((64, 1...  3.98 us
  transfers between devices with their start and end apart: 6, of which 0 were waited for; matrix products, arithmetic and copies ran while one was open for 0% of the time, Pallas kernels for 13%

profile of v3, /device:TPU:1, one launch (start us, length us, event | category | flops | bytes accessed | tf_op | source)
XLA Modules:
  0.0 98.9 jit_solution(3196143698306623150)
XLA Ops:
  0.6 9.7 %rhs.1 = (s32[64,128]{1,0:T(8,128)}, bf16[64,8192]{1,0:T(8,128)(2,1)}, f32[32,768]{1,0:T(8,128)}, f32[32,768]{1,0:T(8,128)}) custom-call(s32[256]{0:T(256)} %tgt_hbm.1, s32[256]{0:T(256)} %src_hbm.1, s32[64,128]{1,0:T(8,128)} %bitcast.3, bf16[256,4096]{1,0:T(8,128)(2,1)} %pb_hbm.1, bf16[32,8192]{1,0:T(8,128)(2,1)} %sv_hbm.1), custom_call_target="tpu_custom_call" | custom-call | tf_op jit(solution)/shard_map/rhs/pallas_call | solution.py:266
  10.3 8.8 %collective-permute-start = (f32[32,768]{1,0:T(8,128)}, f32[32,768]{1,0:T(8,128)S(1)}, u32[]{:S(2)}, u32[]{:S(2)}) collective-permute-start(f32[32,768]{1,0:T(8,128)} %get-tuple-element.20), channel_id=1, source_target_pairs={{0,1},{1,0},{2,3},{3,2},{4,5},{5,4},{6,7},{7,6},{8,9},{9,8},{10,11... | collective-permute-start | bytes 294920 | tf_op jit(solution)/shard_map/ppermute | solution.py:593
  19.1 1.9 %collective-permute-start.1 = (f32[32,768]{1,0:T(8,128)}, f32[32,768]{1,0:T(8,128)S(1)}, u32[]{:S(2)}, u32[]{:S(2)}) collective-permute-start(f32[32,768]{1,0:T(8,128)} %get-tuple-element.21), channel_id=1, source_target_pairs={{1,2},{2,1},{3,4},{4,3},{5,6},{6,5},{7,8},{8,7},{9,10},{10,9},{11,... | collective-permute-start | bytes 294920 | tf_op jit(solution)/shard_map/ppermute | solution.py:592
  21.0 0.0 copy-start.1
  21.1 0.7 copy-done.1
  21.8 1.2 %copy-done.4 = bf16[64,8192]{1,0:T(8,128)(2,1)S(1)} copy-done((bf16[64,8192]{1,0:T(8,128)(2,1)S(1)}, bf16[64,8192]{1,0:T(8,128)(2,1)}, u32[]{:S(2)}) %copy-start.4) | copy-done | bytes 1048600
  23.0 4.2 %own.2.own_ref = f32[32,3584]{1,0:T(8,128)S(1)} custom-call(s32[64,128]{1,0:T(8,128)S(1)} %copy-done.1, bf16[64,8192]{1,0:T(8,128)(2,1)S(1)} %copy-done.4), custom_call_target="tpu_custom_call" | custom-call | flops 3758096384 | bytes 2097152 | tf_op jit(solution)/shard_map/own/pallas_call | solution.py:303
  27.3 0.0 collective-permute-done.1.far_ref
  27.3 1.7 %settle.1 = (f32[32,3456]{1,0:T(8,128)S(1)}, f32[32,768]{1,0:T(8,128)S(1)}, f32[32,768]{1,0:T(8,128)S(1)}, bf16[224,1024]{1,0:T(8,128)(2,1)S(1)}) custom-call(f32[32,3584]{1,0:T(8,128)S(1)} %own.2.own_ref, f32[32,768]{1,0:T(8,128)S(1)} %collective-permute-done.near_ref, f32[32,768]{1,0:T(8,128)S(1)} %collective-permute-done.1.far_ref, ...), custom_call_target="tpu_custom_call" | custom-call | tf_op jit(solution)/shard_map/settle/pallas_call | solution.py:343
  29.1 1.9 %collective-permute-start.2 = (f32[32,768]{1,0:T(8,128)S(1)}, f32[32,768]{1,0:T(8,128)S(1)}, u32[]{:S(2)}, u32[]{:S(2)}) collective-permute-start(f32[32,768]{1,0:T(8,128)S(1)} %get-tuple-element.24), channel_id=1, source_target_pairs={{0,1},{1,0},{2,3},{3,2},{4,5},{5,4},{6,7},{7,6},{8,9},{9,8},{10,11... | collective-permute-start | bytes 294920 | tf_op jit(solution)/shard_map/ppermute | solution.py:593
  31.0 3.8 %collective-permute-start.3 = (f32[32,768]{1,0:T(8,128)S(1)}, f32[32,768]{1,0:T(8,128)S(1)}, u32[]{:S(2)}, u32[]{:S(2)}) collective-permute-start(f32[32,768]{1,0:T(8,128)S(1)} %get-tuple-element.25), channel_id=1, source_target_pairs={{1,2},{2,1},{3,4},{4,3},{5,6},{6,5},{7,8},{8,7},{9,10},{10,9},{11,... | collective-permute-start | bytes 294920 | tf_op jit(solution)/shard_map/ppermute | solution.py:592
  34.8 0.0 copy-start
  34.8 4.0 %gather.1 = (f32[32,8192]{1,0:T(8,128)S(1)}, f32[64,128]{1,0:T(8,128)S(1)}) custom-call(s32[64,128]{1,0:T(8,128)S(1)} %copy-done.1, bf16[224,1024]{1,0:T(8,128)(2,1)S(1)} %get-tuple-element.22.table_ref, f32[1,128]{1,0:T(1,128)S(1)} %bitcast.2), custom_call_target="tpu_custom_call" | custom-call | flops 3758096384 | bytes 2097152 | tf_op jit(solution)/shard_map/gather/pallas_call | solution.py:373
  38.8 0.0 collective-permute-done.2.near_ref
  38.8 0.0 collective-permute-done.3.far_ref
  38.9 6.0 %mass.1 = (bf16[64,8192]{1,0:T(8,128)(2,1)S(1)}, f32[32,768]{1,0:T(8,128)S(1)}, f32[32,768]{1,0:T(8,128)S(1)}) custom-call(s32[64,128]{1,0:T(8,128)S(1)} %copy-done.1, f32[32,8192]{1,0:T(8,128)S(1)} %get-tuple-element.23.start_ref, f32[32,768]{1,0:T(8,128)S(1)} %collective-permute-done.2.near_ref, f32[32,768]{1,0:T(8,128)S(1)} %collective-permute-done.3.far_ref, ...), custom_call_target="tpu_custom_call" | custom-call | tf_op jit(solution)/shard_map/mass/pallas_call | solution.py:426
  44.9 1.9 %collective-permute-start.4 = (f32[32,768]{1,0:T(8,128)S(1)}, f32[32,768]{1,0:T(8,128)S(1)}, u32[]{:S(2)}, u32[]{:S(2)}) collective-permute-start(f32[32,768]{1,0:T(8,128)S(1)} %get-tuple-element.28), channel_id=1, source_target_pairs={{0,1},{1,0},{2,3},{3,2},{4,5},{5,4},{6,7},{7,6},{8,9},{9,8},{10,11... | collective-permute-start | bytes 294920 | tf_op jit(solution)/shard_map/ppermute | solution.py:593
  46.8 2.4 %collective-permute-start.5 = (f32[32,768]{1,0:T(8,128)S(1)}, f32[32,768]{1,0:T(8,128)S(1)}, u32[]{:S(2)}, u32[]{:S(2)}) collective-permute-start(f32[32,768]{1,0:T(8,128)S(1)} %get-tuple-element.29), channel_id=1, source_target_pairs={{1,2},{2,1},{3,4},{4,3},{5,6},{6,5},{7,8},{8,7},{9,10},{10,9},{11,... | collective-permute-start | bytes 294920 | tf_op jit(solution)/shard_map/ppermute | solution.py:592
  49.2 4.2 %own.3.own_ref = f32[32,3584]{1,0:T(8,128)S(1)} custom-call(s32[64,128]{1,0:T(8,128)S(1)} %copy-done.1, bf16[64,8192]{1,0:T(8,128)(2,1)S(1)} %get-tuple-element.27.parts_ref), custom_call_target="tpu_custom_call" | custom-call | flops 3758096384 | bytes 2097152 | tf_op jit(solution)/shard_map/own/pallas_call | solution.py:303
  53.4 0.0 collective-permute-done.4.near_ref
  53.5 1.9 %grams.1 = (f32[32,3456]{1,0:T(8,128)S(1)}, f32[16,128]{1,0:T(8,128)S(1)}) custom-call(f32[32,3584]{1,0:T(8,128)S(1)} %own.3.own_ref, f32[32,768]{1,0:T(8,128)S(1)} %collective-permute-done.4.near_ref, f32[32,768]{1,0:T(8,128)S(1)} %collective-permute-done.5.far_ref, s32[1,768]{1,0:T(1,128)S(1)} %copy-done.2, s32[1,768]{1,0:T(1,128)S(1)} %copy-done.3, ...), custom_call_target="tpu_custom_call" | custom-call | tf_op jit(solution)/shard_map/grams/pallas_call | solution.py:475
  55.4 22.3 %all_to_all.10 = f32[32,16,128]{2,1,0:T(8,128)S(1)} all-to-all(f32[32,16,128]{2,1,0:T(8,128)S(1)} %broadcast_in_dim.7), channel_id=1, replica_groups=mesh['x'=4,'z'=8,'y'=8,'c'=2] {'x','y'}, dimensions={0} | all-to-all | bytes 524288 | tf_op jit(solution)/shard_map/all_to_all | solution.py:600
  77.8 17.1 %all_to_all.11.gram_ref = f32[16,16,128]{2,1,0:T(8,128)S(1)} all-to-all(f32[16,16,128]{2,1,0:T(8,128)S(1)} %broadcast_in_dim.8), channel_id=1, replica_groups=mesh['x'=4,'z'=8,'y'=8,'c'=2] {'z','c'}, dimensions={0} | all-to-all | bytes 262144 | tf_op jit(solution)/shard_map/all_to_all | solution.py:600
  94.9 4.0 %finish.1 = (f32[32,3456]{1,0:T(8,128)}, f32[32,3456]{1,0:T(8,128)}, f32[32,3456]{1,0:T(8,128)}) custom-call(f32[16,16,128]{2,1,0:T(8,128)S(1)} %all_to_all.11.gram_ref, f32[32,3456]{1,0:T(8,128)S(1)} %get-tuple-element.30.right_ref, f32[32,3456]{1,0:T(8,128)S(1)} %get-tuple-element.32.image_ref), custom_call_target="tpu_custom_call" | custom-call | tf_op jit(solution)/shard_map/finish/pallas_call | solution.py:580
  (13 shorter events, 0.1 us)
Async XLA Ops:
  10.3 17.0 %collective-permute-start = (f32[32,768]{1,0:T(8,128)}, f32[32,768]{1,0:T(8,128)S(1)}, u32[]{:S(2)}, u32[]{:S(2)}) collective-permute-start(f32[32,768]{1,0:T(8,128)} %get-tuple-element.20), channel_id=1, source_target_pairs={{0,1},{1,0},{2,3},{3,2},{4,5},{5,4},{6,7},{7,6},{8,9},{9,8},{10,11... | collective-permute-start | bytes 294920 | tf_op jit(solution)/shard_map/ppermute | solution.py:593
  19.1 8.2 %collective-permute-start.1 = (f32[32,768]{1,0:T(8,128)}, f32[32,768]{1,0:T(8,128)S(1)}, u32[]{:S(2)}, u32[]{:S(2)}) collective-permute-start(f32[32,768]{1,0:T(8,128)} %get-tuple-element.21), channel_id=1, source_target_pairs={{1,2},{2,1},{3,4},{4,3},{5,6},{6,5},{7,8},{8,7},{9,10},{10,9},{11,... | collective-permute-start | bytes 294920 | tf_op jit(solution)/shard_map/ppermute | solution.py:592
  21.0 0.8 copy-start.1
  21.8 1.2 %copy-start.4 = (bf16[64,8192]{1,0:T(8,128)(2,1)S(1)}, bf16[64,8192]{1,0:T(8,128)(2,1)}, u32[]{:S(2)}) copy-start(bf16[64,8192]{1,0:T(8,128)(2,1)} %get-tuple-element.19.parts_ref) | copy-start | bytes 3145732
  23.0 4.3 %copy-start.2 = (s32[1,768]{1,0:T(1,128)S(1)}, s32[1,768]{1,0:T(1,128)}, u32[]{:S(2)}) copy-start(s32[1,768]{1,0:T(1,128)} %highs_ref.3) | copy-start | bytes 9220
  23.0 4.3 %copy-start.3 = (s32[1,768]{1,0:T(1,128)S(1)}, s32[1,768]{1,0:T(1,128)}, u32[]{:S(2)}) copy-start(s32[1,768]{1,0:T(1,128)} %lows_ref.3) | copy-start | bytes 9220
  23.0 11.8 %copy-start.5 = (f32[128]{0:T(128)S(1)}, f32[128]{0:T(128)}, u32[]{:S(2)}) copy-start(f32[128]{0:T(128)} %param.12) | copy-start | bytes 1540
  29.1 9.8 %collective-permute-start.2 = (f32[32,768]{1,0:T(8,128)S(1)}, f32[32,768]{1,0:T(8,128)S(1)}, u32[]{:S(2)}, u32[]{:S(2)}) collective-permute-start(f32[32,768]{1,0:T(8,128)S(1)} %get-tuple-element.24), channel_id=1, source_target_pairs={{0,1},{1,0},{2,3},{3,2},{4,5},{5,4},{6,7},{7,6},{8,9},{9,8},{10,11... | collective-permute-start | bytes 294920 | tf_op jit(solution)/shard_map/ppermute | solution.py:593
  31.0 7.8 %collective-permute-start.3 = (f32[32,768]{1,0:T(8,128)S(1)}, f32[32,768]{1,0:T(8,128)S(1)}, u32[]{:S(2)}, u32[]{:S(2)}) collective-permute-start(f32[32,768]{1,0:T(8,128)S(1)} %get-tuple-element.25), channel_id=1, source_target_pairs={{1,2},{2,1},{3,4},{4,3},{5,6},{6,5},{7,8},{8,7},{9,10},{10,9},{11,... | collective-permute-start | bytes 294920 | tf_op jit(solution)/shard_map/ppermute | solution.py:592
  34.8 4.0 %copy-start = (bf16[256,512]{1,0:T(8,128)(2,1)S(1)}, bf16[256,512]{1,0:T(8,128)(2,1)}, u32[]{:S(2)}) copy-start(bf16[256,512]{1,0:T(8,128)(2,1)} %constant.4.clone.mass_ref) | copy-start | bytes 786436
  44.9 8.6 %collective-permute-start.4 = (f32[32,768]{1,0:T(8,128)S(1)}, f32[32,768]{1,0:T(8,128)S(1)}, u32[]{:S(2)}, u32[]{:S(2)}) collective-permute-start(f32[32,768]{1,0:T(8,128)S(1)} %get-tuple-element.28), channel_id=1, source_target_pairs={{0,1},{1,0},{2,3},{3,2},{4,5},{5,4},{6,7},{7,6},{8,9},{9,8},{10,11... | collective-permute-start | bytes 294920 | tf_op jit(solution)/shard_map/ppermute | solution.py:593
  46.8 6.7 %collective-permute-start.5 = (f32[32,768]{1,0:T(8,128)S(1)}, f32[32,768]{1,0:T(8,128)S(1)}, u32[]{:S(2)}, u32[]{:S(2)}) collective-permute-start(f32[32,768]{1,0:T(8,128)S(1)} %get-tuple-element.29), channel_id=1, source_target_pairs={{1,2},{2,1},{3,4},{4,3},{5,6},{6,5},{7,8},{8,7},{9,10},{10,9},{11,... | collective-permute-start | bytes 294920 | tf_op jit(solution)/shard_map/ppermute | solution.py:592

commit v4 on v3

--- a/solution.py
+++ b/solution.py
@@ -13,7 +13,9 @@
 SLOTS = 8192
 L = 512
 OWN_BLOCKS = 7
-HALO_BLOCKS = 3
+HALO = 256
+HALO_FIRST = OWN_BLOCKS * L // HALO
+HALO_BLOCKS = 6
 PAD = OWN_BLOCKS * L - NODE_DEV
 BF = jnp.bfloat16
 F32 = jnp.float32
@@ -71,16 +73,16 @@
     return high, low
 
 
-def one_hot(row):
-    spread = jnp.broadcast_to(row.astype(I16), (L, 128))
-    index = lax.broadcasted_iota(I16, (L, 128), 0)
+def one_hot(row, size=L):
+    spread = jnp.broadcast_to(row.astype(I16), (size, 128))
+    index = lax.broadcasted_iota(I16, (size, 128), 0)
     return jnp.where(spread == index, jnp.ones((), BF), jnp.zeros((), BF))
 
 
-def tiles_of(ids, count):
-    blocks = lax.shift_right_logical(ids, 9)
-    places = ids & (L - 1)
-    hot = jnp.concatenate([one_hot(places[j : j + 1]) for j in range(count)], axis=1)
+def tiles_of(ids, count, size=L):
+    blocks = lax.shift_right_logical(ids, size.bit_length() - 1)
+    places = ids & (size - 1)
+    hot = jnp.concatenate([one_hot(places[j : j + 1], size) for j in range(count)], axis=1)
     return hot, [blocks[j : j + 1] for j in range(count)]
 
 
@@ -109,8 +111,8 @@
     return out
 
 
-def add_scatter(acc, parts, ids, count, first, number):
-    hot, blocks = tiles_of(ids, count)
+def add_scatter(acc, parts, ids, count, first, number, size=L):
+    hot, blocks = tiles_of(ids, count, size)
     acc[...] += lax.dot_general(
         masked(parts, blocks, first, number), hot, NT, preferred_element_type=F32
     )
@@ -220,7 +222,7 @@
         both = join(join(e[0], e[1], odd, 32), join(e[2], e[3], odd, 32), up, 64).T
         for j in range(4):
             high, low = split2(both[j * TR : (j + 1) * TR])
-            parts_ref[:, aligned(g * 512 + j * 128, 128)] = jnp.concatenate([high, low], axis=0)
+            parts_ref[:, aligned(g * 512 + j * 128, 128)] = jnp.concatenate([high, low, id_rows(ids_ref[pl.ds(4 * g + j, 1), :])], axis=0)
 
     results = [
         pltpu.make_async_copy(a, b, sems.at[8 + i]) for i, (a, b) in enumerate(((ids_ref, ids_hbm), (parts_ref, parts_hbm)))
@@ -233,13 +235,69 @@
         copy.wait()
 
 
+def id_rows(ids):
+    row = lax.broadcasted_iota(jnp.int32, (16, 128), 0)
+    ids = jnp.broadcast_to(ids, (16, 128))
+    block = lax.shift_right_logical(ids, 9)
+    half = lax.shift_right_logical(ids, 8) & 1
+    return jnp.where(row == 0, block, jnp.where(row == 1, half, ids & 255)).astype(F32).astype(BF)
+
+
+def rows_to_ids(rows):
+    rows = rows.astype(F32)
+    return (rows[0:1] * 512.0 + rows[1:2] * 256.0 + rows[2:3]).astype(jnp.int32)
+
+
+def own_first_kernel(parts_hbm, out_ref, parts_ref, acc, sems):
+    copies = [
+        pltpu.make_async_copy(
+            parts_hbm.at[:, pl.ds(k * CHUNK, CHUNK)], parts_ref.at[:, pl.ds(k * CHUNK, CHUNK)], sems.at[k]
+        )
+        for k in range(SLOTS // CHUNK)
+    ]
+    for copy in copies:
+        copy.start()
+    acc[...] = jnp.zeros_like(acc)
+    for k, copy in enumerate(copies):
+        copy.wait()
+        ids = jnp.concatenate(
+            [rows_to_ids(parts_ref[2 * TR :, k * CHUNK + j * 128 : k * CHUNK + (j + 1) * 128]) for j in range(TILES)], axis=0
+        )
+        add_scatter(acc, parts_ref[: 2 * TR, k * CHUNK : (k + 1) * CHUNK], ids, TILES, 0, OWN_BLOCKS)
+    for b in range(OWN_BLOCKS):
+        out_ref[:, b * L : (b + 1) * L] = fold(acc, b)
+
+
+def scatter_own_first(parts):
+    return pl.pallas_call(
+        own_first_kernel,
+        out_shape=shape((TR, OWN_BLOCKS * L)),
+        in_specs=hbm(1),
+        out_specs=vmem(1)[0],
+        scratch_shapes=[
+            pltpu.VMEM((2 * TR + 16, SLOTS), BF),
+            pltpu.VMEM((OWN_BLOCKS * 2 * TR, L), F32),
+            pltpu.SemaphoreType.DMA((SLOTS // CHUNK,)),
+        ],
+        compiler_params=pltpu.CompilerParams(vmem_limit_bytes=54784 * 2**10),
+        cost_estimate=pl.CostEstimate(flops=2 * 448 * 512 * 8192, bytes_accessed=2**21, transcendentals=0),
+        name="own_first",
+    )(parts)
+
+
 def scatter_halo(ids_ref, parts_ref, acc):
     acc[...] = jnp.zeros_like(acc)
 
     @pl.loop(0, SLOTS // CHUNK, unroll=True)
     def _(k):
         add_scatter(
-            acc, parts_ref[:, aligned(k * CHUNK, CHUNK)], ids_ref[aligned(k * TILES, TILES), :], TILES, OWN_BLOCKS, HALO_BLOCKS
+            acc,
+            parts_ref[: 2 * TR, aligned(k * CHUNK, CHUNK)],
+            ids_ref[aligned(k * TILES, TILES), :],
+            TILES,
+            HALO_FIRST,
+            HALO_BLOCKS,
+            HALO,
         )
 
 
@@ -248,9 +306,8 @@
 
 
 def halves(acc, near_ref, far_ref):
-    first, middle, last = (fold(acc, b) for b in range(HALO_BLOCKS))
-    low = jnp.concatenate([first, middle[:, : F - L]], axis=1)
-    high = jnp.concatenate([middle[:, F - L :], last], axis=1)
+    half = HALO_BLOCKS // 2
+    low, high = (jnp.concatenate([fold(acc, b) for b in range(i, i + half)], axis=1) for i in (0, half))
     upward = upper_first()
     near_ref[...] = jnp.where(upward, high, low)
     far_ref[...] = jnp.where(upward, low, high)
@@ -265,7 +322,7 @@
 def right_side_halo(tgt, src, conn, pair_blocks, source_values):
     return pl.pallas_call(
         rhs_kernel,
-        out_shape=(shape((64, 128), jnp.int32), shape((2 * TR, SLOTS), BF), shape((TR, F)), shape((TR, F))),
+        out_shape=(shape((64, 128), jnp.int32), shape((2 * TR + 16, SLOTS), BF), shape((TR, F)), shape((TR, F))),
         in_specs=hbm(5),
         out_specs=tuple(hbm(2) + vmem(2)),
         scratch_shapes=[
@@ -275,12 +332,12 @@
             pltpu.VMEM((256, 4096), BF),
             pltpu.VMEM((TR, SLOTS), BF),
             pltpu.VMEM((64, 128), jnp.int32),
-            pltpu.VMEM((2 * TR, SLOTS), BF),
+            pltpu.VMEM((2 * TR + 16, SLOTS), BF),
             pltpu.VMEM((8448, 128), F32),
             pltpu.VMEM((2048, 128), BF),
             pltpu.VMEM((8192, 128), F32),
             pltpu.VMEM((128, 128), jnp.int32),
-            pltpu.VMEM((HALO_BLOCKS * 2 * TR, L), F32),
+            pltpu.VMEM((HALO_BLOCKS * 2 * TR, HALO), F32),
             pltpu.SemaphoreType.DMA((10,)),
         ],
         compiler_params=params(54),
@@ -315,7 +372,7 @@
 def settle(own_ref, near_ref, far_ref, highs_ref, lows_ref, acc):
     rows = [highs_ref[:, j * 128 : (j + 1) * 128] for j in range(6)] + [lows_ref[:, j * 128 : (j + 1) * 128] for j in range(6)]
     hot = jnp.concatenate([one_hot(r & (L - 1)) for r in rows], axis=1)
-    blocks = [lax.shift_right_logical(r, 9) for r in rows]
+    blocks = [lax.shift_right_logical(r, L.bit_length() - 1) for r in rows]
     high, low = split2(jnp.concatenate(arrived(near_ref, far_ref), axis=1))
     parts = jnp.concatenate([high, low], axis=0)
     acc[...] = lax.dot_general(masked(parts, blocks, 0, OWN_BLOCKS), hot, NT, preferred_element_type=F32)
@@ -386,16 +443,16 @@
     above, below = arrived(near_ref, far_ref)
     both = jnp.concatenate([below, above], axis=1)
     for b in range(HALO_BLOCKS):
-        high, low = split2(both[:, b * L : (b + 1) * L])
+        high, low = split2(both[:, b * HALO : (b + 1) * HALO])
         table[b * 2 * TR : (b + 1) * 2 * TR, :] = jnp.concatenate([high, low], axis=0)
     acc[...] = jnp.zeros_like(acc)
 
     @pl.loop(0, SLOTS // CHUNK, unroll=True)
     def _(k):
-        hot, blocks = tiles_of(ids_ref[aligned(k * TILES, TILES), :], TILES)
+        hot, blocks = tiles_of(ids_ref[aligned(k * TILES, TILES), :], TILES, HALO)
         rows = jnp.dot(table[...], hot, preferred_element_type=F32)
         zeros = [jnp.zeros((2 * TR, 128), F32)] * TILES
-        found = picked(rows, blocks, OWN_BLOCKS, HALO_BLOCKS, zeros)
+        found = picked(rows, blocks, HALO_FIRST, HALO_BLOCKS, zeros)
         values = [
             start_ref[:, aligned(k * CHUNK + j * 128, 128)] + found[j][:TR] + found[j][TR:] for j in range(TILES)
         ]
@@ -416,7 +473,7 @@
         parts = jnp.concatenate(tiles, axis=1)
         parts_ref[:, aligned(k * CHUNK, CHUNK)] = parts
         acc[...] += lax.dot_general(
-            masked(parts, blocks, OWN_BLOCKS, HALO_BLOCKS), hot, NT, preferred_element_type=F32
+            masked(parts, blocks, HALO_FIRST, HALO_BLOCKS), hot, NT, preferred_element_type=F32
         )
 
     halves(acc, near_out, far_out)
@@ -429,8 +486,8 @@
         in_specs=vmem(6),
         out_specs=tuple(vmem(3)),
         scratch_shapes=[
-            pltpu.VMEM((HALO_BLOCKS * 2 * TR, L), BF),
-            pltpu.VMEM((HALO_BLOCKS * 2 * TR, L), F32),
+            pltpu.VMEM((HALO_BLOCKS * 2 * TR, HALO), BF),
+            pltpu.VMEM((HALO_BLOCKS * 2 * TR, HALO), F32),
         ],
         compiler_params=params(),
         name="mass",
@@ -606,7 +663,7 @@
     mass = jnp.asarray(mass_tiles())
     ids, parts, near, far = right_side_halo(pair_target, pair_source, connectivity.T, pair_blocks, source_values)
     near, far = swapped(near, far)
-    own = scatter_own(ids, parts)
+    own = scatter_own_first(parts)
     right, near, far, table = settle_right(own, near, far, highs, lows)
     near, far = swapped(near, far)
     start, scale = gather_own(ids, table, jacobian[None, :])

time: 99.3 us -> 98 us (0.987)
  local copies, waits for them, and re-layouts: 2.03 us -> 0.06 us
    pallas_call x0 -> x1, Pallas kernels: none -> 5.72 us  [scatter_own_first(): pl.pallas_call(own_first_kernel, out_shape=shape((TR, OWN_BLOCKS * L)), i...]
    pallas_call x2 -> x1, Pallas kernels: 8.49 us -> 4.24 us  [scatter_own(): pl.pallas_call(own_kernel, out_shape=shape((TR, OWN_BLOCKS * L)), in_spec...]
    unnamed x12 -> x10, local copies, waits for them, and re-layouts: 2 us -> 0.03 us
  transfers between devices with their start and end apart: 6 -> 6, of which waited for: 0 -> 0; matrix products, arithmetic and copies ran while one was open for 0% -> 0% of each run, Pallas kernels for 13% -> 14%
where the time goes in v4:
time: 98 us; the launch traced here: 97.6 us
  blocking collectives  39.7 us (41%)
  Pallas kernels  36.2 us (37%)
  starting transfers between devices  20.8 us (21%)
    all_to_all x2, blocking collectives, exchanged(): return lax.all_to_all(copies, axes, 0, 0)  39.7 us
    ppermute x3, starting transfers between devices, swapped(): near = lax.ppermute(near, AXES, [(i, i ^ 1) for i in range(512)])  12.6 us
    pallas_call x1, Pallas kernels, right_side_halo(): pl.pallas_call(rhs_kernel, out_shape=(shape((64, 128), jnp.int32), shape(...  8.76 us
    ppermute x3, starting transfers between devices, swapped(): far = lax.ppermute(far, AXES, outer)  8.17 us
    pallas_call x1, Pallas kernels, mass_halo(): pl.pallas_call(mass_kernel, out_shape=(shape((2 * TR, SLOTS), BF), shape(...  5.78 us
    pallas_call x1, Pallas kernels, scatter_own_first(): pl.pallas_call(own_first_kernel, out_shape=shape((TR, OWN_BLOCKS * L)), i...  5.72 us
    pallas_call x1, Pallas kernels, scatter_own(): pl.pallas_call(own_kernel, out_shape=shape((TR, OWN_BLOCKS * L)), in_spec...  4.24 us
    pallas_call x1, Pallas kernels, finish(): pl.pallas_call(final_kernel, out_shape=(shape((TR, NODE_DEV)),) * 3, in_s...  4.03 us
  transfers between devices with their start and end apart: 6, of which 0 were waited for; matrix products, arithmetic and copies ran while one was open for 0% of the time, Pallas kernels for 14%

profile of v4, /device:TPU:1, one launch (start us, length us, event | category | flops | bytes accessed | tf_op | source)
XLA Modules:
  0.0 97.6 jit_solution(7002986588733741956)
XLA Ops:
  0.6 8.8 %rhs.1 = (s32[64,128]{1,0:T(8,128)}, bf16[80,8192]{1,0:T(8,128)(2,1)}, f32[32,768]{1,0:T(8,128)}, f32[32,768]{1,0:T(8,128)}) custom-call(s32[256]{0:T(256)} %tgt_hbm.1, s32[256]{0:T(256)} %src_hbm.1, s32[64,128]{1,0:T(8,128)} %bitcast.3, bf16[256,4096]{1,0:T(8,128)(2,1)} %pb_hbm.1, bf16[32,8192]{1,0:T(8,128)(2,1)} %sv_hbm.1), custom_call_target="tpu_custom_call" | custom-call | tf_op jit(solution)/shard_map/rhs/pallas_call | solution.py:323
  9.4 8.8 %collective-permute-start = (f32[32,768]{1,0:T(8,128)}, f32[32,768]{1,0:T(8,128)S(1)}, u32[]{:S(2)}, u32[]{:S(2)}) collective-permute-start(f32[32,768]{1,0:T(8,128)} %get-tuple-element.20), channel_id=1, source_target_pairs={{0,1},{1,0},{2,3},{3,2},{4,5},{5,4},{6,7},{7,6},{8,9},{9,8},{10,11... | collective-permute-start | bytes 294920 | tf_op jit(solution)/shard_map/ppermute | solution.py:650
  18.2 1.9 %collective-permute-start.1 = (f32[32,768]{1,0:T(8,128)}, f32[32,768]{1,0:T(8,128)S(1)}, u32[]{:S(2)}, u32[]{:S(2)}) collective-permute-start(f32[32,768]{1,0:T(8,128)} %get-tuple-element.21), channel_id=1, source_target_pairs={{1,2},{2,1},{3,4},{4,3},{5,6},{6,5},{7,8},{8,7},{9,10},{10,9},{11,... | collective-permute-start | bytes 294920 | tf_op jit(solution)/shard_map/ppermute | solution.py:649
  20.1 0.0 copy-start.2
  20.1 0.0 copy-start.3
  20.2 0.0 copy-start.1
  20.2 0.0 copy-start.4
  20.2 5.7 %own_first.1.own_ref = f32[32,3584]{1,0:T(8,128)S(1)} custom-call(bf16[80,8192]{1,0:T(8,128)(2,1)} %get-tuple-element.19.parts_hbm), custom_call_target="tpu_custom_call" | custom-call | flops 3758096384 | bytes 2097152 | tf_op jit(solution)/shard_map/own_first/pallas_call | solution.py:272
  25.9 0.0 collective-permute-done.near_ref
  25.9 1.7 %settle.1 = (f32[32,3456]{1,0:T(8,128)S(1)}, f32[32,768]{1,0:T(8,128)S(1)}, f32[32,768]{1,0:T(8,128)S(1)}, bf16[224,1024]{1,0:T(8,128)(2,1)S(1)}) custom-call(f32[32,3584]{1,0:T(8,128)S(1)} %own_first.1.own_ref, f32[32,768]{1,0:T(8,128)S(1)} %collective-permute-done.near_ref, f32[32,768]{1,0:T(8,128)S(1)} %collective-permute-done.1.far_ref, ...), custom_call_target="tpu_custom_call" | custom-call | tf_op jit(solution)/shard_map/settle/pallas_call | solution.py:400
  27.7 1.9 %collective-permute-start.2 = (f32[32,768]{1,0:T(8,128)S(1)}, f32[32,768]{1,0:T(8,128)S(1)}, u32[]{:S(2)}, u32[]{:S(2)}) collective-permute-start(f32[32,768]{1,0:T(8,128)S(1)} %get-tuple-element.24), channel_id=1, source_target_pairs={{0,1},{1,0},{2,3},{3,2},{4,5},{5,4},{6,7},{7,6},{8,9},{9,8},{10,11... | collective-permute-start | bytes 294920 | tf_op jit(solution)/shard_map/ppermute | solution.py:650
  29.6 3.8 %collective-permute-start.3 = (f32[32,768]{1,0:T(8,128)S(1)}, f32[32,768]{1,0:T(8,128)S(1)}, u32[]{:S(2)}, u32[]{:S(2)}) collective-permute-start(f32[32,768]{1,0:T(8,128)S(1)} %get-tuple-element.25), channel_id=1, source_target_pairs={{1,2},{2,1},{3,4},{4,3},{5,6},{6,5},{7,8},{8,7},{9,10},{10,9},{11,... | collective-permute-start | bytes 294920 | tf_op jit(solution)/shard_map/ppermute | solution.py:649
  33.5 0.0 copy-start
  33.5 4.0 %gather.1 = (f32[32,8192]{1,0:T(8,128)S(1)}, f32[64,128]{1,0:T(8,128)S(1)}) custom-call(s32[64,128]{1,0:T(8,128)S(1)} %copy-done.1, bf16[224,1024]{1,0:T(8,128)(2,1)S(1)} %get-tuple-element.22.table_ref, f32[1,128]{1,0:T(1,128)S(1)} %bitcast.2), custom_call_target="tpu_custom_call" | custom-call | flops 3758096384 | bytes 2097152 | tf_op jit(solution)/shard_map/gather/pallas_call | solution.py:430
  37.5 0.0 collective-permute-done.2.near_ref
  37.5 5.8 %mass.1 = (bf16[64,8192]{1,0:T(8,128)(2,1)S(1)}, f32[32,768]{1,0:T(8,128)S(1)}, f32[32,768]{1,0:T(8,128)S(1)}) custom-call(s32[64,128]{1,0:T(8,128)S(1)} %copy-done.1, f32[32,8192]{1,0:T(8,128)S(1)} %get-tuple-element.23.start_ref, f32[32,768]{1,0:T(8,128)S(1)} %collective-permute-done.2.near_ref, f32[32,768]{1,0:T(8,128)S(1)} %collective-permute-done.3.far_ref, ...), custom_call_target="tpu_custom_call" | custom-call | tf_op jit(solution)/shard_map/mass/pallas_call | solution.py:483
  43.3 1.9 %collective-permute-start.4 = (f32[32,768]{1,0:T(8,128)S(1)}, f32[32,768]{1,0:T(8,128)S(1)}, u32[]{:S(2)}, u32[]{:S(2)}) collective-permute-start(f32[32,768]{1,0:T(8,128)S(1)} %get-tuple-element.28), channel_id=1, source_target_pairs={{0,1},{1,0},{2,3},{3,2},{4,5},{5,4},{6,7},{7,6},{8,9},{9,8},{10,11... | collective-permute-start | bytes 294920 | tf_op jit(solution)/shard_map/ppermute | solution.py:650
  45.2 2.4 %collective-permute-start.5 = (f32[32,768]{1,0:T(8,128)S(1)}, f32[32,768]{1,0:T(8,128)S(1)}, u32[]{:S(2)}, u32[]{:S(2)}) collective-permute-start(f32[32,768]{1,0:T(8,128)S(1)} %get-tuple-element.29), channel_id=1, source_target_pairs={{1,2},{2,1},{3,4},{4,3},{5,6},{6,5},{7,8},{8,7},{9,10},{10,9},{11,... | collective-permute-start | bytes 294920 | tf_op jit(solution)/shard_map/ppermute | solution.py:649
  47.7 4.2 %own.1.own_ref = f32[32,3584]{1,0:T(8,128)S(1)} custom-call(s32[64,128]{1,0:T(8,128)S(1)} %copy-done.1, bf16[64,8192]{1,0:T(8,128)(2,1)S(1)} %get-tuple-element.27.parts_ref), custom_call_target="tpu_custom_call" | custom-call | flops 3758096384 | bytes 2097152 | tf_op jit(solution)/shard_map/own/pallas_call | solution.py:360
  51.9 0.0 collective-permute-done.4.near_ref
  51.9 1.9 %grams.1 = (f32[32,3456]{1,0:T(8,128)S(1)}, f32[16,128]{1,0:T(8,128)S(1)}) custom-call(f32[32,3584]{1,0:T(8,128)S(1)} %own.1.own_ref, f32[32,768]{1,0:T(8,128)S(1)} %collective-permute-done.4.near_ref, f32[32,768]{1,0:T(8,128)S(1)} %collective-permute-done.5.far_ref, s32[1,768]{1,0:T(1,128)S(1)} %copy-done.2, s32[1,768]{1,0:T(1,128)S(1)} %copy-done.3, ...), custom_call_target="tpu_custom_call" | custom-call | tf_op jit(solution)/shard_map/grams/pallas_call | solution.py:532
  53.9 22.3 %all_to_all.10 = f32[32,16,128]{2,1,0:T(8,128)S(1)} all-to-all(f32[32,16,128]{2,1,0:T(8,128)S(1)} %broadcast_in_dim.7), channel_id=1, replica_groups=mesh['x'=4,'z'=8,'y'=8,'c'=2] {'x','y'}, dimensions={0} | all-to-all | bytes 524288 | tf_op jit(solution)/shard_map/all_to_all | solution.py:657
  76.2 17.4 %all_to_all.11.gram_ref = f32[16,16,128]{2,1,0:T(8,128)S(1)} all-to-all(f32[16,16,128]{2,1,0:T(8,128)S(1)} %broadcast_in_dim.8), channel_id=1, replica_groups=mesh['x'=4,'z'=8,'y'=8,'c'=2] {'z','c'}, dimensions={0} | all-to-all | bytes 262144 | tf_op jit(solution)/shard_map/all_to_all | solution.py:657
  93.6 4.0 %finish.1 = (f32[32,3456]{1,0:T(8,128)}, f32[32,3456]{1,0:T(8,128)}, f32[32,3456]{1,0:T(8,128)}) custom-call(f32[16,16,128]{2,1,0:T(8,128)S(1)} %all_to_all.11.gram_ref, f32[32,3456]{1,0:T(8,128)S(1)} %get-tuple-element.30.right_ref, f32[32,3456]{1,0:T(8,128)S(1)} %get-tuple-element.32.image_ref), custom_call_target="tpu_custom_call" | custom-call | tf_op jit(solution)/shard_map/finish/pallas_call | solution.py:637
  (11 shorter events, 0.1 us)
Async XLA Ops:
  9.4 16.5 %collective-permute-start = (f32[32,768]{1,0:T(8,128)}, f32[32,768]{1,0:T(8,128)S(1)}, u32[]{:S(2)}, u32[]{:S(2)}) collective-permute-start(f32[32,768]{1,0:T(8,128)} %get-tuple-element.20), channel_id=1, source_target_pairs={{0,1},{1,0},{2,3},{3,2},{4,5},{5,4},{6,7},{7,6},{8,9},{9,8},{10,11... | collective-permute-start | bytes 294920 | tf_op jit(solution)/shard_map/ppermute | solution.py:650
  18.2 7.7 %collective-permute-start.1 = (f32[32,768]{1,0:T(8,128)}, f32[32,768]{1,0:T(8,128)S(1)}, u32[]{:S(2)}, u32[]{:S(2)}) collective-permute-start(f32[32,768]{1,0:T(8,128)} %get-tuple-element.21), channel_id=1, source_target_pairs={{1,2},{2,1},{3,4},{4,3},{5,6},{6,5},{7,8},{8,7},{9,10},{10,9},{11,... | collective-permute-start | bytes 294920 | tf_op jit(solution)/shard_map/ppermute | solution.py:649
  20.1 5.8 %copy-start.2 = (s32[1,768]{1,0:T(1,128)S(1)}, s32[1,768]{1,0:T(1,128)}, u32[]{:S(2)}) copy-start(s32[1,768]{1,0:T(1,128)} %highs_ref.3) | copy-start | bytes 9220
  20.1 5.8 %copy-start.3 = (s32[1,768]{1,0:T(1,128)S(1)}, s32[1,768]{1,0:T(1,128)}, u32[]{:S(2)}) copy-start(s32[1,768]{1,0:T(1,128)} %lows_ref.3) | copy-start | bytes 9220
  20.2 13.3 %copy-start.1 = (s32[64,128]{1,0:T(8,128)S(1)}, s32[64,128]{1,0:T(8,128)}, u32[]{:S(2)}) copy-start(s32[64,128]{1,0:T(8,128)} %get-tuple-element.18.ids_ref) | copy-start | bytes 98308
  20.2 13.3 %copy-start.4 = (f32[128]{0:T(128)S(1)}, f32[128]{0:T(128)}, u32[]{:S(2)}) copy-start(f32[128]{0:T(128)} %param.12) | copy-start | bytes 1540
  27.7 9.8 %collective-permute-start.2 = (f32[32,768]{1,0:T(8,128)S(1)}, f32[32,768]{1,0:T(8,128)S(1)}, u32[]{:S(2)}, u32[]{:S(2)}) collective-permute-start(f32[32,768]{1,0:T(8,128)S(1)} %get-tuple-element.24), channel_id=1, source_target_pairs={{0,1},{1,0},{2,3},{3,2},{4,5},{5,4},{6,7},{7,6},{8,9},{9,8},{10,11... | collective-permute-start | bytes 294920 | tf_op jit(solution)/shard_map/ppermute | solution.py:650
  29.6 7.9 %collective-permute-start.3 = (f32[32,768]{1,0:T(8,128)S(1)}, f32[32,768]{1,0:T(8,128)S(1)}, u32[]{:S(2)}, u32[]{:S(2)}) collective-permute-start(f32[32,768]{1,0:T(8,128)S(1)} %get-tuple-element.25), channel_id=1, source_target_pairs={{1,2},{2,1},{3,4},{4,3},{5,6},{6,5},{7,8},{8,7},{9,10},{10,9},{11,... | collective-permute-start | bytes 294920 | tf_op jit(solution)/shard_map/ppermute | solution.py:649
  33.5 4.0 %copy-start = (bf16[256,512]{1,0:T(8,128)(2,1)S(1)}, bf16[256,512]{1,0:T(8,128)(2,1)}, u32[]{:S(2)}) copy-start(bf16[256,512]{1,0:T(8,128)(2,1)} %constant.4.clone.mass_ref) | copy-start | bytes 786436
  43.3 8.6 %collective-permute-start.4 = (f32[32,768]{1,0:T(8,128)S(1)}, f32[32,768]{1,0:T(8,128)S(1)}, u32[]{:S(2)}, u32[]{:S(2)}) collective-permute-start(f32[32,768]{1,0:T(8,128)S(1)} %get-tuple-element.28), channel_id=1, source_target_pairs={{0,1},{1,0},{2,3},{3,2},{4,5},{5,4},{6,7},{7,6},{8,9},{9,8},{10,11... | collective-permute-start | bytes 294920 | tf_op jit(solution)/shard_map/ppermute | solution.py:650
  45.2 6.7 %collective-permute-start.5 = (f32[32,768]{1,0:T(8,128)S(1)}, f32[32,768]{1,0:T(8,128)S(1)}, u32[]{:S(2)}, u32[]{:S(2)}) collective-permute-start(f32[32,768]{1,0:T(8,128)S(1)} %get-tuple-element.29), channel_id=1, source_target_pairs={{1,2},{2,1},{3,4},{4,3},{5,6},{6,5},{7,8},{8,7},{9,10},{10,9},{11,... | collective-permute-start | bytes 294920 | tf_op jit(solution)/shard_map/ppermute | solution.py:649

commit v5 on v4

--- a/solution.py
+++ b/solution.py
@@ -216,19 +216,22 @@
     def join(a, b, mask, by):
         return jnp.where(mask, b, a) + pltpu.roll(jnp.where(mask, a, b), by, 1)
 
-    @pl.loop(0, 16, unroll=True)
-    def _(g):
+    results = [pltpu.make_async_copy(ids_ref, ids_hbm, sems.at[8])] + [
+        pltpu.make_async_copy(
+            parts_ref.at[:, pl.ds(i * CHUNK, CHUNK)], parts_hbm.at[:, pl.ds(i * CHUNK, CHUNK)], sems.at[9 + i]
+        )
+        for i in range(SLOTS // CHUNK)
+    ]
+    results[0].start()
+    for g in range(16):
         e = [total[aligned(g * 512 + j * 128, 128), :] for j in range(4)]
         both = join(join(e[0], e[1], odd, 32), join(e[2], e[3], odd, 32), up, 64).T
         for j in range(4):
             high, low = split2(both[j * TR : (j + 1) * TR])
             parts_ref[:, aligned(g * 512 + j * 128, 128)] = jnp.concatenate([high, low, id_rows(ids_ref[pl.ds(4 * g + j, 1), :])], axis=0)
-
-    results = [
-        pltpu.make_async_copy(a, b, sems.at[8 + i]) for i, (a, b) in enumerate(((ids_ref, ids_hbm), (parts_ref, parts_hbm)))
-    ]
-    for copy in results:
-        copy.start()
+        if g % 4 == 3:
+            results[1 + g // 4].start()
+
     scatter_halo(ids_ref, parts_ref, acc)
     halves(acc, near_ref, far_ref)
     for copy in results:
@@ -241,11 +244,6 @@
     block = lax.shift_right_logical(ids, 9)
     half = lax.shift_right_logical(ids, 8) & 1
     return jnp.where(row == 0, block, jnp.where(row == 1, half, ids & 255)).astype(F32).astype(BF)
-
-
-def rows_to_ids(rows):
-    rows = rows.astype(F32)
-    return (rows[0:1] * 512.0 + rows[1:2] * 256.0 + rows[2:3]).astype(jnp.int32)
 
 
 def own_first_kernel(parts_hbm, out_ref, parts_ref, acc, sems):
@@ -260,10 +258,11 @@
     acc[...] = jnp.zeros_like(acc)
     for k, copy in enumerate(copies):
         copy.wait()
-        ids = jnp.concatenate(
-            [rows_to_ids(parts_ref[2 * TR :, k * CHUNK + j * 128 : k * CHUNK + (j + 1) * 128]) for j in range(TILES)], axis=0
-        )
-        add_scatter(acc, parts_ref[: 2 * TR, k * CHUNK : (k + 1) * CHUNK], ids, TILES, 0, OWN_BLOCKS)
+        rows = [parts_ref[2 * TR :, k * CHUNK + j * 128 : k * CHUNK + (j + 1) * 128].astype(F32) for j in range(TILES)]
+        hot = jnp.concatenate([one_hot((r[1:2] * 256.0 + r[2:3]).astype(jnp.int32)) for r in rows], axis=1)
+        blocks = [r[0:1].astype(jnp.int32) for r in rows]
+        parts = masked(parts_ref[: 2 * TR, k * CHUNK : (k + 1) * CHUNK], blocks, 0, OWN_BLOCKS)
+        acc[...] += lax.dot_general(parts, hot, NT, preferred_element_type=F32)
     for b in range(OWN_BLOCKS):
         out_ref[:, b * L : (b + 1) * L] = fold(acc, b)
 
@@ -338,7 +337,7 @@
             pltpu.VMEM((8192, 128), F32),
             pltpu.VMEM((128, 128), jnp.int32),
             pltpu.VMEM((HALO_BLOCKS * 2 * TR, HALO), F32),
-            pltpu.SemaphoreType.DMA((10,)),
+            pltpu.SemaphoreType.DMA((9 + SLOTS // CHUNK,)),
         ],
         compiler_params=params(54),
         name="rhs",
@@ -586,7 +585,25 @@
     return jnp.concatenate(work, axis=0)
 
 
-def final_kernel(gram_ref, right_ref, image_ref, sol_ref, res_ref, new_ref):
+def final_kernel(gram_ref, right_ref, image_ref, sol_hbm, res_hbm, new_hbm, sol_ref, res_ref, new_ref, sems):
+    outs = [
+        pltpu.make_async_copy(a, b, sems.at[i])
+        for i, (a, b) in enumerate(((sol_ref, sol_hbm), (res_ref, res_hbm), (new_ref, new_hbm)))
+    ]
+    right = right_ref[...]
+    rh, rl = split2(right)
+    ih, il = split2(image_ref[...])
+    highs = jnp.concatenate([rh, ih], axis=0)
+    lows = jnp.concatenate([rl, il], axis=0)
+
+    def combine(coeffs):
+        high, low = split2(coeffs)
+        return (
+            jnp.dot(high, highs, preferred_element_type=F32)
+            + jnp.dot(high, lows, preferred_element_type=F32)
+            + jnp.dot(low, highs, preferred_element_type=F32)
+        )
+
     total = gram_ref[0]
     for i in range(1, gram_ref.shape[0]):
         total = total + gram_ref[i]
@@ -604,33 +621,22 @@
 
     weights_t = eliminate(jnp.concatenate([cross, rhs, zero, zero], axis=1), True)[:, TR : 2 * TR]
     weights = weights_t.T
+    out = combine(
+        jnp.concatenate([jnp.concatenate([weights, zero], axis=1), jnp.concatenate([zero, -weights], axis=1)], axis=0)
+    )
+    sol_ref[...] = out[:TR]
+    res_ref[...] = right + out[TR:]
+    outs[0].start()
+    outs[1].start()
     both = hdot(weights, jnp.concatenate([cross, images], axis=1))
     gram = rhs - 2.0 * both[:, :TR] + hdot(both[:, TR:], weights_t)
     work = eliminate(jnp.concatenate([gram, eye, weights, zero], axis=1), False)
     inverse = work[:, TR : 2 * TR]
     mixed = work[:, 2 * TR : 3 * TR]
-    coeffs = jnp.concatenate(
-        [
-            jnp.concatenate([weights, zero], axis=1),
-            jnp.concatenate([zero, -weights], axis=1),
-            jnp.concatenate([inverse, -mixed], axis=1),
-        ],
-        axis=0,
-    )
-    high, low = split2(coeffs)
-    right = right_ref[...]
-    rh, rl = split2(right)
-    ih, il = split2(image_ref[...])
-    highs = jnp.concatenate([rh, ih], axis=0)
-    lows = jnp.concatenate([rl, il], axis=0)
-    out = (
-        jnp.dot(high, highs, preferred_element_type=F32)
-        + jnp.dot(high, lows, preferred_element_type=F32)
-        + jnp.dot(low, highs, preferred_element_type=F32)
-    )
-    sol_ref[...] = out[:TR]
-    res_ref[...] = right + out[TR : 2 * TR]
-    new_ref[...] = out[2 * TR :]
+    new_ref[...] = combine(jnp.concatenate([inverse, -mixed], axis=1))
+    outs[2].start()
+    for copy in outs:
+        copy.wait()
 
 
 def finish(gram, right, image):
@@ -638,7 +644,8 @@
         final_kernel,
         out_shape=(shape((TR, NODE_DEV)),) * 3,
         in_specs=vmem(3),
-        out_specs=tuple(vmem(3)),
+        out_specs=tuple(hbm(3)),
+        scratch_shapes=[pltpu.VMEM((TR, NODE_DEV), F32)] * 3 + [pltpu.SemaphoreType.DMA((3,))],
         compiler_params=params(),
         name="finish",
     )(gram, right, image)

time: 98 us -> 97.5 us (level)
  no operation moved by 1% of the time
where the time goes in v5:
time: 97.5 us; the launch traced here: 97.1 us
  blocking collectives  39.8 us (41%)
  Pallas kernels  35.4 us (36%)
  starting transfers between devices  20.8 us (21%)
  between operations  1.02 us (1%)
    all_to_all x2, blocking collectives, exchanged(): return lax.all_to_all(copies, axes, 0, 0)  39.8 us
    ppermute x3, starting transfers between devices, swapped(): near = lax.ppermute(near, AXES, [(i, i ^ 1) for i in range(512)])  12.6 us
    pallas_call x1, Pallas kernels, right_side_halo(): pl.pallas_call(rhs_kernel, out_shape=(shape((64, 128), jnp.int32), shape(...  8.32 us
    ppermute x3, starting transfers between devices, swapped(): far = lax.ppermute(far, AXES, outer)  8.15 us
    pallas_call x1, Pallas kernels, mass_halo(): pl.pallas_call(mass_kernel, out_shape=(shape((2 * TR, SLOTS), BF), shape(...  5.78 us
    pallas_call x1, Pallas kernels, scatter_own_first(): pl.pallas_call(own_first_kernel, out_shape=shape((TR, OWN_BLOCKS * L)), i...  5.58 us
    pallas_call x1, Pallas kernels, scatter_own(): pl.pallas_call(own_kernel, out_shape=shape((TR, OWN_BLOCKS * L)), in_spec...  4.24 us
    pallas_call x1, Pallas kernels, gather_own(): pl.pallas_call(gather_kernel, out_shape=(shape((TR, SLOTS)), shape((64, 1...  3.98 us
  transfers between devices with their start and end apart: 6, of which 0 were waited for; matrix products, arithmetic and copies ran while one was open for 0% of the time, Pallas kernels for 14%

profile of v5, /device:TPU:1, one launch (start us, length us, event | category | flops | bytes accessed | tf_op | source)
XLA Modules:
  0.0 97.1 jit_solution(11309647793972194876)
XLA Ops:
  0.6 8.3 %rhs.1 = (s32[64,128]{1,0:T(8,128)}, bf16[80,8192]{1,0:T(8,128)(2,1)}, f32[32,768]{1,0:T(8,128)}, f32[32,768]{1,0:T(8,128)}) custom-call(s32[256]{0:T(256)} %tgt_hbm.1, s32[256]{0:T(256)} %src_hbm.1, s32[64,128]{1,0:T(8,128)} %bitcast.3, bf16[256,4096]{1,0:T(8,128)(2,1)} %pb_hbm.1, bf16[32,8192]{1,0:T(8,128)(2,1)} %sv_hbm.1), custom_call_target="tpu_custom_call" | custom-call | tf_op jit(solution)/shard_map/rhs/pallas_call | solution.py:322
  9.0 8.8 %collective-permute-start = (f32[32,768]{1,0:T(8,128)}, f32[32,768]{1,0:T(8,128)S(1)}, u32[]{:S(2)}, u32[]{:S(2)}) collective-permute-start(f32[32,768]{1,0:T(8,128)} %get-tuple-element.20), channel_id=1, source_target_pairs={{0,1},{1,0},{2,3},{3,2},{4,5},{5,4},{6,7},{7,6},{8,9},{9,8},{10,11... | collective-permute-start | bytes 294920 | tf_op jit(solution)/shard_map/ppermute | solution.py:657
  17.8 1.9 %collective-permute-start.1 = (f32[32,768]{1,0:T(8,128)}, f32[32,768]{1,0:T(8,128)S(1)}, u32[]{:S(2)}, u32[]{:S(2)}) collective-permute-start(f32[32,768]{1,0:T(8,128)} %get-tuple-element.21), channel_id=1, source_target_pairs={{1,2},{2,1},{3,4},{4,3},{5,6},{6,5},{7,8},{8,7},{9,10},{10,9},{11,... | collective-permute-start | bytes 294920 | tf_op jit(solution)/shard_map/ppermute | solution.py:656
  19.7 0.0 copy-start.2
  19.7 0.0 copy-start.3
  19.7 0.0 copy-start.1
  19.7 0.0 copy-start.4
  19.7 5.6 %own_first.1.own_ref = f32[32,3584]{1,0:T(8,128)S(1)} custom-call(bf16[80,8192]{1,0:T(8,128)(2,1)} %get-tuple-element.19.parts_hbm), custom_call_target="tpu_custom_call" | custom-call | flops 3758096384 | bytes 2097152 | tf_op jit(solution)/shard_map/own_first/pallas_call | solution.py:271
  25.3 0.0 collective-permute-done.near_ref
  25.4 1.7 %settle.1 = (f32[32,3456]{1,0:T(8,128)S(1)}, f32[32,768]{1,0:T(8,128)S(1)}, f32[32,768]{1,0:T(8,128)S(1)}, bf16[224,1024]{1,0:T(8,128)(2,1)S(1)}) custom-call(f32[32,3584]{1,0:T(8,128)S(1)} %own_first.1.own_ref, f32[32,768]{1,0:T(8,128)S(1)} %collective-permute-done.near_ref, f32[32,768]{1,0:T(8,128)S(1)} %collective-permute-done.1.far_ref, ...), custom_call_target="tpu_custom_call" | custom-call | tf_op jit(solution)/shard_map/settle/pallas_call | solution.py:399
  27.1 1.9 %collective-permute-start.2 = (f32[32,768]{1,0:T(8,128)S(1)}, f32[32,768]{1,0:T(8,128)S(1)}, u32[]{:S(2)}, u32[]{:S(2)}) collective-permute-start(f32[32,768]{1,0:T(8,128)S(1)} %get-tuple-element.24), channel_id=1, source_target_pairs={{0,1},{1,0},{2,3},{3,2},{4,5},{5,4},{6,7},{7,6},{8,9},{9,8},{10,11... | collective-permute-start | bytes 294920 | tf_op jit(solution)/shard_map/ppermute | solution.py:657
  29.0 3.8 %collective-permute-start.3 = (f32[32,768]{1,0:T(8,128)S(1)}, f32[32,768]{1,0:T(8,128)S(1)}, u32[]{:S(2)}, u32[]{:S(2)}) collective-permute-start(f32[32,768]{1,0:T(8,128)S(1)} %get-tuple-element.25), channel_id=1, source_target_pairs={{1,2},{2,1},{3,4},{4,3},{5,6},{6,5},{7,8},{8,7},{9,10},{10,9},{11,... | collective-permute-start | bytes 294920 | tf_op jit(solution)/shard_map/ppermute | solution.py:656
  32.9 0.0 copy-start
  32.9 4.0 %gather.1 = (f32[32,8192]{1,0:T(8,128)S(1)}, f32[64,128]{1,0:T(8,128)S(1)}) custom-call(s32[64,128]{1,0:T(8,128)S(1)} %copy-done.1, bf16[224,1024]{1,0:T(8,128)(2,1)S(1)} %get-tuple-element.22.table_ref, f32[1,128]{1,0:T(1,128)S(1)} %bitcast.2), custom_call_target="tpu_custom_call" | custom-call | flops 3758096384 | bytes 2097152 | tf_op jit(solution)/shard_map/gather/pallas_call | solution.py:429
  36.9 0.0 collective-permute-done.3.far_ref
  36.9 5.8 %mass.1 = (bf16[64,8192]{1,0:T(8,128)(2,1)S(1)}, f32[32,768]{1,0:T(8,128)S(1)}, f32[32,768]{1,0:T(8,128)S(1)}) custom-call(s32[64,128]{1,0:T(8,128)S(1)} %copy-done.1, f32[32,8192]{1,0:T(8,128)S(1)} %get-tuple-element.23.start_ref, f32[32,768]{1,0:T(8,128)S(1)} %collective-permute-done.2.near_ref, f32[32,768]{1,0:T(8,128)S(1)} %collective-permute-done.3.far_ref, ...), custom_call_target="tpu_custom_call" | custom-call | tf_op jit(solution)/shard_map/mass/pallas_call | solution.py:482
  42.7 1.9 %collective-permute-start.4 = (f32[32,768]{1,0:T(8,128)S(1)}, f32[32,768]{1,0:T(8,128)S(1)}, u32[]{:S(2)}, u32[]{:S(2)}) collective-permute-start(f32[32,768]{1,0:T(8,128)S(1)} %get-tuple-element.28), channel_id=1, source_target_pairs={{0,1},{1,0},{2,3},{3,2},{4,5},{5,4},{6,7},{7,6},{8,9},{9,8},{10,11... | collective-permute-start | bytes 294920 | tf_op jit(solution)/shard_map/ppermute | solution.py:657
  44.6 2.4 %collective-permute-start.5 = (f32[32,768]{1,0:T(8,128)S(1)}, f32[32,768]{1,0:T(8,128)S(1)}, u32[]{:S(2)}, u32[]{:S(2)}) collective-permute-start(f32[32,768]{1,0:T(8,128)S(1)} %get-tuple-element.29), channel_id=1, source_target_pairs={{1,2},{2,1},{3,4},{4,3},{5,6},{6,5},{7,8},{8,7},{9,10},{10,9},{11,... | collective-permute-start | bytes 294920 | tf_op jit(solution)/shard_map/ppermute | solution.py:656
  47.1 4.2 %own.1.own_ref = f32[32,3584]{1,0:T(8,128)S(1)} custom-call(s32[64,128]{1,0:T(8,128)S(1)} %copy-done.1, bf16[64,8192]{1,0:T(8,128)(2,1)S(1)} %get-tuple-element.27.parts_ref), custom_call_target="tpu_custom_call" | custom-call | flops 3758096384 | bytes 2097152 | tf_op jit(solution)/shard_map/own/pallas_call | solution.py:359
  51.3 0.0 collective-permute-done.5.far_ref
  51.3 1.9 %grams.1 = (f32[32,3456]{1,0:T(8,128)S(1)}, f32[16,128]{1,0:T(8,128)S(1)}) custom-call(f32[32,3584]{1,0:T(8,128)S(1)} %own.1.own_ref, f32[32,768]{1,0:T(8,128)S(1)} %collective-permute-done.4.near_ref, f32[32,768]{1,0:T(8,128)S(1)} %collective-permute-done.5.far_ref, s32[1,768]{1,0:T(1,128)S(1)} %copy-done.2, s32[1,768]{1,0:T(1,128)S(1)} %copy-done.3, ...), custom_call_target="tpu_custom_call" | custom-call | tf_op jit(solution)/shard_map/grams/pallas_call | solution.py:531
  53.3 22.3 %all_to_all.10 = f32[32,16,128]{2,1,0:T(8,128)S(1)} all-to-all(f32[32,16,128]{2,1,0:T(8,128)S(1)} %broadcast_in_dim.7), channel_id=1, replica_groups=mesh['x'=4,'z'=8,'y'=8,'c'=2] {'x','y'}, dimensions={0} | all-to-all | bytes 524288 | tf_op jit(solution)/shard_map/all_to_all | solution.py:664
  75.6 17.5 %all_to_all.11.gram_ref = f32[16,16,128]{2,1,0:T(8,128)S(1)} all-to-all(f32[16,16,128]{2,1,0:T(8,128)S(1)} %broadcast_in_dim.8), channel_id=1, replica_groups=mesh['x'=4,'z'=8,'y'=8,'c'=2] {'z','c'}, dimensions={0} | all-to-all | bytes 262144 | tf_op jit(solution)/shard_map/all_to_all | solution.py:664
  93.1 3.8 %finish.1 = (f32[32,3456]{1,0:T(8,128)}, f32[32,3456]{1,0:T(8,128)}, f32[32,3456]{1,0:T(8,128)}) custom-call(f32[16,16,128]{2,1,0:T(8,128)S(1)} %all_to_all.11.gram_ref, f32[32,3456]{1,0:T(8,128)S(1)} %get-tuple-element.30.right_ref, f32[32,3456]{1,0:T(8,128)S(1)} %get-tuple-element.32.image_ref), custom_call_target="tpu_custom_call" | custom-call | tf_op jit(solution)/shard_map/finish/pallas_call | solution.py:643
  (11 shorter events, 0.1 us)
Async XLA Ops:
  9.0 16.4 %collective-permute-start = (f32[32,768]{1,0:T(8,128)}, f32[32,768]{1,0:T(8,128)S(1)}, u32[]{:S(2)}, u32[]{:S(2)}) collective-permute-start(f32[32,768]{1,0:T(8,128)} %get-tuple-element.20), channel_id=1, source_target_pairs={{0,1},{1,0},{2,3},{3,2},{4,5},{5,4},{6,7},{7,6},{8,9},{9,8},{10,11... | collective-permute-start | bytes 294920 | tf_op jit(solution)/shard_map/ppermute | solution.py:657
  17.8 7.6 %collective-permute-start.1 = (f32[32,768]{1,0:T(8,128)}, f32[32,768]{1,0:T(8,128)S(1)}, u32[]{:S(2)}, u32[]{:S(2)}) collective-permute-start(f32[32,768]{1,0:T(8,128)} %get-tuple-element.21), channel_id=1, source_target_pairs={{1,2},{2,1},{3,4},{4,3},{5,6},{6,5},{7,8},{8,7},{9,10},{10,9},{11,... | collective-permute-start | bytes 294920 | tf_op jit(solution)/shard_map/ppermute | solution.py:656
  19.7 5.7 %copy-start.2 = (s32[1,768]{1,0:T(1,128)S(1)}, s32[1,768]{1,0:T(1,128)}, u32[]{:S(2)}) copy-start(s32[1,768]{1,0:T(1,128)} %highs_ref.3) | copy-start | bytes 9220
  19.7 5.7 %copy-start.3 = (s32[1,768]{1,0:T(1,128)S(1)}, s32[1,768]{1,0:T(1,128)}, u32[]{:S(2)}) copy-start(s32[1,768]{1,0:T(1,128)} %lows_ref.3) | copy-start | bytes 9220
  19.7 13.2 %copy-start.1 = (s32[64,128]{1,0:T(8,128)S(1)}, s32[64,128]{1,0:T(8,128)}, u32[]{:S(2)}) copy-start(s32[64,128]{1,0:T(8,128)} %get-tuple-element.18.ids_ref) | copy-start | bytes 98308
  19.7 13.2 %copy-start.4 = (f32[128]{0:T(128)S(1)}, f32[128]{0:T(128)}, u32[]{:S(2)}) copy-start(f32[128]{0:T(128)} %param.12) | copy-start | bytes 1540
  27.1 9.8 %collective-permute-start.2 = (f32[32,768]{1,0:T(8,128)S(1)}, f32[32,768]{1,0:T(8,128)S(1)}, u32[]{:S(2)}, u32[]{:S(2)}) collective-permute-start(f32[32,768]{1,0:T(8,128)S(1)} %get-tuple-element.24), channel_id=1, source_target_pairs={{0,1},{1,0},{2,3},{3,2},{4,5},{5,4},{6,7},{7,6},{8,9},{9,8},{10,11... | collective-permute-start | bytes 294920 | tf_op jit(solution)/shard_map/ppermute | solution.py:657
  29.0 7.9 %collective-permute-start.3 = (f32[32,768]{1,0:T(8,128)S(1)}, f32[32,768]{1,0:T(8,128)S(1)}, u32[]{:S(2)}, u32[]{:S(2)}) collective-permute-start(f32[32,768]{1,0:T(8,128)S(1)} %get-tuple-element.25), channel_id=1, source_target_pairs={{1,2},{2,1},{3,4},{4,3},{5,6},{6,5},{7,8},{8,7},{9,10},{10,9},{11,... | collective-permute-start | bytes 294920 | tf_op jit(solution)/shard_map/ppermute | solution.py:656
  32.9 4.0 %copy-start = (bf16[256,512]{1,0:T(8,128)(2,1)S(1)}, bf16[256,512]{1,0:T(8,128)(2,1)}, u32[]{:S(2)}) copy-start(bf16[256,512]{1,0:T(8,128)(2,1)} %constant.4.clone.mass_ref) | copy-start | bytes 786436
  42.7 8.6 %collective-permute-start.4 = (f32[32,768]{1,0:T(8,128)S(1)}, f32[32,768]{1,0:T(8,128)S(1)}, u32[]{:S(2)}, u32[]{:S(2)}) collective-permute-start(f32[32,768]{1,0:T(8,128)S(1)} %get-tuple-element.28), channel_id=1, source_target_pairs={{0,1},{1,0},{2,3},{3,2},{4,5},{5,4},{6,7},{7,6},{8,9},{9,8},{10,11... | collective-permute-start | bytes 294920 | tf_op jit(solution)/shard_map/ppermute | solution.py:657
  44.6 6.7 %collective-permute-start.5 = (f32[32,768]{1,0:T(8,128)S(1)}, f32[32,768]{1,0:T(8,128)S(1)}, u32[]{:S(2)}, u32[]{:S(2)}) collective-permute-start(f32[32,768]{1,0:T(8,128)S(1)} %get-tuple-element.29), channel_id=1, source_target_pairs={{1,2},{2,1},{3,4},{4,3},{5,6},{6,5},{7,8},{8,7},{9,10},{10,9},{11,... | collective-permute-start | bytes 294920 | tf_op jit(solution)/shard_map/ppermute | solution.py:656

commit v6 on v5

--- a/solution.py
+++ b/solution.py
@@ -124,7 +124,7 @@
 
 CHUNK = 2048
 TILES = CHUNK // 128
-UNROLL = 128
+UNROLL = 64
 
 
 def rhs_kernel(
@@ -169,14 +169,28 @@
         source[g * 128 : (g + 1) * 128, :] = stack.astype(F32).T.astype(BF)
     for copy in small[1:]:
         copy.wait()
-    for i in range(4):
-        large[i].wait()
-
-        @pl.loop(4 * i, 4 * i + 4)
-        def _(g):
+    low32 = lax.broadcasted_iota(jnp.int32, (32, 128), 1) < 64
+    group = lax.shift_right_logical(lax.broadcasted_iota(jnp.int32, (64, 128), 1), 5).astype(I16)
+
+    @pl.loop(0, 256 // UNROLL)
+    def _(i):
+        pltpu.make_async_copy(pb_hbm.at[aligned(64 * i, 64), :], pb_ref.at[aligned(64 * i, 64), :], sems.at[4 + i]).wait()
+        for q in range(4):
             for c in range(32):
-                rows = pb_ref[aligned(g * 16, 16), c * 128 : (c + 1) * 128].astype(F32)
-                blocks[pl.ds(g * 528 + c, 16, stride=33), :] = rows
+                rows = pb_ref[aligned(i * 64 + q * 16, 16), c * 128 : (c + 1) * 128].astype(F32)
+                blocks[pl.ds((i * 4 + q) * 528 + c, 16, stride=33), :] = rows
+        for u in range(UNROLL):
+            p = i * UNROLL + u
+            s = src_ref[p]
+            e = tgt_ref[p]
+            k = lax.shift_right_logical(s, 1) & 3
+            start = lax.shift_right_logical(s, 3) * 128 + (s & 1) * 64
+            value = jnp.where(group == k.astype(I16), source[aligned(start, 64), :], zero16)
+            block = blocks[pl.ds(p * 33,32), :]
+            rows = jnp.concatenate([jnp.where(low32, block, zero), jnp.where(low32, zero, block)], axis=0).astype(BF)
+            total[aligned(e * 64, 64), :] += jnp.dot(
+                rows, jnp.concatenate([value, value], axis=0), preferred_element_type=F32
+            )
 
     conn = conn_ref[...].astype(F32).T.astype(jnp.int32)
     row = lax.broadcasted_iota(jnp.int32, (64, 64), 0)
@@ -190,24 +204,6 @@
     wide[...] = jnp.concatenate([ids, ids], axis=1)
     lane64 = lax.broadcasted_iota(jnp.int32, (64, 128), 1)
     ids_ref[...] = jnp.where(lane64 < 64, wide[pl.ds(0, 64, stride=2), :], wide[pl.ds(1, 64, stride=2), :])
-
-    low32 = lax.broadcasted_iota(jnp.int32, (32, 128), 1) < 64
-    group = lax.shift_right_logical(lane64, 5).astype(I16)
-
-    @pl.loop(0, 256 // UNROLL)
-    def _(i):
-        for u in range(UNROLL):
-            p = i * UNROLL + u
-            s = src_ref[p]
-            e = tgt_ref[p]
-            k = lax.shift_right_logical(s, 1) & 3
-            start = lax.shift_right_logical(s, 3) * 128 + (s & 1) * 64
-            value = jnp.where(group == k.astype(I16), source[aligned(start, 64), :], zero16)
-            block = blocks[pl.ds(p * 33,32), :]
-            rows = jnp.concatenate([jnp.where(low32, block, zero), jnp.where(low32, zero, block)], axis=0).astype(BF)
-            total[aligned(e * 64, 64), :] += jnp.dot(
-                rows, jnp.concatenate([value, value], axis=0), preferred_element_type=F32
-            )
 
     lanes = lax.shift_right_logical(lax.broadcasted_iota(jnp.int32, (128, 128), 1), 5)
     odd = (lanes & 1) == 1

time: 97.5 us -> 97.2 us (level)
  no operation moved by 1% of the time
where the time goes in v6:
time: 97.2 us; the launch traced here: 96.9 us
  blocking collectives  39.9 us (41%)
  Pallas kernels  35.1 us (36%)
  starting transfers between devices  20.8 us (21%)
  between operations  1.02 us (1%)
    all_to_all x2, blocking collectives, exchanged(): return lax.all_to_all(copies, axes, 0, 0)  39.9 us
    ppermute x3, starting transfers between devices, swapped(): near = lax.ppermute(near, AXES, [(i, i ^ 1) for i in range(512)])  12.6 us
    ppermute x3, starting transfers between devices, swapped(): far = lax.ppermute(far, AXES, outer)  8.14 us
    pallas_call x1, Pallas kernels, right_side_halo(): pl.pallas_call(rhs_kernel, out_shape=(shape((64, 128), jnp.int32), shape(...  8.04 us
    pallas_call x1, Pallas kernels, mass_halo(): pl.pallas_call(mass_kernel, out_shape=(shape((2 * TR, SLOTS), BF), shape(...  5.78 us
    pallas_call x1, Pallas kernels, scatter_own_first(): pl.pallas_call(own_first_kernel, out_shape=shape((TR, OWN_BLOCKS * L)), i...  5.59 us
    pallas_call x1, Pallas kernels, scatter_own(): pl.pallas_call(own_kernel, out_shape=shape((TR, OWN_BLOCKS * L)), in_spec...  4.24 us
    pallas_call x1, Pallas kernels, gather_own(): pl.pallas_call(gather_kernel, out_shape=(shape((TR, SLOTS)), shape((64, 1...  3.98 us
  transfers between devices with their start and end apart: 6, of which 0 were waited for; matrix products, arithmetic and copies ran while one was open for 0% of the time, Pallas kernels for 14%

profile of v6, /device:TPU:1, one launch (start us, length us, event | category | flops | bytes accessed | tf_op | source)
XLA Modules:
  0.0 96.9 jit_solution(5719834784240340950)
XLA Ops:
  0.6 8.0 %rhs.1 = (s32[64,128]{1,0:T(8,128)}, bf16[80,8192]{1,0:T(8,128)(2,1)}, f32[32,768]{1,0:T(8,128)}, f32[32,768]{1,0:T(8,128)}) custom-call(s32[256]{0:T(256)} %tgt_hbm.1, s32[256]{0:T(256)} %src_hbm.1, s32[64,128]{1,0:T(8,128)} %bitcast.3, bf16[256,4096]{1,0:T(8,128)(2,1)} %pb_hbm.1, bf16[32,8192]{1,0:T(8,128)(2,1)} %sv_hbm.1), custom_call_target="tpu_custom_call" | custom-call | tf_op jit(solution)/shard_map/rhs/pallas_call | solution.py:318
  8.7 8.8 %collective-permute-start = (f32[32,768]{1,0:T(8,128)}, f32[32,768]{1,0:T(8,128)S(1)}, u32[]{:S(2)}, u32[]{:S(2)}) collective-permute-start(f32[32,768]{1,0:T(8,128)} %get-tuple-element.20), channel_id=1, source_target_pairs={{0,1},{1,0},{2,3},{3,2},{4,5},{5,4},{6,7},{7,6},{8,9},{9,8},{10,11... | collective-permute-start | bytes 294920 | tf_op jit(solution)/shard_map/ppermute | solution.py:653
  17.5 1.9 %collective-permute-start.1 = (f32[32,768]{1,0:T(8,128)}, f32[32,768]{1,0:T(8,128)S(1)}, u32[]{:S(2)}, u32[]{:S(2)}) collective-permute-start(f32[32,768]{1,0:T(8,128)} %get-tuple-element.21), channel_id=1, source_target_pairs={{1,2},{2,1},{3,4},{4,3},{5,6},{6,5},{7,8},{8,7},{9,10},{10,9},{11,... | collective-permute-start | bytes 294920 | tf_op jit(solution)/shard_map/ppermute | solution.py:652
  19.4 0.0 copy-start.2
  19.4 0.0 copy-start.3
  19.4 0.0 copy-start.1
  19.4 0.0 copy-start.4
  19.5 5.6 %own_first.1.own_ref = f32[32,3584]{1,0:T(8,128)S(1)} custom-call(bf16[80,8192]{1,0:T(8,128)(2,1)} %get-tuple-element.19.parts_hbm), custom_call_target="tpu_custom_call" | custom-call | flops 3758096384 | bytes 2097152 | tf_op jit(solution)/shard_map/own_first/pallas_call | solution.py:267
  25.0 0.0 collective-permute-done.near_ref
  25.1 1.7 %settle.1 = (f32[32,3456]{1,0:T(8,128)S(1)}, f32[32,768]{1,0:T(8,128)S(1)}, f32[32,768]{1,0:T(8,128)S(1)}, bf16[224,1024]{1,0:T(8,128)(2,1)S(1)}) custom-call(f32[32,3584]{1,0:T(8,128)S(1)} %own_first.1.own_ref, f32[32,768]{1,0:T(8,128)S(1)} %collective-permute-done.near_ref, f32[32,768]{1,0:T(8,128)S(1)} %collective-permute-done.1.far_ref, ...), custom_call_target="tpu_custom_call" | custom-call | tf_op jit(solution)/shard_map/settle/pallas_call | solution.py:395
  26.8 1.9 %collective-permute-start.2 = (f32[32,768]{1,0:T(8,128)S(1)}, f32[32,768]{1,0:T(8,128)S(1)}, u32[]{:S(2)}, u32[]{:S(2)}) collective-permute-start(f32[32,768]{1,0:T(8,128)S(1)} %get-tuple-element.24), channel_id=1, source_target_pairs={{0,1},{1,0},{2,3},{3,2},{4,5},{5,4},{6,7},{7,6},{8,9},{9,8},{10,11... | collective-permute-start | bytes 294920 | tf_op jit(solution)/shard_map/ppermute | solution.py:653
  28.8 3.8 %collective-permute-start.3 = (f32[32,768]{1,0:T(8,128)S(1)}, f32[32,768]{1,0:T(8,128)S(1)}, u32[]{:S(2)}, u32[]{:S(2)}) collective-permute-start(f32[32,768]{1,0:T(8,128)S(1)} %get-tuple-element.25), channel_id=1, source_target_pairs={{1,2},{2,1},{3,4},{4,3},{5,6},{6,5},{7,8},{8,7},{9,10},{10,9},{11,... | collective-permute-start | bytes 294920 | tf_op jit(solution)/shard_map/ppermute | solution.py:652
  32.6 0.0 copy-start
  32.6 4.0 %gather.1 = (f32[32,8192]{1,0:T(8,128)S(1)}, f32[64,128]{1,0:T(8,128)S(1)}) custom-call(s32[64,128]{1,0:T(8,128)S(1)} %copy-done.1, bf16[224,1024]{1,0:T(8,128)(2,1)S(1)} %get-tuple-element.22.table_ref, f32[1,128]{1,0:T(1,128)S(1)} %bitcast.2), custom_call_target="tpu_custom_call" | custom-call | flops 3758096384 | bytes 2097152 | tf_op jit(solution)/shard_map/gather/pallas_call | solution.py:425
  36.6 5.8 %mass.1 = (bf16[64,8192]{1,0:T(8,128)(2,1)S(1)}, f32[32,768]{1,0:T(8,128)S(1)}, f32[32,768]{1,0:T(8,128)S(1)}) custom-call(s32[64,128]{1,0:T(8,128)S(1)} %copy-done.1, f32[32,8192]{1,0:T(8,128)S(1)} %get-tuple-element.23.start_ref, f32[32,768]{1,0:T(8,128)S(1)} %collective-permute-done.2.near_ref, f32[32,768]{1,0:T(8,128)S(1)} %collective-permute-done.3.far_ref, ...), custom_call_target="tpu_custom_call" | custom-call | tf_op jit(solution)/shard_map/mass/pallas_call | solution.py:478
  42.4 1.9 %collective-permute-start.4 = (f32[32,768]{1,0:T(8,128)S(1)}, f32[32,768]{1,0:T(8,128)S(1)}, u32[]{:S(2)}, u32[]{:S(2)}) collective-permute-start(f32[32,768]{1,0:T(8,128)S(1)} %get-tuple-element.28), channel_id=1, source_target_pairs={{0,1},{1,0},{2,3},{3,2},{4,5},{5,4},{6,7},{7,6},{8,9},{9,8},{10,11... | collective-permute-start | bytes 294920 | tf_op jit(solution)/shard_map/ppermute | solution.py:653
  44.4 2.4 %collective-permute-start.5 = (f32[32,768]{1,0:T(8,128)S(1)}, f32[32,768]{1,0:T(8,128)S(1)}, u32[]{:S(2)}, u32[]{:S(2)}) collective-permute-start(f32[32,768]{1,0:T(8,128)S(1)} %get-tuple-element.29), channel_id=1, source_target_pairs={{1,2},{2,1},{3,4},{4,3},{5,6},{6,5},{7,8},{8,7},{9,10},{10,9},{11,... | collective-permute-start | bytes 294920 | tf_op jit(solution)/shard_map/ppermute | solution.py:652
  46.8 4.2 %own.1.own_ref = f32[32,3584]{1,0:T(8,128)S(1)} custom-call(s32[64,128]{1,0:T(8,128)S(1)} %copy-done.1, bf16[64,8192]{1,0:T(8,128)(2,1)S(1)} %get-tuple-element.27.parts_ref), custom_call_target="tpu_custom_call" | custom-call | flops 3758096384 | bytes 2097152 | tf_op jit(solution)/shard_map/own/pallas_call | solution.py:355
  51.0 0.0 collective-permute-done.4.near_ref
  51.0 0.0 collective-permute-done.5.far_ref
  51.0 1.9 %grams.1 = (f32[32,3456]{1,0:T(8,128)S(1)}, f32[16,128]{1,0:T(8,128)S(1)}) custom-call(f32[32,3584]{1,0:T(8,128)S(1)} %own.1.own_ref, f32[32,768]{1,0:T(8,128)S(1)} %collective-permute-done.4.near_ref, f32[32,768]{1,0:T(8,128)S(1)} %collective-permute-done.5.far_ref, s32[1,768]{1,0:T(1,128)S(1)} %copy-done.2, s32[1,768]{1,0:T(1,128)S(1)} %copy-done.3, ...), custom_call_target="tpu_custom_call" | custom-call | tf_op jit(solution)/shard_map/grams/pallas_call | solution.py:527
  53.0 22.3 %all_to_all.10 = f32[32,16,128]{2,1,0:T(8,128)S(1)} all-to-all(f32[32,16,128]{2,1,0:T(8,128)S(1)} %broadcast_in_dim.7), channel_id=1, replica_groups=mesh['x'=4,'z'=8,'y'=8,'c'=2] {'x','y'}, dimensions={0} | all-to-all | bytes 524288 | tf_op jit(solution)/shard_map/all_to_all | solution.py:660
  75.3 17.5 %all_to_all.11.gram_ref = f32[16,16,128]{2,1,0:T(8,128)S(1)} all-to-all(f32[16,16,128]{2,1,0:T(8,128)S(1)} %broadcast_in_dim.8), channel_id=1, replica_groups=mesh['x'=4,'z'=8,'y'=8,'c'=2] {'z','c'}, dimensions={0} | all-to-all | bytes 262144 | tf_op jit(solution)/shard_map/all_to_all | solution.py:660
  92.9 3.8 %finish.1 = (f32[32,3456]{1,0:T(8,128)}, f32[32,3456]{1,0:T(8,128)}, f32[32,3456]{1,0:T(8,128)}) custom-call(f32[16,16,128]{2,1,0:T(8,128)S(1)} %all_to_all.11.gram_ref, f32[32,3456]{1,0:T(8,128)S(1)} %get-tuple-element.30.right_ref, f32[32,3456]{1,0:T(8,128)S(1)} %get-tuple-element.32.image_ref), custom_call_target="tpu_custom_call" | custom-call | tf_op jit(solution)/shard_map/finish/pallas_call | solution.py:639
  (11 shorter events, 0.1 us)
Async XLA Ops:
  8.7 16.4 %collective-permute-start = (f32[32,768]{1,0:T(8,128)}, f32[32,768]{1,0:T(8,128)S(1)}, u32[]{:S(2)}, u32[]{:S(2)}) collective-permute-start(f32[32,768]{1,0:T(8,128)} %get-tuple-element.20), channel_id=1, source_target_pairs={{0,1},{1,0},{2,3},{3,2},{4,5},{5,4},{6,7},{7,6},{8,9},{9,8},{10,11... | collective-permute-start | bytes 294920 | tf_op jit(solution)/shard_map/ppermute | solution.py:653
  17.5 7.6 %collective-permute-start.1 = (f32[32,768]{1,0:T(8,128)}, f32[32,768]{1,0:T(8,128)S(1)}, u32[]{:S(2)}, u32[]{:S(2)}) collective-permute-start(f32[32,768]{1,0:T(8,128)} %get-tuple-element.21), channel_id=1, source_target_pairs={{1,2},{2,1},{3,4},{4,3},{5,6},{6,5},{7,8},{8,7},{9,10},{10,9},{11,... | collective-permute-start | bytes 294920 | tf_op jit(solution)/shard_map/ppermute | solution.py:652
  19.4 5.7 %copy-start.2 = (s32[1,768]{1,0:T(1,128)S(1)}, s32[1,768]{1,0:T(1,128)}, u32[]{:S(2)}) copy-start(s32[1,768]{1,0:T(1,128)} %highs_ref.3) | copy-start | bytes 9220
  19.4 5.7 %copy-start.3 = (s32[1,768]{1,0:T(1,128)S(1)}, s32[1,768]{1,0:T(1,128)}, u32[]{:S(2)}) copy-start(s32[1,768]{1,0:T(1,128)} %lows_ref.3) | copy-start | bytes 9220
  19.4 13.2 %copy-start.1 = (s32[64,128]{1,0:T(8,128)S(1)}, s32[64,128]{1,0:T(8,128)}, u32[]{:S(2)}) copy-start(s32[64,128]{1,0:T(8,128)} %get-tuple-element.18.ids_ref) | copy-start | bytes 98308
  19.4 13.2 %copy-start.4 = (f32[128]{0:T(128)S(1)}, f32[128]{0:T(128)}, u32[]{:S(2)}) copy-start(f32[128]{0:T(128)} %param.12) | copy-start | bytes 1540
  26.8 9.8 %collective-permute-start.2 = (f32[32,768]{1,0:T(8,128)S(1)}, f32[32,768]{1,0:T(8,128)S(1)}, u32[]{:S(2)}, u32[]{:S(2)}) collective-permute-start(f32[32,768]{1,0:T(8,128)S(1)} %get-tuple-element.24), channel_id=1, source_target_pairs={{0,1},{1,0},{2,3},{3,2},{4,5},{5,4},{6,7},{7,6},{8,9},{9,8},{10,11... | collective-permute-start | bytes 294920 | tf_op jit(solution)/shard_map/ppermute | solution.py:653
  28.8 7.9 %collective-permute-start.3 = (f32[32,768]{1,0:T(8,128)S(1)}, f32[32,768]{1,0:T(8,128)S(1)}, u32[]{:S(2)}, u32[]{:S(2)}) collective-permute-start(f32[32,768]{1,0:T(8,128)S(1)} %get-tuple-element.25), channel_id=1, source_target_pairs={{1,2},{2,1},{3,4},{4,3},{5,6},{6,5},{7,8},{8,7},{9,10},{10,9},{11,... | collective-permute-start | bytes 294920 | tf_op jit(solution)/shard_map/ppermute | solution.py:652
  32.6 4.0 %copy-start = (bf16[256,512]{1,0:T(8,128)(2,1)S(1)}, bf16[256,512]{1,0:T(8,128)(2,1)}, u32[]{:S(2)}) copy-start(bf16[256,512]{1,0:T(8,128)(2,1)} %constant.4.clone.mass_ref) | copy-start | bytes 786436
  42.4 8.6 %collective-permute-start.4 = (f32[32,768]{1,0:T(8,128)S(1)}, f32[32,768]{1,0:T(8,128)S(1)}, u32[]{:S(2)}, u32[]{:S(2)}) collective-permute-start(f32[32,768]{1,0:T(8,128)S(1)} %get-tuple-element.28), channel_id=1, source_target_pairs={{0,1},{1,0},{2,3},{3,2},{4,5},{5,4},{6,7},{7,6},{8,9},{9,8},{10,11... | collective-permute-start | bytes 294920 | tf_op jit(solution)/shard_map/ppermute | solution.py:653
  44.4 6.7 %collective-permute-start.5 = (f32[32,768]{1,0:T(8,128)S(1)}, f32[32,768]{1,0:T(8,128)S(1)}, u32[]{:S(2)}, u32[]{:S(2)}) collective-permute-start(f32[32,768]{1,0:T(8,128)S(1)} %get-tuple-element.29), channel_id=1, source_target_pairs={{1,2},{2,1},{3,4},{4,3},{5,6},{6,5},{7,8},{8,7},{9,10},{10,9},{11,... | collective-permute-start | bytes 294920 | tf_op jit(solution)/shard_map/ppermute | solution.py:652
